TPU v7x, 32 devices: a whole 2x2x4 slice. The times are simulated.
32 devices in a mesh: section: 2 (over core), dp: 2 (over y), ctx: 2 (over x), tp: 4 (over z).
Axes of the slice: x: 2, y: 2, z: 4, core: 2. Of those that a mesh axis runs over, the one named last changes fastest.
Arguments:
- acts: bfloat16 [4, 2, 2048, 1024], P(None, 'dp', 'ctx'), may hold values from -6 to 6
- cotangent: float32 [4, 2, 2048, 1024], P(None, 'dp', 'ctx'), may hold values from -6 to 6
- lengths: int32 [4, 2], P(None, 'dp'), may hold values from 1024 to 2048, as said below
- norm_gain: bfloat16 [2, 1024], P('section', ('dp', 'ctx')), may hold values from 0.099609375 to 1.8984375
- proj_gate_x: bfloat16 [2, 1024, 2, 2048], P('section', ('dp', 'ctx'), None, 'tp'), may hold values from -0.1875 to 0.1875
- proj_state: bfloat16 [2, 1024, 256], P('section', ('dp', 'ctx')), may hold values from -0.1875 to 0.1875
- proj_step: bfloat16 [2, 1024, 32], P('section', ('dp', 'ctx'), 'tp'), may hold values from -0.1875 to 0.1875
- conv_inner: float32 [2, 5, 2048], P('section', None, 'tp'), may hold values from -3 to 3
- conv_state: float32 [2, 5, 256], P('section'), may hold values from -3 to 3
- step_bias: float32 [2, 32], P('section', 'tp'), may hold values from -10 to -2
- decay_log: float32 [2, 32], P('section', 'tp'), may hold values from -1 to 2
- skip_weight: float32 [2, 32], P('section', 'tp'), may hold values from 0.5 to 1.5
- out_gain: float32 [2, 2048], P('section', 'tp'), may hold values from 0.1 to 1.9
- proj_out: bfloat16 [2, 2048, 1024], P('section', 'tp', ('dp', 'ctx')), may hold values from -0.125 to 0.125
Outputs:
- section_out: bfloat16 [2, 4, 2, 2048, 1024], P('section', None, 'dp', ('ctx', 'tp'))
- input_grad: float32 [2, 4, 2, 2048, 1024], P('section', None, 'dp', ('ctx', 'tp'))
- grad_norm_gain: float32 [2, 1024], P('section', ('dp', 'ctx'))
- grad_gate_x: float32 [2, 1024, 2, 2048], P('section', ('dp', 'ctx'), None, 'tp')
- grad_state: float32 [2, 1024, 256], P('section', ('dp', 'ctx'))
- grad_step: float32 [2, 1024, 32], P('section', ('dp', 'ctx'), 'tp')
- grad_conv_inner: float32 [2, 5, 2048], P('section', None, 'tp')
- grad_conv_state: float32 [2, 5, 256], P('section')
- grad_step_bias: float32 [2, 32], P('section', 'tp')
- grad_decay_log: float32 [2, 32], P('section', 'tp')
- grad_skip: float32 [2, 32], P('section', 'tp')
- grad_out_gain: float32 [2, 2048], P('section', 'tp')
- grad_out: float32 [2, 2048, 1024], P('section', 'tp', ('dp', 'ctx'))
Inputs may be any that keep to these rules, and one draw needn't show every extreme that they name: `lengths`: every data rank has, in one of its 4 micro-batches drawn from the seed, a sequence that fills all 2048 positions of its row.
All inputs are finite; a program needn't handle non-finite values.
Results may differ from a plain program's by a relative error of at most 0.024.
Values may be sent and summed in bfloat16 or wider, within the bound.
No kernel may reach another device: no remote copies, remote signals or barrier semaphores. Data moves between devices by JAX's collectives and lax.ppermute only.
A program may use at most 384 MiB of HBM per device.

v0:
```python
import jax
import jax.numpy as jnp
from jax import lax
from jax.sharding import PartitionSpec as P

HEADDIM = 64
STATE = 128
INNER = 2048
CONV = 4
BLOCK = 256


highest = lax.Precision.HIGHEST
epsilon = 1e-05


def shifted(value, axis, steps):
    count = lax.axis_size(axis)
    leading, last = (max(0, -steps), min(count, count - steps))
    return lax.ppermute(value, axis, [(source, source + steps) for source in range(leading, last)])


def carried_in(x, axis, join, neutral, backward):
    count = lax.axis_size(axis)
    place = lax.axis_index(axis)
    ahead = count - 1 - place if backward else place
    gathered = jax.tree.map(
        lambda a, kind: lax.all_gather(a.astype(kind), axis), x, (jnp.bfloat16, jnp.bfloat16)
    )
    state = jax.tree.map(lambda a, e: jnp.zeros_like(a) + jnp.asarray(e, a.dtype), x, neutral)

    def one(hop, state):
        source = count - 1 - hop if backward else hop
        return join(
            state,
            jax.tree.map(
                lambda a, own: lax.dynamic_index_in_dim(a, source, 0, False).astype(own.dtype),
                gathered,
                x,
            ),
        )

    return lax.fori_loop(0, ahead, one, state)


def root_scale(values, gain_row):
    return (
        values * lax.rsqrt(jnp.mean(values * values, axis=-1, keepdims=True) + epsilon) * gain_row
    )


def conv_apply(padded, conv_taps, raw_step, step_bias, decay_log):
    seg_rows = raw_step.shape[0]
    conv_total = conv_taps[CONV] + sum(
        (conv_taps[offset] * padded[offset : offset + seg_rows] for offset in range(CONV))
    )
    step_size = jax.nn.softplus(raw_step + step_bias)
    return (jax.nn.silu(conv_total), step_size, -jnp.exp(decay_log) * step_size)


def into_blocks(values):
    return values.reshape((values.shape[0] // BLOCK, BLOCK) + values.shape[1:])


def advance(carried, element):
    running, factor = carried
    addition, shrink = element
    return ((shrink[:, None, None] * running + addition, factor * shrink), (running, factor))


def block_states(inner_x, b_rows, step_size, log_decay):
    blocks_x = into_blocks(inner_x)
    blocks_b = into_blocks(b_rows)
    blocks_step = into_blocks(step_size)
    cumulative = jnp.cumsum(into_blocks(log_decay), axis=1)
    block_end = cumulative[:, -1]
    weights = jnp.exp(block_end[:, None] - cumulative) * blocks_step
    fresh_state = jnp.einsum("csh,cshp,csn->chpn", weights, blocks_x, blocks_b, precision=highest)
    starting = (jnp.zeros_like(fresh_state[0]), jnp.ones_like(block_end[0]))
    (local_state, local_decay), (starts, scales) = lax.scan(
        advance, starting, (fresh_state, jnp.exp(block_end))
    )
    return (starts, scales, local_state, local_decay)


def block_output(
    inner_x, b_rows, c_rows, step_size, log_decay, starts, scales, entering, skip_weight
):
    blocks_x = into_blocks(inner_x)
    blocks_b = into_blocks(b_rows)
    blocks_c = into_blocks(c_rows)
    blocks_step = into_blocks(step_size)
    cumulative = jnp.cumsum(into_blocks(log_decay), axis=1)
    by_head = jnp.swapaxes(cumulative, 1, 2)
    causal = jnp.arange(BLOCK)[:, None] >= jnp.arange(BLOCK)[None, :]
    gap_logs = by_head[:, :, :, None] - by_head[:, :, None, :]
    decays = jnp.where(causal, jnp.exp(jnp.where(causal, gap_logs, 0.0)), 0.0)
    affinity = jnp.einsum("ctn,csn->cts", blocks_c, blocks_b, precision=highest)
    mixing = affinity[:, None] * decays * jnp.swapaxes(blocks_step, 1, 2)[:, :, None, :]
    inside = jnp.einsum("chts,cshp->cthp", mixing, blocks_x, precision=highest)
    begins = starts + scales[:, :, None, None] * entering[None]
    carried = jnp.exp(cumulative)[..., None] * jnp.einsum(
        "ctn,chpn->cthp", blocks_c, begins, precision=highest
    )
    result = (inside + carried).reshape(inner_x.shape) + skip_weight[:, None] * inner_x
    return result.reshape(inner_x.shape[0], -1)


def gate_norm(ssm_out, gate_pre, total_sq, out_gain):
    gated_out = ssm_out * jax.nn.silu(gate_pre)
    return gated_out * lax.rsqrt(total_sq / INNER + epsilon)[:, None] * out_gain


def gate_squares(ssm_out, gate_pre):
    gated_out = ssm_out * jax.nn.silu(gate_pre)
    return jnp.sum(gated_out * gated_out, axis=-1)


def chain_join(earlier, latter):
    return (earlier[0] * latter[0], latter[0][:, None, None] * earlier[1] + latter[1])


def contract_rows(left_side, right_side):
    return lax.dot_general(
        left_side, right_side, (((0,), (0,)), ((), ())), preferred_element_type=jnp.float32
    )


def contract_cols(left_side, right_side):
    return lax.dot_general(
        left_side, right_side, (((1,), (1,)), ((), ())), preferred_element_type=jnp.float32
    )


def project_in(normed, gathered):
    gate_full, state_full, step_full = (gathered[1], gathered[2], gathered[3])
    gate_pre = jnp.dot(normed, gate_full[:, 0], preferred_element_type=jnp.float32)
    feed_x = jnp.dot(normed, gate_full[:, 1], preferred_element_type=jnp.float32)
    feed_state = jnp.dot(normed, state_full, preferred_element_type=jnp.float32)
    feed_in = jnp.concatenate([feed_x, feed_state], axis=-1).astype(jnp.bfloat16)
    raw_step = jnp.dot(normed, step_full, preferred_element_type=jnp.float32)
    return (gate_pre, feed_in, raw_step)


def split_act(activated, inner_local):
    seg_rows = activated.shape[0]
    inner_x = activated[:, :inner_local].reshape(seg_rows, -1, HEADDIM)
    return (
        inner_x,
        activated[:, inner_local : inner_local + STATE],
        activated[:, inner_local + STATE :],
    )


def layer_forward(hidden_part, valid_part, gathered, local_params):
    conv_taps, step_bias, decay_log, skip_weight, out_gain = local_params
    inner_local = gathered[1].shape[2]
    normed_part = root_scale(hidden_part, gathered[0].astype(jnp.float32)).astype(jnp.bfloat16)
    seg_rows = normed_part.shape[0]
    gate_pre, feed_in, raw_step = project_in(normed_part, gathered)
    rim_rows = shifted(feed_in[seg_rows - CONV + 1 :], "ctx", 1)
    padded = jnp.concatenate([rim_rows, feed_in], axis=0).astype(jnp.float32)
    activated, step_size, log_decay = conv_apply(padded, conv_taps, raw_step, step_bias, decay_log)
    inner_x, b_rows, c_rows = split_act(activated, inner_local)
    starts, scales, local_state, local_decay = block_states(inner_x, b_rows, step_size, log_decay)
    identity = (jnp.ones_like(local_decay), jnp.zeros_like(local_state))
    entering = carried_in((local_decay, local_state), "ctx", chain_join, identity, False)[1]
    ssm_out = block_output(
        inner_x, b_rows, c_rows, step_size, log_decay, starts, scales, entering, skip_weight
    )
    gated_out = ssm_out * jax.nn.silu(gate_pre)
    total_sq = lax.psum(jnp.sum(gated_out * gated_out, axis=-1), "tp")
    normed_out = (gated_out * lax.rsqrt(total_sq / INNER + epsilon)[:, None] * out_gain).astype(
        jnp.bfloat16
    )
    terms = jnp.dot(normed_out, gathered[4], preferred_element_type=jnp.float32)
    branch = lax.psum(terms, "tp")
    return (hidden_part + valid_part[:, None] * branch, normed_part, rim_rows, entering, total_sq)


def layer_backward(
    hidden_part, valid_part, normed, rim_rows, entering, total_sq, incoming, gathered, local_params
):
    conv_taps, step_bias, decay_log, skip_weight, out_gain = local_params
    seg_rows = normed.shape[0]
    inner_local = gathered[1].shape[2]
    gate_full, state_full, step_full, out_full = (
        gathered[1],
        gathered[2],
        gathered[3],
        gathered[4],
    )
    unused_normed, norm_pull = jax.vjp(root_scale, hidden_part, gathered[0].astype(jnp.float32))
    gate_pre, feed_in, raw_step = project_in(normed, gathered)
    padded = jnp.concatenate([rim_rows, feed_in], axis=0).astype(jnp.float32)
    (activated, step_size, log_decay), conv_pull = jax.vjp(
        conv_apply, padded, conv_taps, raw_step, step_bias, decay_log
    )
    inner_x, b_rows, c_rows = split_act(activated, inner_local)
    (starts, scales, local_state, local_decay), states_pull = jax.vjp(
        block_states, inner_x, b_rows, step_size, log_decay
    )
    ssm_out, output_pull = jax.vjp(
        block_output,
        inner_x,
        b_rows,
        c_rows,
        step_size,
        log_decay,
        starts,
        scales,
        entering,
        skip_weight,
    )
    normed_f2, gate_pull = jax.vjp(gate_norm, ssm_out, gate_pre, total_sq, out_gain)
    normed_out = normed_f2.astype(jnp.bfloat16)
    back_part = (valid_part[:, None] * incoming).astype(jnp.bfloat16)
    grad_out = contract_rows(normed_out, back_part)
    back_normed = contract_cols(back_part, out_full)
    back_ssm, back_gate, back_total, grad_out_gain = gate_pull(back_normed)
    total_back = lax.psum(back_total, "tp")
    squares_out, squares_pull = jax.vjp(gate_squares, ssm_out, gate_pre)
    more_ssm, more_gate = squares_pull(total_back)
    back_ssm = back_ssm + more_ssm
    back_gate = (back_gate + more_gate).astype(jnp.bfloat16)
    (
        back_x,
        back_b,
        back_c,
        back_step,
        back_log,
        back_starts,
        back_scales,
        back_entering,
        grad_skip,
    ) = output_pull(back_ssm)
    identity = (jnp.ones_like(local_decay), jnp.zeros_like(local_state))
    later_grad = carried_in((local_decay, back_entering), "ctx", chain_join, identity, True)[1]
    back_decay = jnp.sum(later_grad * entering, axis=(1, 2))
    more_x, more_b, more_step, more_log = states_pull(
        (back_starts, back_scales, later_grad, back_decay)
    )
    back_states = lax.psum(
        jnp.concatenate([back_b + more_b, back_c], axis=-1).astype(jnp.bfloat16), "tp"
    ).astype(jnp.float32)
    back_act = jnp.concatenate([(back_x + more_x).reshape(seg_rows, -1), back_states], axis=-1)
    back_padded, grad_taps, back_raw, grad_step_bias, grad_decay_log = conv_pull(
        (back_act, back_step + more_step, back_log + more_log)
    )
    returned = shifted(back_padded[: CONV - 1], "ctx", -1)
    back_feed = back_padded[CONV - 1 :] + jnp.pad(returned, ((seg_rows - CONV + 1, 0), (0, 0)))
    back_feed = back_feed.astype(jnp.bfloat16)
    back_raw = back_raw.astype(jnp.bfloat16)
    back_inner = back_feed[:, :inner_local]
    back_pair = back_feed[:, inner_local:]
    local_terms = (
        contract_cols(back_gate, gate_full[:, 0])
        + contract_cols(back_inner, gate_full[:, 1])
        + contract_cols(back_raw, step_full)
    )
    back_normed_in = lax.psum(local_terms.astype(jnp.bfloat16), "tp").astype(
        jnp.float32
    ) + contract_cols(back_pair, state_full)
    back_hidden, grad_norm_gain = norm_pull(back_normed_in)
    grad_gate_x = jnp.stack(
        [contract_rows(normed, back_gate), contract_rows(normed, back_inner)], axis=1
    )
    large_grads = (
        grad_norm_gain,
        grad_gate_x,
        contract_rows(normed, back_pair),
        contract_rows(normed, back_raw),
        grad_out,
    )
    small_grads = (grad_taps, grad_step_bias, grad_decay_log, grad_skip, grad_out_gain)
    return (incoming + back_hidden, large_grads, small_grads)


def on_device(
    acts,
    cotangent,
    lengths,
    norm_gain,
    proj_gate_x,
    proj_state,
    proj_step,
    conv_inner,
    conv_state,
    step_bias,
    decay_log,
    skip_weight,
    out_gain,
    proj_out,
):
    micro_count, seg_rows, model_width = (acts.shape[0], acts.shape[2], acts.shape[3])
    inner_local = proj_gate_x.shape[3]
    heads_local = proj_step.shape[2]
    feed_width = inner_local + 2 * STATE
    section_index = lax.axis_index("section")
    first_section = section_index == 0
    quarter_rows = seg_rows // lax.axis_size("tp")
    own_start = lax.axis_index("tp") * quarter_rows
    places = lax.axis_index("ctx") * seg_rows + jnp.arange(seg_rows, dtype=jnp.int32)
    local_params = (
        jnp.concatenate([conv_inner[0], conv_state[0]], axis=-1),
        step_bias[0],
        decay_log[0],
        skip_weight[0],
        out_gain[0],
    )

    def fetch_weights():
        return (
            lax.all_gather(norm_gain[0], ("dp", "ctx"), axis=0, tiled=True),
            lax.all_gather(proj_gate_x[0], ("dp", "ctx"), axis=0, tiled=True),
            lax.all_gather(proj_state[0], ("dp", "ctx"), axis=0, tiled=True),
            lax.all_gather(proj_step[0], ("dp", "ctx"), axis=0, tiled=True),
            lax.all_gather(proj_out[0], ("dp", "ctx"), axis=1, tiled=True),
        )

    received = jnp.zeros((seg_rows, model_width), jnp.bfloat16)
    section_out = jnp.zeros((micro_count, quarter_rows, model_width), jnp.bfloat16)
    kept_in = jnp.zeros((micro_count, seg_rows, model_width), jnp.bfloat16)
    kept_normed = jnp.zeros((micro_count, seg_rows, model_width), jnp.bfloat16)
    kept_rim = jnp.zeros((micro_count, CONV - 1, feed_width), jnp.bfloat16)
    kept_entering = jnp.zeros((micro_count, heads_local, HEADDIM, STATE), jnp.float32)
    kept_sq = jnp.zeros((micro_count, seg_rows), jnp.float32)
    for tick_index in range(micro_count + 1):
        offset_index = tick_index - section_index
        slot_index = jnp.clip(offset_index, 0, micro_count - 1)
        active = (offset_index >= 0) & (offset_index < micro_count)
        own_acts = acts[min(tick_index, micro_count - 1), 0]
        hidden_in = jnp.where(first_section, own_acts, received)
        valid_part = (places < lengths[slot_index, 0]).astype(jnp.float32)
        gathered = fetch_weights()
        result, normed, rim_rows, entering, total_sq = layer_forward(
            hidden_in.astype(jnp.float32), valid_part, gathered, local_params
        )
        result_low = result.astype(jnp.bfloat16)
        received = shifted(result_low, "section", 1)
        own_out = lax.dynamic_slice_in_dim(result_low, own_start, quarter_rows, 0)
        section_out = jnp.where(active, section_out.at[slot_index].set(own_out), section_out)
        kept_in = jnp.where(active, kept_in.at[slot_index].set(hidden_in), kept_in)
        kept_normed = jnp.where(active, kept_normed.at[slot_index].set(normed), kept_normed)
        kept_rim = jnp.where(active, kept_rim.at[slot_index].set(rim_rows), kept_rim)
        kept_entering = jnp.where(active, kept_entering.at[slot_index].set(entering), kept_entering)
        kept_sq = jnp.where(active, kept_sq.at[slot_index].set(total_sq), kept_sq)
    shares = tuple(
        (
            jnp.zeros(member.shape[1:], jnp.float32)
            for member in (norm_gain, proj_gate_x, proj_state, proj_step, proj_out)
        )
    )
    small_totals = tuple((jnp.zeros_like(member) for member in local_params))
    back_received = jnp.zeros((seg_rows, model_width), jnp.bfloat16)
    input_grad = jnp.zeros((micro_count, quarter_rows, model_width), jnp.float32)
    for tick_index in range(micro_count + 1):
        offset_index = tick_index - 1 + section_index
        slot_index = jnp.clip(offset_index, 0, micro_count - 1)
        active = (offset_index >= 0) & (offset_index < micro_count)
        own_cot = cotangent[min(tick_index, micro_count - 1), 0]
        incoming = jnp.where(first_section, back_received.astype(jnp.float32), own_cot)
        valid_part = (places < lengths[slot_index, 0]).astype(jnp.float32)
        gathered = fetch_weights()
        back_in, large_grads, small_grads = layer_backward(
            kept_in[slot_index].astype(jnp.float32),
            valid_part,
            kept_normed[slot_index],
            kept_rim[slot_index],
            kept_entering[slot_index],
            kept_sq[slot_index],
            incoming,
            gathered,
            local_params,
        )
        back_received = shifted(back_in.astype(jnp.bfloat16), "section", -1)
        own_grad = lax.dynamic_slice_in_dim(back_in, own_start, quarter_rows, 0)
        input_grad = jnp.where(active, input_grad.at[slot_index].set(own_grad), input_grad)
        large_grads = tuple((jnp.where(active, member, 0.0) for member in large_grads))
        small_totals = tuple(
            (
                former + jnp.where(active, latter, 0.0)
                for former, latter in zip(small_totals, small_grads)
            )
        )
        fresh_shares = (
            lax.psum_scatter(
                large_grads[0].astype(jnp.bfloat16), ("dp", "ctx"), scatter_dimension=0, tiled=True
            ).astype(jnp.float32),
            lax.psum_scatter(
                large_grads[1].astype(jnp.bfloat16), ("dp", "ctx"), scatter_dimension=0, tiled=True
            ).astype(jnp.float32),
            lax.psum_scatter(
                large_grads[2].astype(jnp.bfloat16), ("dp", "ctx"), scatter_dimension=0, tiled=True
            ).astype(jnp.float32),
            lax.psum_scatter(
                large_grads[3].astype(jnp.bfloat16), ("dp", "ctx"), scatter_dimension=0, tiled=True
            ).astype(jnp.float32),
            lax.psum_scatter(
                large_grads[4].astype(jnp.bfloat16), ("dp", "ctx"), scatter_dimension=1, tiled=True
            ).astype(jnp.float32),
        )
        shares = tuple((former + latter for former, latter in zip(shares, fresh_shares)))
    gain_share = shares[0]
    small_sums = lax.psum(
        (small_totals[0], small_totals[1], small_totals[2], small_totals[3], small_totals[4]),
        ("dp", "ctx"),
    )
    grad_taps = small_sums[0]
    return (
        section_out[None, :, None],
        input_grad[None, :, None],
        gain_share[None],
        shares[1][None],
        shares[2][None],
        shares[3][None],
        grad_taps[:, :inner_local][None],
        grad_taps[:, inner_local:][None],
        small_sums[1][None],
        small_sums[2][None],
        small_sums[3][None],
        small_sums[4][None],
        shares[4][None],
    )


def solution(mesh):
    placed = (
        P(None, "dp", "ctx", None),
        P(None, "dp", "ctx", None),
        P(None, "dp"),
        P("section", ("dp", "ctx")),
        P("section", ("dp", "ctx"), None, "tp"),
        P("section", ("dp", "ctx"), None),
        P("section", ("dp", "ctx"), "tp"),
        P("section", None, "tp"),
        P("section", None, None),
        P("section", "tp"),
        P("section", "tp"),
        P("section", "tp"),
        P("section", "tp"),
        P("section", "tp", ("dp", "ctx")),
    )
    return jax.shard_map(
        on_device,
        mesh=mesh,
        in_specs=placed,
        out_specs=(
            P("section", None, "dp", ("ctx", "tp"), None),
            P("section", None, "dp", ("ctx", "tp"), None),
            P("section", ("dp", "ctx")),
            P("section", ("dp", "ctx"), None, "tp"),
            P("section", ("dp", "ctx"), None),
            P("section", ("dp", "ctx"), "tp"),
            P("section", None, "tp"),
            P("section", None, None),
            P("section", "tp"),
            P("section", "tp"),
            P("section", "tp"),
            P("section", "tp"),
            P("section", "tp", ("dp", "ctx")),
        ),
        check_vma=False,
    )
```

profile of v0, /device:TPU:1, one launch (start us, length us, event | category | flops | bytes accessed | tf_op | source)
XLA Modules:
  0.0 3675.3 jit_solution(694886573389190713)
XLA Ops:
  80.4 18.7 while.460
  151.7 160.5 %all-reduce.89.cloned.1.call-done = f32[1024,1024]{1,0:T(8,128)} async-done(((f32[1024,1024]{1,0:T(8,128)}), f32[1024,1024]{1,0:T(8,128)}) %all-reduce.89.cloned.1.call-update) | async-done | bytes 4194320 | tf_op jit(solution)/shard_map/psum | solution.py:177
  415.4 159.6 %all-reduce.91.cloned.1.call-done = f32[1024,1024]{1,0:T(8,128)} async-done(((f32[1024,1024]{1,0:T(8,128)}), f32[1024,1024]{1,0:T(8,128)}) %all-reduce.91.cloned.1.call-update) | async-done | bytes 4194320 | tf_op jit(solution)/shard_map/psum | solution.py:177
  694.3 158.0 %all-reduce.93.cloned.1.call-done = f32[1024,1024]{1,0:T(8,128)} async-done(((f32[1024,1024]{1,0:T(8,128)}), f32[1024,1024]{1,0:T(8,128)}) %all-reduce.93.cloned.1.call-update) | async-done | bytes 4194320 | tf_op jit(solution)/shard_map/psum | solution.py:177
  977.8 151.9 %all-reduce.95.cloned.1.call-done = f32[1024,1024]{1,0:T(8,128)} async-done(((f32[1024,1024]{1,0:T(8,128)}), f32[1024,1024]{1,0:T(8,128)}) %all-reduce.95.cloned.1.call-update) | async-done | bytes 4194320 | tf_op jit(solution)/shard_map/psum | solution.py:177
  1322.4 18.7 while.465
  1352.4 21.6 while.466
  1676.8 89.5 %all-reduce.101.cloned.1.call-done = bf16[1024,1024]{1,0:T(8,128)(2,1)} async-done(((bf16[1024,1024]{1,0:T(8,128)(2,1)}), bf16[1024,1024]{1,0:T(8,128)(2,1)}) %all-reduce.101.cloned.1.call-update) | async-done | bytes 2097168 | tf_op jit(solution)/shard_map/psum | solution.py:261
  1842.6 15.1 fusion.156
  1978.2 84.4 %all-reduce.105.cloned.1.call-done = bf16[1024,1024]{1,0:T(8,128)(2,1)} async-done(((bf16[1024,1024]{1,0:T(8,128)(2,1)}), bf16[1024,1024]{1,0:T(8,128)(2,1)}) %all-reduce.105.cloned.1.call-update) | async-done | bytes 2097168 | tf_op jit(solution)/shard_map/psum | solution.py:261
  2272.3 84.4 %all-reduce.109.cloned.1.call-done = bf16[1024,1024]{1,0:T(8,128)(2,1)} async-done(((bf16[1024,1024]{1,0:T(8,128)(2,1)}), bf16[1024,1024]{1,0:T(8,128)(2,1)}) %all-reduce.109.cloned.1.call-update) | async-done | bytes 2097168 | tf_op jit(solution)/shard_map/psum | solution.py:261
  2430.7 15.1 fusion.160
  2566.0 84.4 %all-reduce.113.cloned.1.call-done = bf16[1024,1024]{1,0:T(8,128)(2,1)} async-done(((bf16[1024,1024]{1,0:T(8,128)(2,1)}), bf16[1024,1024]{1,0:T(8,128)(2,1)}) %all-reduce.113.cloned.1.call-update) | async-done | bytes 2097168 | tf_op jit(solution)/shard_map/psum | solution.py:261
  2721.0 15.1 fusion.162
  2994.2 22.0 reduce-scatter.43.cloned.1.call-done
  3016.2 25.3 reduce-scatter.45.cloned.1.call-done
  3041.5 25.2 reduce-scatter.47.cloned.1.call-done
  3066.7 25.3 reduce-scatter.49.cloned.1.call-done
  3120.3 27.6 reduce-scatter.33.cloned.1.call-done
  3147.9 27.7 reduce-scatter.35.cloned.1.call-done
  3175.7 27.6 reduce-scatter.37.cloned.1.call-done
  3203.3 28.3 reduce-scatter.39.cloned.1.call-done
  3233.5 28.6 reduce-scatter.51.cloned.1.call-done
  3262.2 30.9 reduce-scatter.53.cloned.1.call-done
  3293.1 30.7 reduce-scatter.55.cloned.1.call-done
  3323.7 30.8 reduce-scatter.57.cloned.1.call-done
  3354.5 30.6 reduce-scatter.59.cloned.1.call-done
  3387.3 86.8 %all-reduce.117.cloned.1.call-done = bf16[1024,1024]{1,0:T(8,128)(2,1)} async-done(((bf16[1024,1024]{1,0:T(8,128)(2,1)}), bf16[1024,1024]{1,0:T(8,128)(2,1)}) %all-reduce.117.cloned.1.call-update) | async-done | bytes 2097168 | tf_op jit(solution)/shard_map/psum | solution.py:261
  3511.5 38.4 %reduce-scatter.23.cloned.1.call-done = bf16[256,2,512]{2,0,1:T(8,128)(2,1)} async-done(((bf16[1024,2,512]{2,0,1:T(8,128)(2,1)}), bf16[256,2,512]{2,0,1:T(8,128)(2,1)}) %reduce-scatter.23.cloned.1.call-update) | async-done | bytes 524304 | tf_op jit(solution)/shard_map/reduce_scatter | solution.py:390
  3549.9 38.2 %reduce-scatter.25.cloned.1.call-done = bf16[256,2,512]{2,0,1:T(8,128)(2,1)} async-done(((bf16[1024,2,512]{2,0,1:T(8,128)(2,1)}), bf16[256,2,512]{2,0,1:T(8,128)(2,1)}) %reduce-scatter.25.cloned.1.call-update) | async-done | bytes 524304 | tf_op jit(solution)/shard_map/reduce_scatter | solution.py:390
  3588.1 38.3 %reduce-scatter.27.cloned.1.call-done = bf16[256,2,512]{2,0,1:T(8,128)(2,1)} async-done(((bf16[1024,2,512]{2,0,1:T(8,128)(2,1)}), bf16[256,2,512]{2,0,1:T(8,128)(2,1)}) %reduce-scatter.27.cloned.1.call-update) | async-done | bytes 524304 | tf_op jit(solution)/shard_map/reduce_scatter | solution.py:390
  3626.4 38.1 %reduce-scatter.29.cloned.1.call-done = bf16[256,2,512]{2,0,1:T(8,128)(2,1)} async-done(((bf16[1024,2,512]{2,0,1:T(8,128)(2,1)}), bf16[256,2,512]{2,0,1:T(8,128)(2,1)}) %reduce-scatter.29.cloned.1.call-update) | async-done | bytes 524304 | tf_op jit(solution)/shard_map/reduce_scatter | solution.py:390
  (2641 shorter events, 2178.3 us)
Async XLA Ops:
  9.9 302.3 %all-reduce.89.cloned.1.call-start = ((), (), s32[]{:S(2)}) async-start(), calls=%async_computation.20 | async-start | bytes 8388608 | tf_op jit(solution)/shard_map/psum | solution.py:177
  149.7 425.3 %all-reduce.91.cloned.1.call-start = ((), (), s32[]{:S(2)}) async-start(), calls=%async_computation.21 | async-start | bytes 8388608 | tf_op jit(solution)/shard_map/psum | solution.py:177
  414.7 437.6 %all-reduce.93.cloned.1.call-start = ((), (), s32[]{:S(2)}) async-start(), calls=%async_computation.22 | async-start | bytes 8388608 | tf_op jit(solution)/shard_map/psum | solution.py:177
  693.7 436.1 %all-reduce.95.cloned.1.call-start = ((), (), s32[]{:S(2)}) async-start(), calls=%async_computation.23 | async-start | bytes 8388608 | tf_op jit(solution)/shard_map/psum | solution.py:177
  971.0 679.1 %all-reduce.99.cloned.1.call-start = ((), (), s32[]{:S(2)}) async-start(), calls=%async_computation.25 | async-start | bytes 1048576 | tf_op jit(solution)/shard_map/psum | solution.py:243
  1605.3 161.0 %all-reduce.101.cloned.1.call-start = ((), (), s32[]{:S(2)}) async-start(), calls=%async_computation.26 | async-start | bytes 4194304 | tf_op jit(solution)/shard_map/psum | solution.py:261
  1674.6 275.3 %all-reduce.103.cloned.1.call-start = ((), (), s32[]{:S(2)}) async-start(), calls=%async_computation.27 | async-start | bytes 1048576 | tf_op jit(solution)/shard_map/psum | solution.py:243
  1977.6 266.3 %all-reduce.107.cloned.1.call-start = ((), (), s32[]{:S(2)}) async-start(), calls=%async_computation.29 | async-start | bytes 1048576 | tf_op jit(solution)/shard_map/psum | solution.py:243
  2271.6 266.2 %all-reduce.111.cloned.1.call-start = ((), (), s32[]{:S(2)}) async-start(), calls=%async_computation.31 | async-start | bytes 1048576 | tf_op jit(solution)/shard_map/psum | solution.py:243
  2565.4 284.3 %all-reduce.115.cloned.1.call-start = ((), (), s32[]{:S(2)}) async-start(), calls=%async_computation.33 | async-start | bytes 1048576 | tf_op jit(solution)/shard_map/psum | solution.py:243
  2772.8 201.4 %all-reduce.97.cloned.1.call-start = ((), (), s32[]{:S(2)}) async-start(), calls=%async_computation.24 | async-start | bytes 8388608 | tf_op jit(solution)/shard_map/psum | solution.py:177
  2777.9 216.2 %reduce-scatter.41.cloned.1.call-start = ((), (), s32[]{:S(2)}) async-start(), calls=%async_computation.45 | async-start | bytes 20480 | tf_op jit(solution)/shard_map/reduce_scatter | solution.py:396
  2781.3 235.0 %reduce-scatter.43.cloned.1.call-start = ((), (), s32[]{:S(2)}) async-start(), calls=%async_computation.46 | async-start | bytes 20480 | tf_op jit(solution)/shard_map/reduce_scatter | solution.py:396
  2783.9 257.6 %reduce-scatter.45.cloned.1.call-start = ((), (), s32[]{:S(2)}) async-start(), calls=%async_computation.47 | async-start | bytes 20480 | tf_op jit(solution)/shard_map/reduce_scatter | solution.py:396
  2786.7 280.0 %reduce-scatter.47.cloned.1.call-start = ((), (), s32[]{:S(2)}) async-start(), calls=%async_computation.48 | async-start | bytes 20480 | tf_op jit(solution)/shard_map/reduce_scatter | solution.py:396
  2789.4 302.6 %reduce-scatter.49.cloned.1.call-start = ((), (), s32[]{:S(2)}) async-start(), calls=%async_computation.49 | async-start | bytes 20480 | tf_op jit(solution)/shard_map/reduce_scatter | solution.py:396
  2820.8 299.5 %reduce-scatter.31.cloned.1.call-start = ((), (), s32[]{:S(2)}) async-start(), calls=%async_computation.40 | async-start | bytes 655360 | tf_op jit(solution)/shard_map/reduce_scatter | solution.py:393
  2824.2 323.8 %reduce-scatter.33.cloned.1.call-start = ((), (), s32[]{:S(2)}) async-start(), calls=%async_computation.41 | async-start | bytes 655360 | tf_op jit(solution)/shard_map/reduce_scatter | solution.py:393
  2827.5 348.2 %reduce-scatter.35.cloned.1.call-start = ((), (), s32[]{:S(2)}) async-start(), calls=%async_computation.42 | async-start | bytes 655360 | tf_op jit(solution)/shard_map/reduce_scatter | solution.py:393
  2830.9 372.4 %reduce-scatter.37.cloned.1.call-start = ((), (), s32[]{:S(2)}) async-start(), calls=%async_computation.43 | async-start | bytes 655360 | tf_op jit(solution)/shard_map/reduce_scatter | solution.py:393
  2834.4 397.2 %reduce-scatter.39.cloned.1.call-start = ((), (), s32[]{:S(2)}) async-start(), calls=%async_computation.44 | async-start | bytes 655360 | tf_op jit(solution)/shard_map/reduce_scatter | solution.py:393
  2876.1 386.0 %reduce-scatter.51.cloned.1.call-start = ((), (), s32[]{:S(2)}) async-start(), calls=%async_computation.50 | async-start | bytes 1310720 | tf_op jit(solution)/shard_map/reduce_scatter | solution.py:399
  2880.8 412.3 %reduce-scatter.53.cloned.1.call-start = ((), (), s32[]{:S(2)}) async-start(), calls=%async_computation.51 | async-start | bytes 1310720 | tf_op jit(solution)/shard_map/reduce_scatter | solution.py:399
  2885.5 438.2 %reduce-scatter.55.cloned.1.call-start = ((), (), s32[]{:S(2)}) async-start(), calls=%async_computation.52 | async-start | bytes 1310720 | tf_op jit(solution)/shard_map/reduce_scatter | solution.py:399
  2889.5 465.0 %reduce-scatter.57.cloned.1.call-start = ((), (), s32[]{:S(2)}) async-start(), calls=%async_computation.53 | async-start | bytes 1310720 | tf_op jit(solution)/shard_map/reduce_scatter | solution.py:399
  2894.3 490.8 %reduce-scatter.59.cloned.1.call-start = ((), (), s32[]{:S(2)}) async-start(), calls=%async_computation.54 | async-start | bytes 1310720 | tf_op jit(solution)/shard_map/reduce_scatter | solution.py:399
  2899.8 574.4 %all-reduce.117.cloned.1.call-start = ((), (), s32[]{:S(2)}) async-start(), calls=%async_computation.34 | async-start | bytes 4194304 | tf_op jit(solution)/shard_map/psum | solution.py:261
  2905.7 605.8 %reduce-scatter.21.cloned.1.call-start = ((), (), s32[]{:S(2)}) async-start(), calls=%async_computation.35 | async-start | bytes 2621440 | tf_op jit(solution)/shard_map/reduce_scatter | solution.py:390
  2914.4 635.5 %reduce-scatter.23.cloned.1.call-start = ((), (), s32[]{:S(2)}) async-start(), calls=%async_computation.36 | async-start | bytes 2621440 | tf_op jit(solution)/shard_map/reduce_scatter | solution.py:390
  2923.2 664.9 %reduce-scatter.25.cloned.1.call-start = ((), (), s32[]{:S(2)}) async-start(), calls=%async_computation.37 | async-start | bytes 2621440 | tf_op jit(solution)/shard_map/reduce_scatter | solution.py:390
  2931.9 694.5 %reduce-scatter.27.cloned.1.call-start = ((), (), s32[]{:S(2)}) async-start(), calls=%async_computation.38 | async-start | bytes 2621440 | tf_op jit(solution)/shard_map/reduce_scatter | solution.py:390
  2940.7 723.8 %reduce-scatter.29.cloned.1.call-start = ((), (), s32[]{:S(2)}) async-start(), calls=%async_computation.39 | async-start | bytes 2621440 | tf_op jit(solution)/shard_map/reduce_scatter | solution.py:390
  (646 other events, 14926.2 us)
Sparse Core Ops, SparseCore 0:
  10.5 41.7 all-gather.27
  54.0 26.9 all-gather.29
  149.8 162.3 all-reduce.88
  414.9 160.1 all-reduce.90
  693.8 158.4 all-reduce.92
  971.2 158.4 all-reduce.94
  1605.5 44.6 all-reduce.98
  1674.8 91.4 all-reduce.100
  1908.5 35.9 all-reduce.102
  1977.7 84.8 all-reduce.104
  2202.6 35.7 all-reduce.106
  2271.7 84.8 all-reduce.108
  2496.6 35.7 all-reduce.110
  2565.5 84.8 all-reduce.112
  2773.0 35.5 all-reduce.114
  2811.3 155.9 all-reduce.96
  3095.1 25.1 reduce-scatter.30
  3123.1 24.7 reduce-scatter.32
  3150.8 24.7 reduce-scatter.34
  3178.5 24.7 reduce-scatter.36
  3206.8 24.7 reduce-scatter.38
  3234.3 27.7 reduce-scatter.50
  3265.3 27.7 reduce-scatter.52
  3296.0 27.7 reduce-scatter.54
  3326.7 27.7 reduce-scatter.56
  3357.4 27.6 reduce-scatter.58
  3387.6 86.5 all-reduce.116
  3477.0 34.4 reduce-scatter.20
  3514.7 35.1 reduce-scatter.22
  3552.9 35.1 reduce-scatter.24
  3591.2 35.1 reduce-scatter.26
  3629.2 35.1 reduce-scatter.28
  (5 shorter events, 109.9 us)
where the time goes:
time: 3700 us; the launch traced here: 3680 us
  waiting for transfers between devices  1660 us (45%)
  matrix products  729 us (20%)
  other arithmetic  671 us (18%)
  local copies, waits for them, and re-layouts  338 us (9%)
  blocking collectives  203 us (5%)
  starting transfers between devices  48.1 us (1%)
    psum x5, waiting for transfers between devices, layer_forward(): branch = lax.psum(terms, 'tp')  630 us
    psum x5, waiting for transfers between devices, layer_backward(): lax.psum(local_terms.astype(jnp.bfloat16), 'tp').astype(jnp.float32)  429 us
    dot_general x20, matrix products, block_output(): inside = jnp.einsum('chts,cshp->cthp', mixing, blocks_x, precision=highest)  217 us
    reduce_scatter x5, waiting for transfers between devices, on_device(): lax.psum_scatter(large_grads[1].astype(jnp.bfloat16), ('dp', 'ctx'), scat...  167 us
    reduce_scatter x5, waiting for transfers between devices, on_device(): lax.psum_scatter(large_grads[4].astype(jnp.bfloat16), ('dp', 'ctx'), scat...  152 us
    another operation x67, other arithmetic  135 us
    reduce_scatter x5, waiting for transfers between devices, on_device(): lax.psum_scatter(large_grads[2].astype(jnp.bfloat16), ('dp', 'ctx'), scat...  124 us
    dot_general x25, matrix products, contract_cols(): lax.dot_general(left_side, right_side, (((1,), (1,)), ((), ())), preferre...  110 us
  transfers between devices with their start and end apart: 55, of which 41 were waited for; matrix products, arithmetic and copies ran while one was open for 17% of the time, Pallas kernels for 0%

commit v1 on v0

v1 whole, which is shorter than its diff:
```python
import functools

import jax
import jax.numpy as jnp
from jax import lax
from jax.experimental import pallas as pl
from jax.experimental.pallas import tpu as pltpu
from jax.sharding import PartitionSpec as P

HEADDIM = 64
STATE = 128
INNER = 2048
CONV = 4
CHUNK = 128
LANES = 128

highest = lax.Precision.HIGHEST
epsilon = 1e-05
low = jnp.bfloat16
full = jnp.float32


def dot_nn(a, b, precision=None):
    return lax.dot_general(
        a, b, (((1,), (0,)), ((), ())), precision=precision, preferred_element_type=full
    )


def dot_nt(a, b, precision=None):
    return lax.dot_general(
        a, b, (((1,), (1,)), ((), ())), precision=precision, preferred_element_type=full
    )


def dot_tn(a, b, precision=None):
    return lax.dot_general(
        a, b, (((0,), (0,)), ((), ())), precision=precision, preferred_element_type=full
    )


def shifted(value, axis, steps):
    count = lax.axis_size(axis)
    first, last = (max(0, -steps), min(count, count - steps))
    return lax.ppermute(value, axis, [(source, source + steps) for source in range(first, last)])


def rotated(value, axis, steps):
    count = lax.axis_size(axis)
    return lax.ppermute(value, axis, [(i, (i + steps) % count) for i in range(count)])


def line_gather(value, axis):
    count = lax.axis_size(axis)
    place = lax.axis_index(axis)
    if count == 1:
        return value[None]
    if count == 2:
        other = rotated(value, axis, 1)
        first = place == 0
        return jnp.stack([jnp.where(first, value, other), jnp.where(first, other, value)])
    up = down = value
    before, after = [], []
    for _ in range(1, count):
        up = shifted(up, axis, 1)
        down = shifted(down, axis, -1)
        before.insert(0, up)
        after.append(down)
    line = jnp.stack(before + [value] + after)
    return lax.dynamic_slice_in_dim(line, count - 1 - place, count, 0)


def scatter_sum(value, axis):
    count = lax.axis_size(axis)
    place = lax.axis_index(axis)
    total = lax.dynamic_index_in_dim(value, place, 0, False).astype(full)
    for steps in range(1, count):
        block = lax.dynamic_index_in_dim(value, (place + steps) % count, 0, False)
        total = total + rotated(block, axis, steps).astype(full)
    return total


def all_sum(value, axis):
    total = value
    for steps in range(1, lax.axis_size(axis)):
        total = total + rotated(value, axis, steps)
    return total


def swap_cores(value):
    return lax.ppermute(value, "section", [(0, 1), (1, 0)])


def spread_rows(value, pairs_of):
    count = lax.axis_size("tp")
    place = lax.axis_index("tp")
    result = jnp.zeros_like(value)
    own = lax.dynamic_index_in_dim(value, place, 0, False)
    result = lax.dynamic_update_index_in_dim(result, own, place, 0)
    for steps in range(1, count):
        block = lax.dynamic_index_in_dim(value, (place + steps) % count, 0, False)
        pairs = [
            (core * count + i, core * count + (i + steps) % count)
            for core in pairs_of
            for i in range(count)
        ]
        arrived = lax.ppermute(block, ("section", "tp"), pairs)
        result = lax.dynamic_update_index_in_dim(result, arrived, (place - steps) % count, 0)
    return result


def gather_along_tp(packs):
    return [line_gather(pack, "tp") for pack in packs]


def gather_rows(early, late):
    width = early.shape[-1]
    half_a = line_gather(line_gather(early, "ctx"), "dp").reshape(-1, width)
    half_b = jnp.swapaxes(line_gather(line_gather(late, "dp"), "ctx"), 0, 1).reshape(-1, width)
    return half_a, half_b


def columns(pieces):
    return jnp.concatenate(list(pieces), axis=-1)


def reduce_rows(half_a, half_b):
    ndp, nctx = lax.axis_size("dp"), lax.axis_size("ctx")
    rows = half_a.shape[0] // (ndp * nctx)
    blocks_a = jnp.swapaxes(half_a.reshape(ndp, nctx, rows, -1), 0, 1)
    blocks_b = half_b.reshape(ndp, nctx, rows, -1)
    sum_a = scatter_sum(blocks_a, "ctx").astype(low)
    sum_b = scatter_sum(blocks_b, "dp").astype(low)
    return scatter_sum(sum_a, "dp").astype(low), scatter_sum(sum_b, "ctx").astype(low)


def fwd_kernel(x_ref, bc_ref, dt_ref, cum_ref, cumt_ref, skip_ref, enter_ref, y_ref, start_ref, state):
    @pl.when(pl.program_id(0) == 0)
    def _():
        state[...] = enter_ref[...].astype(full)

    heads = cumt_ref.shape[0]
    start_ref[0] = state[...].astype(low)
    b_low = bc_ref[:, :STATE].astype(low)
    c_low = bc_ref[:, STATE:].astype(low)
    row = lax.broadcasted_iota(jnp.int32, (CHUNK, CHUNK), 0)
    col = lax.broadcasted_iota(jnp.int32, (CHUNK, CHUNK), 1)
    left = col < HEADDIM
    upper = row < HEADDIM
    masked = jnp.where(row >= col, dot_nt(c_low, b_low), 0.0)
    for pair in range(heads // 2):
        h0, h1 = 2 * pair, 2 * pair + 1
        span = slice(pair * LANES, (pair + 1) * LANES)
        cum0 = jnp.broadcast_to(cum_ref[:, h0 : h0 + 1], (CHUNK, CHUNK))
        cum1 = jnp.broadcast_to(cum_ref[:, h1 : h1 + 1], (CHUNK, CHUNK))
        w0 = jnp.exp(jnp.minimum(cum0 - cumt_ref[h0 : h0 + 1, :], 0.0)) * masked
        w1 = jnp.exp(jnp.minimum(cum1 - cumt_ref[h1 : h1 + 1, :], 0.0)) * masked
        weights = jnp.concatenate([w0.astype(low), w1.astype(low)], axis=1)
        x_pair = x_ref[:, span]
        u = x_pair * jnp.where(left, dt_ref[:, h0 : h0 + 1], dt_ref[:, h1 : h1 + 1])
        u_low = u.astype(low)
        zero = jnp.zeros_like(u_low)
        u_both = jnp.concatenate([jnp.where(left, u_low, zero), jnp.where(left, zero, u_low)], axis=0)
        cum_pair = jnp.where(left, cum0, cum1)
        s_pair = state[span, :]
        carried = jnp.exp(cum_pair) * dot_nt(c_low, s_pair.astype(low))
        y_ref[:, span] = dot_nn(weights, u_both) + carried + skip_ref[:, span] * x_pair
        end0 = cum_ref[CHUNK - 1 : CHUNK, h0 : h0 + 1]
        end1 = cum_ref[CHUNK - 1 : CHUNK, h1 : h1 + 1]
        ahead = jnp.exp(jnp.where(left, end0, end1) - cum_pair)
        fresh = dot_tn((u * ahead).astype(low), b_low)
        state[span, :] = jnp.exp(jnp.where(upper, end0, end1)) * s_pair + fresh


def bwd_kernel(
    x_ref, bc_ref, dt_ref, cum_ref, cumt_ref, skip_ref, dy_ref, start_ref, later_ref,
    dx_ref, dbc_ref, ddt_ref, dlog_ref,
    adjoint, dye, uw, xdu, dyi, udu,
):
    @pl.when(pl.program_id(0) == 0)
    def _():
        adjoint[...] = later_ref[...].astype(full)

    heads = cumt_ref.shape[0]
    inner = heads * HEADDIM
    b_low = bc_ref[:, :STATE].astype(low)
    c_low = bc_ref[:, STATE:].astype(low)
    row = lax.broadcasted_iota(jnp.int32, (CHUNK, CHUNK), 0)
    col = lax.broadcasted_iota(jnp.int32, (CHUNK, CHUNK), 1)
    left = col < HEADDIM
    causal = row >= col
    onward = (row <= col).astype(low)
    masked = jnp.where(causal, dot_nt(c_low, b_low), 0.0)
    d_affinity = jnp.zeros((CHUNK, CHUNK), full)
    dlog = jnp.zeros((CHUNK, LANES), full)
    for pair in range(heads // 2):
        h0, h1 = 2 * pair, 2 * pair + 1
        span = slice(pair * LANES, (pair + 1) * LANES)
        cum0 = jnp.broadcast_to(cum_ref[:, h0 : h0 + 1], (CHUNK, CHUNK))
        cum1 = jnp.broadcast_to(cum_ref[:, h1 : h1 + 1], (CHUNK, CHUNK))
        m0 = jnp.exp(jnp.minimum(cum0 - cumt_ref[h0 : h0 + 1, :], 0.0))
        m1 = jnp.exp(jnp.minimum(cum1 - cumt_ref[h1 : h1 + 1, :], 0.0))
        w0 = m0 * masked
        w1 = m1 * masked
        dt_pair = jnp.where(left, dt_ref[:, h0 : h0 + 1], dt_ref[:, h1 : h1 + 1])
        x_pair = x_ref[:, span]
        u = x_pair * dt_pair
        u_low = u.astype(low)
        dy_pair = dy_ref[:, span]
        dy_low = dy_pair.astype(low)
        zero = jnp.zeros_like(dy_low)
        dy_both = jnp.concatenate([jnp.where(left, dy_low, zero), jnp.where(left, zero, dy_low)], axis=0)
        dw = dot_nt(dy_both, u_low)
        dw0, dw1 = dw[:CHUNK], dw[CHUNK:]
        d_affinity = d_affinity + dw0 * m0 + dw1 * m1
        z_both = jnp.concatenate([(dw0 * w0).astype(low), (dw1 * w1).astype(low)], axis=1)
        reach = dot_nn(onward, z_both)
        k0 = jnp.sum(jnp.where(row > col, reach[:, :CHUNK], 0.0), axis=1, keepdims=True)
        k1 = jnp.sum(jnp.where(row > col, reach[:, CHUNK:], 0.0), axis=1, keepdims=True)
        dlog = jnp.where(col == h0, k0, jnp.where(col == h1, k1, dlog))
        w_both = jnp.concatenate([w0.astype(low), w1.astype(low)], axis=0)
        cum_pair = jnp.where(left, cum0, cum1)
        end0 = cum_ref[CHUNK - 1 : CHUNK, h0 : h0 + 1]
        end1 = cum_ref[CHUNK - 1 : CHUNK, h1 : h1 + 1]
        ahead = jnp.exp(jnp.where(left, end0, end1) - cum_pair)
        since = jnp.exp(cum_pair)
        du_state = ahead * dot_nt(b_low, adjoint[span, :].astype(low))
        du = dot_tn(w_both, dy_both) + du_state
        dx_ref[:, span] = dt_pair * du + skip_ref[:, span] * dy_pair
        y_state = since * dot_nt(c_low, start_ref[0, span, :])
        xdu[:, span] = x_pair * du
        dyi[:, span] = dy_pair * y_state
        udu[:, span] = u * du_state
        dye[:, span] = (dy_pair * since).astype(low)
        uw[:, span] = (u * ahead).astype(low)
    inner_row = lax.broadcasted_iota(jnp.int32, (inner, LANES), 0)
    inner_col = lax.broadcasted_iota(jnp.int32, (inner, LANES), 1)
    pick = (inner_row // HEADDIM == inner_col).astype(full)
    ddt_ref[...] = dot_nn(xdu[...], pick, highest)
    by_state = dot_nn(dyi[...], pick, highest)
    by_later = dot_nn(udu[...], pick, highest)
    adjoint_now = adjoint[...]
    start_now = start_ref[0]
    both = adjoint_now * start_now.astype(full)
    over = dot_nn(dot_nt(jnp.ones((8, STATE), full), both, highest), pick, highest)
    ends = jnp.exp(cum_ref[CHUNK - 1 : CHUNK, :])
    dlog = dlog + over[0:1] * ends
    dlog = dlog + dot_nn((row <= col).astype(full), by_state, highest)
    dlog_ref[...] = dlog + dot_nn((row > col).astype(full), by_later, highest)
    d_aff = jnp.where(causal, d_affinity, 0.0).astype(low)
    dbc_ref[:, :STATE] = dot_tn(d_aff, c_low) + dot_nn(uw[...], adjoint_now.astype(low))
    dbc_ref[:, STATE:] = dot_nn(d_aff, b_low) + dot_nn(dye[...], start_now)
    fresh = dot_tn(dye[...], c_low)
    for pair in range(heads // 2):
        h0, h1 = 2 * pair, 2 * pair + 1
        span = slice(pair * LANES, (pair + 1) * LANES)
        shrink = jnp.where(row < HEADDIM, ends[:, h0 : h0 + 1], ends[:, h1 : h1 + 1])
        adjoint[span, :] = shrink * adjoint_now[span, :] + fresh[span, :]


def ssm_forward(act, dt, cum, cum_t, skip_row, entering):
    rows = act.shape[0]
    heads = cum_t.shape[0]
    inner = heads * HEADDIM
    blocks = rows // CHUNK
    return pl.pallas_call(
        fwd_kernel,
        grid=(blocks,),
        in_specs=[
            pl.BlockSpec((CHUNK, inner), lambda i: (i, 0)),
            pl.BlockSpec((CHUNK, 2 * STATE), lambda i: (i, inner // (2 * STATE))),
            pl.BlockSpec((CHUNK, LANES), lambda i: (i, 0)),
            pl.BlockSpec((CHUNK, LANES), lambda i: (i, 0)),
            pl.BlockSpec((heads, CHUNK), lambda i: (0, i)),
            pl.BlockSpec((1, inner), lambda i: (0, 0)),
            pl.BlockSpec((inner, STATE), lambda i: (0, 0)),
        ],
        out_specs=[
            pl.BlockSpec((CHUNK, inner), lambda i: (i, 0)),
            pl.BlockSpec((1, inner, STATE), lambda i: (i, 0, 0)),
        ],
        out_shape=[
            jax.ShapeDtypeStruct((rows, inner), full),
            jax.ShapeDtypeStruct((blocks, inner, STATE), low),
        ],
        scratch_shapes=[pltpu.VMEM((inner, STATE), full)],
        compiler_params=pltpu.CompilerParams(
            dimension_semantics=("arbitrary",), vmem_limit_bytes=40 * 1024 * 1024
        ),
        cost_estimate=pl.CostEstimate(
            flops=rows * inner * 2 * 4 * STATE,
            bytes_accessed=rows * inner * 10,
            transcendentals=rows * heads * CHUNK * 2,
        ),
        name="ssm_forward",
    )(act, act, dt, cum, cum_t, skip_row, entering)


def ssm_backward(act, dt, cum, cum_t, skip_row, dy, starts, later):
    rows = act.shape[0]
    heads = cum_t.shape[0]
    inner = heads * HEADDIM
    blocks = rows // CHUNK
    last = blocks - 1
    return pl.pallas_call(
        bwd_kernel,
        grid=(blocks,),
        in_specs=[
            pl.BlockSpec((CHUNK, inner), lambda i: (last - i, 0)),
            pl.BlockSpec((CHUNK, 2 * STATE), lambda i: (last - i, inner // (2 * STATE))),
            pl.BlockSpec((CHUNK, LANES), lambda i: (last - i, 0)),
            pl.BlockSpec((CHUNK, LANES), lambda i: (last - i, 0)),
            pl.BlockSpec((heads, CHUNK), lambda i: (0, last - i)),
            pl.BlockSpec((1, inner), lambda i: (0, 0)),
            pl.BlockSpec((CHUNK, inner), lambda i: (last - i, 0)),
            pl.BlockSpec((1, inner, STATE), lambda i: (last - i, 0, 0)),
            pl.BlockSpec((inner, STATE), lambda i: (0, 0)),
        ],
        out_specs=[
            pl.BlockSpec((CHUNK, inner), lambda i: (last - i, 0)),
            pl.BlockSpec((CHUNK, 2 * STATE), lambda i: (last - i, 0)),
            pl.BlockSpec((CHUNK, LANES), lambda i: (last - i, 0)),
            pl.BlockSpec((CHUNK, LANES), lambda i: (last - i, 0)),
        ],
        out_shape=[
            jax.ShapeDtypeStruct((rows, inner), full),
            jax.ShapeDtypeStruct((rows, 2 * STATE), full),
            jax.ShapeDtypeStruct((rows, LANES), full),
            jax.ShapeDtypeStruct((rows, LANES), full),
        ],
        scratch_shapes=[
            pltpu.VMEM((inner, STATE), full),
            pltpu.VMEM((CHUNK, inner), low),
            pltpu.VMEM((CHUNK, inner), low),
            pltpu.VMEM((CHUNK, inner), full),
            pltpu.VMEM((CHUNK, inner), full),
            pltpu.VMEM((CHUNK, inner), full),
        ],
        compiler_params=pltpu.CompilerParams(
            dimension_semantics=("arbitrary",), vmem_limit_bytes=40 * 1024 * 1024
        ),
        cost_estimate=pl.CostEstimate(
            flops=rows * inner * 2 * 16 * STATE,
            bytes_accessed=rows * inner * 16,
            transcendentals=rows * heads * CHUNK * 2,
        ),
        name="ssm_backward",
    )(act, act, dt, cum, cum_t, skip_row, dy, starts, later)


def heads_to_channels(values):
    return jnp.repeat(values, HEADDIM, axis=-1)


def silu_slope(value, sig):
    return sig * (1.0 + value * (1.0 - sig))


def layer_forward(hidden, valid, weights, params):
    gain, taps, step_bias, decay_log, skip, out_gain = params
    feed_weight, gate_weight, out_weight = weights
    rows, width = hidden.shape
    heads = step_bias.shape[0]
    inner = heads * HEADDIM
    channels = inner + 2 * STATE
    norm = lax.rsqrt(jnp.mean(hidden * hidden, axis=-1, keepdims=True) + epsilon)
    normed = (hidden * norm * gain).astype(low)
    feed_all = dot_nn(normed, feed_weight)
    feed = feed_all[:, :channels].astype(low)
    raw_step = steps_out(feed_all[:, channels:], heads)
    rim = shifted(feed[rows - CONV + 1 :], "ctx", 1)
    padded = jnp.concatenate([rim, feed], axis=0)
    gate = dot_nn(normed, gate_weight)
    pre = conv_total(padded, taps, rows)
    act = pre * jax.nn.sigmoid(pre)
    dt = jax.nn.softplus(raw_step + step_bias)
    log_decay = -jnp.exp(decay_log) * dt
    blocks = rows // CHUNK
    tril = jnp.tril(jnp.ones((CHUNK, CHUNK), full))
    cum = jnp.einsum("ts,csh->cth", tril, log_decay.reshape(blocks, CHUNK, heads), precision=highest)
    ends = cum[:, -1]
    running = jnp.cumsum(ends, axis=0)
    total = running[-1]
    since = (running - ends)[:, None] + cum
    decay_in = jnp.exp(since).reshape(rows, heads)
    to_end = jnp.exp(total - since).reshape(rows, heads) * dt
    cum = cum.reshape(rows, heads)
    weighted = (act[:, :inner] * heads_to_channels(to_end)).astype(low)
    local_state = dot_tn(weighted, act[:, inner : inner + STATE].astype(low))
    shrink = jnp.repeat(jnp.exp(total), HEADDIM)[:, None]
    entering = chain(local_state, shrink, 1)
    lanes = ((0, 0), (0, LANES - heads))
    skip_row = jnp.repeat(skip, HEADDIM)[None]
    scan = (jnp.pad(dt, lanes), jnp.pad(cum, lanes), cum.T, skip_row)
    ssm_out, starts = ssm_forward(act, *scan, entering)
    gated = ssm_out * (gate * jax.nn.sigmoid(gate))
    squares = jnp.sum(gated * gated, axis=-1)
    scaled = (gated * out_gain).astype(low)
    term = dot_nt(scaled, out_weight).astype(low)
    branch = term.astype(full) + swap_cores(term).astype(full)
    squares = squares + swap_cores(squares)
    out_norm = lax.rsqrt(squares / INNER + epsilon)[:, None]
    result = hidden + valid * out_norm * branch
    kept = (
        hidden, norm, normed, padded, act, gate, raw_step, dt, log_decay, decay_in, shrink,
        scan, starts, ssm_out, scaled, branch.astype(low), out_norm,
    )
    return result, kept


def steps_out(block, heads):
    count = lax.axis_size("tp")
    each = heads // count
    wide = block.shape[1] // count
    return columns(block[:, j * wide : j * wide + each] for j in range(count))


def steps_in(values, wide):
    count = lax.axis_size("tp")
    each = values.shape[1] // count
    return columns(
        jnp.pad(values[:, j * each : (j + 1) * each], ((0, 0), (0, wide - each))) for j in range(count)
    )


def conv_total(padded, taps, rows):
    wide = padded.astype(full)
    return taps[CONV] + sum(taps[k] * wide[k : k + rows] for k in range(CONV))


def chain(local_state, shrink, steps):
    entering = shifted(local_state.astype(low), "ctx", steps)
    for _ in range(lax.axis_size("ctx") - 2):
        leaving = shrink * entering.astype(full) + local_state
        entering = shifted(leaving.astype(low), "ctx", steps)
    return entering


def layer_backward(incoming, valid, weights, params, kept):
    gain, taps, step_bias, decay_log, skip, out_gain = params
    feed_weight, gate_weight, out_weight = weights
    (
        hidden, norm, normed, padded, act, gate, raw_step, dt, log_decay, decay_in, shrink,
        scan, starts, ssm_out, scaled, branch, out_norm,
    ) = kept
    rows, width = hidden.shape
    heads = step_bias.shape[0]
    inner = heads * HEADDIM
    channels = inner + 2 * STATE
    back_branch = (valid * incoming).astype(low)
    back_normed = dot_nn(back_branch, out_weight)
    back_wide = back_branch.astype(full)
    grad_out = dot_tn((back_wide * out_norm).astype(low), scaled).astype(low)
    along = jnp.sum(back_wide * branch.astype(full), axis=-1, keepdims=True)
    sig = jax.nn.sigmoid(gate)
    silu = gate * sig
    gated = ssm_out * silu
    grad_out_gain = jnp.sum(back_normed * gated * out_norm, axis=0)
    back_gated = out_norm * out_gain * back_normed - gated * (out_norm**3 * along / INNER)
    back_ssm = back_gated * silu
    back_gate = (back_gated * ssm_out * silu_slope(gate, sig)).astype(low)
    grad_gate = dot_tn(normed, back_gate).astype(low)
    weighted = (back_ssm * heads_to_channels(decay_in)).astype(low)
    local_adjoint = dot_tn(weighted, act[:, inner + STATE :].astype(low))
    later = chain(local_adjoint, shrink, -1)
    back_x, back_bc, back_dt, back_log = ssm_backward(act, *scan, back_ssm, starts, later)
    back_dt, back_log = back_dt[:, :heads], back_log[:, :heads]
    grad_skip = jnp.sum((back_ssm * act[:, :inner]).reshape(rows, heads, HEADDIM), axis=(0, 2))
    grad_decay = jnp.sum(back_log * log_decay, axis=0)
    back_raw = (back_dt - jnp.exp(decay_log) * back_log) * jax.nn.sigmoid(raw_step + step_bias)
    grad_step_bias = jnp.sum(back_raw, axis=0)
    pre = conv_total(padded, taps, rows)
    back_pre = columns([back_x, back_bc]) * silu_slope(pre, jax.nn.sigmoid(pre))
    following = shifted(back_pre[: CONV - 1], "ctx", -1)
    wide = padded.astype(full)
    grad_taps = jnp.stack(
        [jnp.sum(back_pre * wide[k : k + rows], axis=0) for k in range(CONV)]
        + [jnp.sum(back_pre, axis=0)]
    )
    extended = jnp.concatenate([back_pre, following], axis=0)
    back_feed = sum(taps[k] * extended[CONV - 1 - k : CONV - 1 - k + rows] for k in range(CONV))
    step_lanes = (feed_weight.shape[1] - channels) // lax.axis_size("tp")
    back_all = columns([back_feed.astype(low), steps_in(back_raw.astype(low), step_lanes)])
    term = (dot_nt(back_all, feed_weight) + dot_nt(back_gate, gate_weight)).astype(low)
    back_in = term.astype(full) + swap_cores(term).astype(full)
    grad_feed = dot_tn(normed, back_all).astype(low)
    grad_gain = jnp.sum(back_in * hidden * norm, axis=0)
    scaled_in = back_in * gain
    along_in = jnp.sum(scaled_in * hidden, axis=-1, keepdims=True)
    delta = norm * scaled_in - hidden * (norm**3 * along_in / width)
    small = jnp.concatenate(
        [
            grad_taps[:, :inner].reshape(-1), grad_taps[:, inner:].reshape(-1),
            grad_out_gain, grad_step_bias, grad_decay, grad_skip, grad_gain,
        ]
    )
    return delta, (grad_feed, grad_gate, grad_out), small


def reduce_grads(grads, inner):
    grad_feed, grad_gate, grad_out = grads
    count = lax.axis_size("tp")
    half = inner // 2

    def by_tp(half_a, half_b):
        rows = half_a.shape[0]
        joined = jnp.concatenate([half_a, half_b], axis=1).reshape(rows, count, -1)
        return jnp.moveaxis(joined, 1, 0)

    def plain(value):
        half_a, half_b = reduce_rows(value[:, :half], value[:, half:])
        return scatter_sum(by_tp(half_a, half_b), "tp")

    out_sum = plain(grad_out)
    gate_sum = plain(grad_gate)
    rest = grad_feed[:, inner:]
    steps = rest.shape[1] - 2 * STATE
    half_a, half_b = reduce_rows(
        columns([grad_feed[:, :half], rest[:, :STATE], rest[:, 2 * STATE : 2 * STATE + steps // 2]]),
        columns([grad_feed[:, half:inner], rest[:, STATE : 2 * STATE], rest[:, 2 * STATE + steps // 2 :]]),
    )
    split = half + STATE
    state = columns([half_a[:, half:split], half_b[:, half:split]])
    feed_parts = columns(
        [
            by_tp(half_a[:, :half], half_b[:, :half]),
            by_tp(half_a[:, split:], half_b[:, split:]),
            jnp.broadcast_to(state[None], (count,) + state.shape),
        ]
    )
    feed_sum = scatter_sum(feed_parts, "tp")
    return columns([feed_sum, gate_sum, out_sum])


def on_device(
    acts,
    cotangent,
    lengths,
    norm_gain,
    proj_gate_x,
    proj_state,
    proj_step,
    conv_inner,
    conv_state,
    step_bias,
    decay_log,
    skip_weight,
    out_gain,
    proj_out,
):
    micro_count, rows, width = (acts.shape[0], acts.shape[2], acts.shape[3])
    tp_count = lax.axis_size("tp")
    core = lax.axis_index("section")
    lane = lax.axis_index("tp")
    first = core == 0
    own_rows = proj_gate_x.shape[1]
    half = proj_gate_x.shape[3] // 2
    step_half = proj_step.shape[2] // 2
    heads = step_half * tp_count
    inner = half * tp_count
    quarter = 2 * STATE // tp_count
    wide = quarter

    state_part = lax.dynamic_slice_in_dim(proj_state[0], lane * quarter, quarter, 1)

    def pack(c):
        step = proj_step[0, :, c * step_half : (c + 1) * step_half]
        tail = jnp.pad(columns([step, norm_gain[0][:, None]]), ((0, 0), (0, wide - step_half - 1)))
        return columns(
            [
                proj_gate_x[0, :, 1, c * half : (c + 1) * half],
                state_part,
                tail,
                proj_gate_x[0, :, 0, c * half : (c + 1) * half],
                proj_out[0, c * half : (c + 1) * half].T,
            ]
        )

    def pack_small(c):
        return jnp.concatenate(
            [
                conv_inner[0, :, c * half : (c + 1) * half].reshape(-1),
                out_gain[0, c * half : (c + 1) * half],
                step_bias[0, c * step_half : (c + 1) * step_half],
                decay_log[0, c * step_half : (c + 1) * step_half],
                skip_weight[0, c * step_half : (c + 1) * step_half],
                conv_state[0].reshape(-1),
            ]
        )

    def both_layers(make):
        zero, one = make(0), make(1)
        keep = jnp.where(first, zero, one)
        came = swap_cores(jnp.where(first, one, zero))
        return jnp.where(first, keep, came), jnp.where(first, came, keep)

    small_layers = line_gather(jnp.stack(both_layers(pack_small)), "tp")

    def layer_params(layer):
        part = small_layers[:, layer]
        at = (CONV + 1) * half
        taps_inner = jnp.moveaxis(part[:, :at].reshape(tp_count, CONV + 1, half), 0, 1)
        gains = part[:, at : at + half].reshape(-1)
        at += half
        scalars = []
        for _ in range(3):
            scalars.append(part[:, at : at + step_half].reshape(-1))
            at += step_half
        taps_state = part[0, at:].reshape(CONV + 1, 2 * STATE)
        taps = columns([taps_inner.reshape(CONV + 1, inner), taps_state])
        return taps, scalars[0], scalars[1], scalars[2], gains

    cut = half + quarter + wide
    middle = tp_count // 2

    def gather_feed(part):
        def side(pieces):
            return columns(
                [
                    columns(pieces[..., :half]),
                    columns(pieces[..., half : half + quarter]),
                    columns(pieces[..., half + quarter :]),
                ]
            )

        half_a, half_b = gather_rows(side(part[:middle]), side(part[middle:]))
        x_end, s_end = middle * half, middle * (half + quarter)
        feed = columns(
            [
                half_a[:, :x_end], half_b[:, :x_end], half_a[:, x_end:s_end], half_b[:, x_end:s_end],
                half_a[:, s_end:], half_b[:, s_end:],
            ]
        )
        return feed, half_a[:, s_end + step_half].astype(full)

    def gather_pair(part):
        def side(pieces):
            return columns([columns(pieces[..., :half]), columns(pieces[..., half:])])

        half_a, half_b = gather_rows(side(part[:middle]), side(part[middle:]))
        x_end = middle * half
        return (
            columns([half_a[:, :x_end], half_b[:, :x_end]]),
            columns([half_a[:, x_end:], half_b[:, x_end:]]),
        )

    packs = both_layers(pack)
    along = []
    previous = None
    for layer in range(2):
        for part in (packs[layer][:, :cut], packs[layer][:, cut:]):
            if previous is not None:
                part, previous = lax.optimization_barrier((part, previous))
            previous = line_gather(part, "tp")
            along.append(previous)
    weights, params = [], []
    for layer in range(2):
        feed, gain = gather_feed(along[2 * layer])
        gate, out = gather_pair(along[2 * layer + 1])
        weights.append((feed, gate, out))
        params.append((gain,) + layer_params(layer))

    places = lax.axis_index("ctx") * rows + jnp.arange(rows, dtype=jnp.int32)
    length = lax.dynamic_index_in_dim(lengths[:, 0], lane, 0, False)
    valid = (places < length).astype(full)[:, None]
    hidden = lax.dynamic_index_in_dim(acts[:, 0], lane, 0, False).astype(full)
    out_grad = lax.dynamic_index_in_dim(cotangent[:, 0], lane, 0, False)

    result_first, kept_first = layer_forward(hidden, valid, weights[0], params[0])
    low_first = result_first.astype(low)
    result_last, kept_last = layer_forward(low_first.astype(full), valid, weights[1], params[1])
    own_result = jnp.where(first, low_first, result_last.astype(low))
    quarter_rows = rows // tp_count
    section_out = spread_rows(own_result.reshape(tp_count, quarter_rows, width), (0, 1))

    delta_last, grads_last, small_last = layer_backward(
        out_grad, valid, weights[1], params[1], kept_last
    )
    spread_last = spread_rows(delta_last.astype(low).reshape(tp_count, quarter_rows, width), (1,))
    sums_last = reduce_grads(grads_last, inner)
    incoming = (out_grad + delta_last).astype(low).astype(full)
    delta_first, grads_first, small_first = layer_backward(
        incoming, valid, weights[0], params[0], kept_first
    )
    grad_first = (incoming + delta_first).astype(low)
    spread_first = spread_rows(grad_first.reshape(tp_count, quarter_rows, width), (0,))
    sums_first = reduce_grads(grads_first, inner)
    own_cotangent = lax.dynamic_slice_in_dim(
        cotangent[:, 0], lane * quarter_rows, quarter_rows, 1
    )
    input_grad = jnp.where(
        first, spread_first.astype(full), own_cotangent + spread_last.astype(full)
    )

    small = jnp.stack([small_first, small_last])
    for axis in ("dp", "ctx", "tp"):
        small = all_sum(small, axis)
    small_keep = jnp.where(first, small[0], small[1])
    small_came = swap_cores(jnp.where(first, small[1], small[0]))
    keep = jnp.where(first, sums_first, sums_last)
    came = swap_cores(jnp.where(first, sums_last, sums_first))

    def halves(kept_part, came_part, axis):
        zero = jnp.where(first, kept_part, came_part)
        one = jnp.where(first, came_part, kept_part)
        return jnp.concatenate([zero, one], axis=axis)

    def own_lane(value, shape, axis):
        return lax.dynamic_index_in_dim(value.reshape(shape), lane, axis, False)

    at = half
    grad_x = halves(keep[:, :at], came[:, :at], 1)
    grad_step = halves(keep[:, at : at + step_half], came[:, at : at + step_half], 1)
    at += wide
    grad_state = keep[:, at : at + 2 * STATE] + came[:, at : at + 2 * STATE]
    at += 2 * STATE
    grad_gate = halves(keep[:, at : at + half], came[:, at : at + half], 1)
    at += half
    grad_out = halves(keep[:, at : at + half].T, came[:, at : at + half].T, 0)
    grad_gate_x = jnp.stack([grad_gate, grad_x], axis=1)

    at = (CONV + 1) * inner
    taps_shape = (CONV + 1, tp_count, half)
    grad_conv_inner = halves(
        own_lane(small_keep[:at], taps_shape, 1), own_lane(small_came[:at], taps_shape, 1), 1
    )
    end = at + (CONV + 1) * 2 * STATE
    grad_conv_state = (small_keep[at:end] + small_came[at:end]).reshape(CONV + 1, 2 * STATE)
    at = end
    vectors = []
    for size in (inner, heads, heads, heads):
        shape = (tp_count, size // tp_count)
        vectors.append(
            halves(
                own_lane(small_keep[at : at + size], shape, 0),
                own_lane(small_came[at : at + size], shape, 0),
                0,
            )
        )
        at += size
    owner = lax.axis_index("dp") * lax.axis_size("ctx") + lax.axis_index("ctx")
    grad_norm_gain = lax.dynamic_slice_in_dim(small_keep[at:], owner * own_rows, own_rows, 0)
    return (
        section_out[None, :, None],
        input_grad[None, :, None],
        grad_norm_gain[None],
        grad_gate_x[None],
        grad_state[None],
        grad_step[None],
        grad_conv_inner[None],
        grad_conv_state[None],
        vectors[1][None],
        vectors[2][None],
        vectors[3][None],
        vectors[0][None],
        grad_out[None],
    )


def solution(mesh):
    placed = (
        P(None, "dp", "ctx", None),
        P(None, "dp", "ctx", None),
        P(None, "dp"),
        P("section", ("dp", "ctx")),
        P("section", ("dp", "ctx"), None, "tp"),
        P("section", ("dp", "ctx"), None),
        P("section", ("dp", "ctx"), "tp"),
        P("section", None, "tp"),
        P("section", None, None),
        P("section", "tp"),
        P("section", "tp"),
        P("section", "tp"),
        P("section", "tp"),
        P("section", "tp", ("dp", "ctx")),
    )
    return jax.shard_map(
        on_device,
        mesh=mesh,
        in_specs=placed,
        out_specs=(
            P("section", None, "dp", ("ctx", "tp"), None),
            P("section", None, "dp", ("ctx", "tp"), None),
            P("section", ("dp", "ctx")),
            P("section", ("dp", "ctx"), None, "tp"),
            P("section", ("dp", "ctx"), None),
            P("section", ("dp", "ctx"), "tp"),
            P("section", None, "tp"),
            P("section", None, None),
            P("section", "tp"),
            P("section", "tp"),
            P("section", "tp"),
            P("section", "tp"),
            P("section", "tp", ("dp", "ctx")),
        ),
        check_vma=False,
    )
```

time: 3700 us -> 971 us (0.26)
  waiting for transfers between devices: 1660 us -> 195 us
  matrix products: 729 us -> 102 us
  other arithmetic: 671 us -> 145 us
  blocking collectives: 203 us -> 0 us
  starting transfers between devices: 48.1 us -> 209 us
  local copies, waits for them, and re-layouts: 338 us -> 201 us
  Pallas kernels: 0 us -> 100 us
    psum x15 -> x0, waiting for transfers between devices: 1060 us -> none  [the longest x5 630 us: layer_forward(): branch = lax.psum(terms, 'tp')]
    dot_general x175 -> x24, matrix products: 729 us -> 102 us  [the longest x6 38.2 us: dot_nn(): lax.dot_general(a, b, (((1,), (0,)), ((), ())), precision=precision, pref...]
    reduce_scatter x20 -> x0, waiting for transfers between devices: 540 us -> none  [the longest x5 167 us: on_device(): lax.psum_scatter(large_grads[1].astype(jnp.bfloat16), ('dp', 'ctx'), scat...]
    ppermute x18 -> x120, starting transfers between devices: 45.3 us -> 209 us  [the longest x38 98.5 us: shifted(): lax.ppermute(value, axis, [(source, source + steps) for source in range(f...]
    ppermute x18 -> x120, waiting for transfers between devices: 51.5 us -> 195 us  [the longest x63 159 us: rotated(): lax.ppermute(value, axis, [(i, (i + steps) % count) for i in range(count)])]
    another operation x67 -> x36, other arithmetic: 135 us -> 29.8 us  [the longest x28 19.9 us: line_gather(): jnp.stack([jnp.where(first, value, other), jnp.where(first, other, value)])]
    pallas_call x0 -> x4, Pallas kernels: none -> 100 us  [the longest x2 75 us: ssm_backward(): pl.pallas_call(bwd_kernel, grid=(blocks,), in_specs=[pl.BlockSpec((CHUNK,...]
    psum x11 -> x0, blocking collectives: 91.6 us -> none  [the longest x5 41.3 us: layer_forward(): total_sq = lax.psum(jnp.sum(gated_out * gated_out, axis=-1), 'tp')]
  transfers between devices with their start and end apart: 55 -> 120, of which waited for: 41 -> 31; matrix products, arithmetic and copies ran while one was open for 17% -> 37% of each run, Pallas kernels for 0% -> 9%
where the time goes in v1:
time: 971 us; the launch traced here: 957 us
  starting transfers between devices  209 us (22%)
  local copies, waits for them, and re-layouts  201 us (21%)
  waiting for transfers between devices  195 us (20%)
  other arithmetic  145 us (15%)
  matrix products  102 us (11%)
  Pallas kernels  100 us (10%)
    ppermute x63, waiting for transfers between devices, rotated(): lax.ppermute(value, axis, [(i, (i + steps) % count) for i in range(count)])  159 us
    ppermute x38, starting transfers between devices, shifted(): lax.ppermute(value, axis, [(source, source + steps) for source in range(f...  98.5 us
    pallas_call x2, Pallas kernels, ssm_backward(): pl.pallas_call(bwd_kernel, grid=(blocks,), in_specs=[pl.BlockSpec((CHUNK,...  75 us
    ppermute x63, starting transfers between devices, rotated(): lax.ppermute(value, axis, [(i, (i + steps) % count) for i in range(count)])  64.7 us
    unnamed x457, local copies, waits for them, and re-layouts  64 us
    dot_general x6, matrix products, dot_nn(): lax.dot_general(a, b, (((1,), (0,)), ((), ())), precision=precision, pref...  38.2 us
    dot_general x10, matrix products, dot_tn(): lax.dot_general(a, b, (((0,), (0,)), ((), ())), precision=precision, pref...  37.6 us
    ppermute x38, waiting for transfers between devices, shifted(): lax.ppermute(value, axis, [(source, source + steps) for source in range(f...  36.1 us
  transfers between devices with their start and end apart: 120, of which 31 were waited for; matrix products, arithmetic and copies ran while one was open for 37% of the time, Pallas kernels for 9%

profile of v1, /device:TPU:1, one launch (start us, length us, event | category | flops | bytes accessed | tf_op | source)
XLA Modules:
  0.0 957.4 jit_solution(2893655582630404540)
XLA Ops:
  73.9 7.2 collective-permute-done.35
  149.4 6.4 collective-permute-done.52
  160.1 12.5 %collective-permute-done.15 = bf16[2,256,768]{2,1,0:T(8,128)(2,1)S(1)} collective-permute-done((bf16[2,256,768]{2,1,0:T(8,128)(2,1)S(1)}, bf16[2,256,768]{2,1,0:T(8,128)(2,1)S(1)}, u32[]{:S(2)}, u32[]{:S(2)}) %collective-permute-start.15) | collective-permute-done | bytes 786464 | tf_op jit(solution)/shard_map/ppermute | solution.py:49
  176.0 7.9 fusion.248
  212.7 18.4 %collective-permute-done.18 = bf16[3,1280]{1,0:T(4,128)(2,1)S(1)} collective-permute-done((bf16[3,1280]{1,0:T(4,128)(2,1)S(1)}, bf16[3,1280]{1,0:T(4,128)(2,1)S(1)}, u32[]{:S(2)}, u32[]{:S(2)}) %collective-permute-start.18) | collective-permute-done | bytes 7712 | tf_op jit(solution)/shard_map/ppermute | solution.py:44
  249.7 12.7 %ssm_forward.2 = (f32[1024,1024]{1,0:T(8,128)S(1)}, bf16[8,1024,128]{2,1,0:T(8,128)(2,1)S(1)}) custom-call(f32[1024,1280]{1,0:T(8,128)S(1)} %copy-done.3, f32[1024,1280]{1,0:T(8,128)S(1)} %copy-done.3, f32[1024,128]{1,0:T(8,128)S(1)} %pad.47.dt_ref, f32[1024,128]{1,0:T(8,128)S(1)} %pad.48.clone.cum_ref, f32[16,1024]{1,0:T(8,128)S(1)} %get-tuple-element.374.cumt_ref, ...), custom_call_target="tpu_custom_call" | custom-call | flops 1073741824 | bytes 10485760 | tf_op jit(solution)/shard_map/ssm_forward/pallas_call | solution.py:265
  278.8 10.8 %collective-permute-start.31 = (bf16[1024,1024]{1,0:T(8,128)(2,1)S(1)}, bf16[1024,1024]{1,0:T(8,128)(2,1)S(1)}, u32[]{:S(2)}, u32[]{:S(2)}) collective-permute-start(bf16[1024,1024]{1,0:T(8,128)(2,1)S(1)} %convolution_convert_fusion.5), channel_id=1, source_target_pairs={{0,16},{16,0},{1,17},{17,1},{2,18},{18,2},{3,19},{19,3},{4,20},{20... | collective-permute-start | bytes 6291464 | tf_op jit(solution)/shard_map/ppermute | solution.py:90
  342.9 12.2 %ssm_forward.3 = (f32[1024,1024]{1,0:T(8,128)S(1)}, bf16[8,1024,128]{2,1,0:T(8,128)(2,1)S(1)}) custom-call(f32[1024,1280]{1,0:T(8,128)S(1)} %copy-done.5, f32[1024,1280]{1,0:T(8,128)S(1)} %copy-done.5, f32[1024,128]{1,0:T(8,128)S(1)} %pad.49.dt_ref, f32[1024,128]{1,0:T(8,128)S(1)} %pad.50.clone.cum_ref, f32[16,1024]{1,0:T(8,128)S(1)} %get-tuple-element.372.cumt_ref, ...), custom_call_target="tpu_custom_call" | custom-call | flops 1073741824 | bytes 10485760 | tf_op jit(solution)/shard_map/ssm_forward/pallas_call | solution.py:265
  391.5 7.9 multiply_reduce_fusion.8
  449.6 37.5 %ssm_backward.2 = (f32[1024,1024]{1,0:T(8,128)S(1)}, f32[1024,256]{1,0:T(8,128)S(1)}, f32[1024,128]{1,0:T(8,128)S(1)}, f32[1024,128]{1,0:T(8,128)S(1)}) custom-call(f32[1024,1280]{1,0:T(8,128)} %copy-done.4, f32[1024,1280]{1,0:T(8,128)} %copy-done.4, f32[1024,128]{1,0:T(8,128)S(1)} %pad.49.dt_ref, f32[1024,128]{1,0:T(8,128)S(1)} %pad.50.clone.cum_ref, ...), custom_call_target="tpu_custom_call" | custom-call | flops 4294967296 | bytes 16777216 | tf_op jit(solution)/shard_map/ssm_backward/pallas_call | solution.py:304
  487.1 13.1 %multiply_reduce_fusion = (f32[1280]{0:T(1024)S(1)}, f32[1280]{0:T(1024)S(1)}, f32[1280]{0:T(1024)S(1)}, f32[1280]{0:T(1024)S(1)}, f32[1280]{0:T(1024)S(1)}, /*index=5*/f32[1024,1280]{1,0:T(8,128)}) fusion(f32[1027,1280]{1,0:T(8,128)} %copy-done.25, f32[1024,1280]{1,0:T(8,128)} %get-tuple-element.147, f32[1024,256]{1,0:T(8,128)S(1)} %get-tuple-element.35, ...), kind=kLoop, calls=%fused_computation.44 | loop fusion | flops 23586560 | bytes 36725760 | tf_op jit(solution)/shard_map/reduce_sum | solution.py:476
  509.6 10.3 %fusion.13 = bf16[1024,1280]{1,0:T(8,128)(2,1)} fusion(f32[3,1280]{1,0:T(4,128)S(1)} %collective-permute-done.60, f32[1024,1280]{1,0:T(8,128)} %get-tuple-element.136, f32[1280]{0:T(1024)S(1)} %get-tuple-element.113, f32[1280]{0:T(1024)S(1)} %get-tuple-element.110, f32[1280]{0:T(1024)S(1)} %get-tuple-element.111, f32[1280]{0:T(1024)S(1)} %get-tuple-element.112), kind=kLoop, calls=%fused_computation.35 | loop fusion | flops 14417920 | bytes 7900160 | tf_op jit(solution)/shard_map/convert_element_type | solution.py:482
  519.9 6.0 concatenate.243
  542.3 7.9 collective-permute-done.106
  577.7 9.7 %collective-permute-done.109 = bf16[256,256]{0,1:T(8,128)(2,1)S(1)} collective-permute-done((bf16[256,256]{0,1:T(8,128)(2,1)S(1)}, bf16[256,256]{0,1:T(8,128)(2,1)S(1)}, u32[]{:S(2)}, u32[]{:S(2)}) %collective-permute-start.109) | collective-permute-done | bytes 131104 | tf_op jit(solution)/shard_map/ppermute | solution.py:49
  611.6 9.2 multiply_reduce_fusion.10
  650.4 6.4 fusion.79
  656.9 37.5 %ssm_backward.3 = (f32[1024,1024]{1,0:T(8,128)S(1)}, f32[1024,256]{1,0:T(8,128)S(1)}, f32[1024,128]{1,0:T(8,128)S(1)}, f32[1024,128]{1,0:T(8,128)S(1)}) custom-call(f32[1024,1280]{1,0:T(8,128)} %copy-done.2, f32[1024,1280]{1,0:T(8,128)} %copy-done.2, f32[1024,128]{1,0:T(8,128)S(1)} %pad.47.dt_ref, f32[1024,128]{1,0:T(8,128)S(1)} %copy-done.11, ...), custom_call_target="tpu_custom_call" | custom-call | flops 4294967296 | bytes 16777216 | tf_op jit(solution)/shard_map/ssm_backward/pallas_call | solution.py:304
  694.4 11.5 %multiply_reduce_fusion.4 = (f32[1280]{0:T(1024)S(1)}, f32[1280]{0:T(1024)S(1)}, f32[1280]{0:T(1024)S(1)}, f32[1280]{0:T(1024)S(1)}, f32[1280]{0:T(1024)S(1)}, /*index=5*/f32[1024,1280]{1,0:T(8,128)S(1)}) fusion(f32[1027,1280]{1,0:T(8,128)} %copy-done.24, f32[1024,1280]{1,0:T(8,128)} %get-tuple-element.158, f32[1024,256]{1,0:T(8,128)S(1)} %get-tuple-element.40, ...), kind=kLoop, calls=%fused_computation.48 | loop fusion | flops 23586560 | bytes 36725760 | tf_op jit(solution)/shard_map/reduce_sum | solution.py:476
  713.0 9.2 fusion.5
  727.8 6.3 convolution_convert_fusion.1
  764.6 7.7 collective-permute-done.85
  779.7 18.8 %collective-permute-done.93 = bf16[256,512]{0,1:T(8,128)(2,1)S(1)} collective-permute-done((bf16[256,512]{0,1:T(8,128)(2,1)S(1)}, bf16[256,512]{0,1:T(8,128)(2,1)S(1)}, u32[]{:S(2)}, u32[]{:S(2)}) %collective-permute-start.93) | collective-permute-done | bytes 262176 | tf_op jit(solution)/shard_map/ppermute | solution.py:49
  805.0 8.3 collective-permute-done.95
  815.8 16.2 %collective-permute-done.78 = bf16[2,256,768]{1,2,0:T(8,128)(2,1)S(1)} collective-permute-done((bf16[2,256,768]{1,2,0:T(8,128)(2,1)S(1)}, bf16[2,256,768]{1,2,0:T(8,128)(2,1)S(1)}, u32[]{:S(2)}, u32[]{:S(2)}) %collective-permute-start.78) | collective-permute-done | bytes 786464 | tf_op jit(solution)/shard_map/ppermute | solution.py:49
  834.1 7.3 collective-permute-done.100
  843.6 6.3 collective-permute-done.79
  853.9 9.7 %collective-permute-done.87 = bf16[256,256]{0,1:T(8,128)(2,1)S(1)} collective-permute-done((bf16[256,256]{0,1:T(8,128)(2,1)S(1)}, bf16[256,256]{0,1:T(8,128)(2,1)S(1)}, u32[]{:S(2)}, u32[]{:S(2)}) %collective-permute-start.87) | collective-permute-done | bytes 131104 | tf_op jit(solution)/shard_map/ppermute | solution.py:49
  863.6 14.8 %collective-permute-start.81 = (bf16[256,576]{0,1:T(8,128)(2,1)S(1)}, bf16[256,576]{0,1:T(8,128)(2,1)S(1)}, u32[]{:S(2)}, u32[]{:S(2)}) collective-permute-start(bf16[256,576]{0,1:T(8,128)(2,1)S(1)} %get-tuple-element.292), channel_id=1, source_target_pairs={{0,2},{1,3},{2,0},{3,1},{4,6},{5,7},{6,4},{7,5},{8,10},{9,11},{10,... | collective-permute-start | bytes 884744 | tf_op jit(solution)/shard_map/ppermute | solution.py:49
  880.0 6.2 collective-permute-done.82
  886.2 17.9 %collective-permute-done.81 = bf16[256,576]{0,1:T(8,128)(2,1)S(1)} collective-permute-done((bf16[256,576]{0,1:T(8,128)(2,1)S(1)}, bf16[256,576]{0,1:T(8,128)(2,1)S(1)}, u32[]{:S(2)}, u32[]{:S(2)}) %collective-permute-start.81) | collective-permute-done | bytes 294944 | tf_op jit(solution)/shard_map/ppermute | solution.py:49
  929.5 7.2 collective-permute-start.119
  (1105 shorter events, 570.7 us)
Async XLA Ops:
  54.7 27.8 %collective-permute-start.20 = (bf16[256,512]{1,0:T(8,128)(2,1)S(1)}, bf16[256,512]{1,0:T(8,128)(2,1)S(1)}, u32[]{:S(2)}, u32[]{:S(2)}) collective-permute-start(bf16[256,512]{1,0:T(8,128)(2,1)S(1)} %slice.942), channel_id=1, source_target_pairs={{0,1},{1,2},{2,3},{4,5},{5,6},{6,7},{8,9},{9,10},{10,11},{12,13},{... | collective-permute-start | bytes 786440 | tf_op jit(solution)/shard_map/ppermute | solution.py:44
  60.6 28.6 %collective-permute-start.44 = (bf16[256,512]{1,0:T(8,128)(2,1)S(1)}, bf16[256,512]{1,0:T(8,128)(2,1)S(1)}, u32[]{:S(2)}, u32[]{:S(2)}) collective-permute-start(bf16[256,512]{1,0:T(8,128)(2,1)S(1)} %slice.974), channel_id=1, source_target_pairs={{0,1},{1,2},{2,3},{4,5},{5,6},{6,7},{8,9},{9,10},{10,11},{12,13},{... | collective-permute-start | bytes 786440 | tf_op jit(solution)/shard_map/ppermute | solution.py:44
  137.5 35.2 %collective-permute-start.15 = (bf16[2,256,768]{2,1,0:T(8,128)(2,1)S(1)}, bf16[2,256,768]{2,1,0:T(8,128)(2,1)S(1)}, u32[]{:S(2)}, u32[]{:S(2)}) collective-permute-start(bf16[2,256,768]{2,1,0:T(8,128)(2,1)S(1)} %pad_maximum_fusion.30), channel_id=1, source_target_pairs={{0,8},{8,0},{1,9},{9,1},{2,10},{10,2},{3,11},{11,3},{4,12},{12,4},... | collective-permute-start | bytes 2359304 | tf_op jit(solution)/shard_map/ppermute | solution.py:49
  144.6 28.7 %collective-permute-start.17 = (bf16[2,256,768]{2,1,0:T(8,128)(2,1)S(1)}, bf16[2,256,768]{2,1,0:T(8,128)(2,1)S(1)}, u32[]{:S(2)}, u32[]{:S(2)}) collective-permute-start(bf16[2,256,768]{2,1,0:T(8,128)(2,1)S(1)} %pad_maximum_fusion.31), channel_id=1, source_target_pairs={{0,4},{4,0},{1,5},{5,1},{2,6},{6,2},{3,7},{7,3},{8,12},{12,8},{9,1... | collective-permute-start | bytes 2359304 | tf_op jit(solution)/shard_map/ppermute | solution.py:49
  147.5 42.1 %collective-permute-start.39 = (bf16[2,256,768]{2,1,0:T(8,128)(2,1)}, bf16[2,256,768]{2,1,0:T(8,128)(2,1)}, u32[]{:S(2)}, u32[]{:S(2)}) collective-permute-start(bf16[2,256,768]{2,1,0:T(8,128)(2,1)} %pad_maximum_fusion.32), channel_id=1, source_target_pairs={{0,8},{8,0},{1,9},{9,1},{2,10},{10,2},{3,11},{11,3},{4,12},{12,4},... | collective-permute-start | bytes 2359304 | tf_op jit(solution)/shard_map/ppermute | solution.py:49
  155.8 38.0 %collective-permute-start.41 = (bf16[2,256,768]{2,1,0:T(8,128)(2,1)}, bf16[2,256,768]{2,1,0:T(8,128)(2,1)}, u32[]{:S(2)}, u32[]{:S(2)}) collective-permute-start(bf16[2,256,768]{2,1,0:T(8,128)(2,1)} %pad_maximum_fusion.33), channel_id=1, source_target_pairs={{0,4},{4,0},{1,5},{5,1},{2,6},{6,2},{3,7},{7,3},{8,12},{12,8},{9,1... | collective-permute-start | bytes 2359304 | tf_op jit(solution)/shard_map/ppermute | solution.py:49
  158.6 103.8 %collective-permute-start.29 = (bf16[2,256,1024]{2,1,0:T(8,128)(2,1)}, bf16[2,256,1024]{2,1,0:T(8,128)(2,1)}, u32[]{:S(2)}, u32[]{:S(2)}) collective-permute-start(bf16[2,256,1024]{2,1,0:T(8,128)(2,1)} %pad_maximum_fusion.27), channel_id=1, source_target_pairs={{0,4},{4,0},{1,5},{5,1},{2,6},{6,2},{3,7},{7,3},{8,12},{12,8},{9,1... | collective-permute-start | bytes 3145736 | tf_op jit(solution)/shard_map/ppermute | solution.py:49
  172.7 92.5 %collective-permute-start.27 = (bf16[2,256,1024]{2,1,0:T(8,128)(2,1)}, bf16[2,256,1024]{2,1,0:T(8,128)(2,1)}, u32[]{:S(2)}, u32[]{:S(2)}) collective-permute-start(bf16[2,256,1024]{2,1,0:T(8,128)(2,1)} %pad_maximum_fusion.26), channel_id=1, source_target_pairs={{0,8},{8,0},{1,9},{9,1},{2,10},{10,2},{3,11},{11,3},{4,12},{12,4},... | collective-permute-start | bytes 3145736 | tf_op jit(solution)/shard_map/ppermute | solution.py:49
  173.3 119.5 %collective-permute-start.53 = (bf16[2,256,1024]{2,1,0:T(8,128)(2,1)}, bf16[2,256,1024]{2,1,0:T(8,128)(2,1)}, u32[]{:S(2)}, u32[]{:S(2)}) collective-permute-start(bf16[2,256,1024]{2,1,0:T(8,128)(2,1)} %pad_maximum_fusion.29), channel_id=1, source_target_pairs={{0,4},{4,0},{1,5},{5,1},{2,6},{6,2},{3,7},{7,3},{8,12},{12,8},{9,1... | collective-permute-start | bytes 3145736 | tf_op jit(solution)/shard_map/ppermute | solution.py:49
  189.6 105.0 %collective-permute-start.51 = (bf16[2,256,1024]{2,1,0:T(8,128)(2,1)}, bf16[2,256,1024]{2,1,0:T(8,128)(2,1)}, u32[]{:S(2)}, u32[]{:S(2)}) collective-permute-start(bf16[2,256,1024]{2,1,0:T(8,128)(2,1)} %pad_maximum_fusion.28), channel_id=1, source_target_pairs={{0,8},{8,0},{1,9},{9,1},{2,10},{10,2},{3,11},{11,3},{4,12},{12,4},... | collective-permute-start | bytes 3145736 | tf_op jit(solution)/shard_map/ppermute | solution.py:49
  193.8 37.2 %collective-permute-start.18 = (bf16[3,1280]{1,0:T(4,128)(2,1)S(1)}, bf16[3,1280]{1,0:T(4,128)(2,1)S(1)}, u32[]{:S(2)}, u32[]{:S(2)}) collective-permute-start(bf16[3,1280]{1,0:T(4,128)(2,1)S(1)} %slice.926), channel_id=1, source_target_pairs={{0,4},{1,5},{2,6},{3,7},{8,12},{9,13},{10,14},{11,15},{16,20},{17,... | collective-permute-start | bytes 23048 | tf_op jit(solution)/shard_map/ppermute | solution.py:44
  412.7 140.5 %collective-permute-start.56 = (bf16[256,1024]{1,0:T(8,128)(2,1)}, bf16[256,1024]{1,0:T(8,128)(2,1)}, u32[]{:S(2)}, u32[]{:S(2)}) collective-permute-start(bf16[256,1024]{1,0:T(8,128)(2,1)} %get-tuple-element.215), channel_id=1, source_target_pairs={{0,1},{1,2},{2,3},{3,0},{16,17},{17,18},{18,19},{19,16},{4,5},{5,6... | collective-permute-start | bytes 1572872 | tf_op jit(solution)/shard_map/ppermute | solution.py:106
  414.7 139.6 %collective-permute-start.57 = (bf16[256,1024]{1,0:T(8,128)(2,1)}, bf16[256,1024]{1,0:T(8,128)(2,1)}, u32[]{:S(2)}, u32[]{:S(2)}) collective-permute-start(bf16[256,1024]{1,0:T(8,128)(2,1)} %get-tuple-element.214), channel_id=1, source_target_pairs={{0,2},{1,3},{2,0},{3,1},{16,18},{17,19},{18,16},{19,17},{4,6},{5,7... | collective-permute-start | bytes 1572872 | tf_op jit(solution)/shard_map/ppermute | solution.py:106
  418.0 140.4 %collective-permute-start.58 = (bf16[256,1024]{1,0:T(8,128)(2,1)}, bf16[256,1024]{1,0:T(8,128)(2,1)}, u32[]{:S(2)}, u32[]{:S(2)}) collective-permute-start(bf16[256,1024]{1,0:T(8,128)(2,1)} %get-tuple-element.213), channel_id=1, source_target_pairs={{0,3},{1,0},{2,1},{3,2},{16,19},{17,16},{18,17},{19,18},{4,7},{5,4... | collective-permute-start | bytes 1572872 | tf_op jit(solution)/shard_map/ppermute | solution.py:106
  430.0 108.5 %collective-permute-start.113 = (bf16[2,256,512]{1,2,0:T(8,128)(2,1)}, bf16[2,256,512]{1,2,0:T(8,128)(2,1)}, u32[]{:S(2)}, u32[]{:S(2)}) collective-permute-start(bf16[2,256,512]{1,2,0:T(8,128)(2,1)} %bitcast.744), channel_id=1, source_target_pairs={{0,8},{8,0},{1,9},{9,1},{2,10},{10,2},{3,11},{11,3},{4,12},{12,4},... | collective-permute-start | bytes 1572872 | tf_op jit(solution)/shard_map/ppermute | solution.py:49
  507.4 33.7 %collective-permute-start.111 = (bf16[2,256,512]{1,2,0:T(8,128)(2,1)}, bf16[2,256,512]{1,2,0:T(8,128)(2,1)}, u32[]{:S(2)}, u32[]{:S(2)}) collective-permute-start(bf16[2,256,512]{1,2,0:T(8,128)(2,1)} %bitcast.278), channel_id=1, source_target_pairs={{0,4},{4,0},{1,5},{5,1},{2,6},{6,2},{3,7},{7,3},{8,12},{12,8},{9,1... | collective-permute-start | bytes 1572872 | tf_op jit(solution)/shard_map/ppermute | solution.py:49
  550.2 38.0 %collective-permute-start.61 = (bf16[1024,1024]{1,0:T(8,128)(2,1)S(1)}, bf16[1024,1024]{1,0:T(8,128)(2,1)S(1)}, u32[]{:S(2)}, u32[]{:S(2)}) collective-permute-start(bf16[1024,1024]{1,0:T(8,128)(2,1)S(1)} %add_convert_fusion.1), channel_id=1, source_target_pairs={{0,16},{16,0},{1,17},{17,1},{2,18},{18,2},{3,19},{19,3},{4,20},{20... | collective-permute-start | bytes 6291464 | tf_op jit(solution)/shard_map/ppermute | solution.py:90
  596.4 176.7 %collective-permute-start.68 = (bf16[256,1024]{1,0:T(8,128)(2,1)}, bf16[256,1024]{1,0:T(8,128)(2,1)}, u32[]{:S(2)}, u32[]{:S(2)}) collective-permute-start(bf16[256,1024]{1,0:T(8,128)(2,1)} %get-tuple-element.211), channel_id=1, source_target_pairs={{16,17},{17,18},{18,19},{19,16},{20,21},{21,22},{22,23},{23,20},{2... | collective-permute-start | bytes 1572872 | tf_op jit(solution)/shard_map/ppermute | solution.py:106
  598.9 175.9 %collective-permute-start.69 = (bf16[256,1024]{1,0:T(8,128)(2,1)}, bf16[256,1024]{1,0:T(8,128)(2,1)}, u32[]{:S(2)}, u32[]{:S(2)}) collective-permute-start(bf16[256,1024]{1,0:T(8,128)(2,1)} %get-tuple-element.210), channel_id=1, source_target_pairs={{16,18},{17,19},{18,16},{19,17},{20,22},{21,23},{22,20},{23,21},{2... | collective-permute-start | bytes 1572872 | tf_op jit(solution)/shard_map/ppermute | solution.py:106
  602.7 175.2 %collective-permute-start.70 = (bf16[256,1024]{1,0:T(8,128)(2,1)}, bf16[256,1024]{1,0:T(8,128)(2,1)}, u32[]{:S(2)}, u32[]{:S(2)}) collective-permute-start(bf16[256,1024]{1,0:T(8,128)(2,1)} %get-tuple-element.209), channel_id=1, source_target_pairs={{16,19},{17,16},{18,17},{19,18},{20,23},{21,20},{22,21},{23,22},{2... | collective-permute-start | bytes 1572872 | tf_op jit(solution)/shard_map/ppermute | solution.py:106
  624.4 32.5 %collective-permute-start.62 = (bf16[1024,128]{1,0:T(8,128)(2,1)}, bf16[1024,128]{1,0:T(8,128)(2,1)S(1)}, u32[]{:S(2)}, u32[]{:S(2)}) collective-permute-start(bf16[1024,128]{1,0:T(8,128)(2,1)} %fusion.81), channel_id=1, source_target_pairs={{4,0},{5,1},{6,2},{7,3},{12,8},{13,9},{14,10},{15,11},{20,16},{21,... | collective-permute-start | bytes 786440 | tf_op jit(solution)/shard_map/ppermute | solution.py:44
  636.6 124.7 %collective-permute-start.92 = (bf16[2,256,512]{1,2,0:T(8,128)(2,1)}, bf16[2,256,512]{1,2,0:T(8,128)(2,1)}, u32[]{:S(2)}, u32[]{:S(2)}) collective-permute-start(bf16[2,256,512]{1,2,0:T(8,128)(2,1)} %bitcast.742), channel_id=1, source_target_pairs={{0,8},{8,0},{1,9},{9,1},{2,10},{10,2},{3,11},{11,3},{4,12},{12,4},... | collective-permute-start | bytes 1572872 | tf_op jit(solution)/shard_map/ppermute | solution.py:49
  711.1 52.0 %collective-permute-start.90 = (bf16[2,256,512]{1,2,0:T(8,128)(2,1)}, bf16[2,256,512]{1,2,0:T(8,128)(2,1)}, u32[]{:S(2)}, u32[]{:S(2)}) collective-permute-start(bf16[2,256,512]{1,2,0:T(8,128)(2,1)} %bitcast.230), channel_id=1, source_target_pairs={{0,4},{4,0},{1,5},{5,1},{2,6},{6,2},{3,7},{7,3},{8,12},{12,8},{9,1... | collective-permute-start | bytes 1572872 | tf_op jit(solution)/shard_map/ppermute | solution.py:49
  772.3 42.6 %collective-permute-start.99 = (bf16[2,256,768]{1,2,0:T(8,128)(2,1)S(1)}, bf16[2,256,768]{1,2,0:T(8,128)(2,1)S(1)}, u32[]{:S(2)}, u32[]{:S(2)}) collective-permute-start(bf16[2,256,768]{1,2,0:T(8,128)(2,1)S(1)} %bitcast.730), channel_id=1, source_target_pairs={{0,8},{8,0},{1,9},{9,1},{2,10},{10,2},{3,11},{11,3},{4,12},{12,4},... | collective-permute-start | bytes 2359304 | tf_op jit(solution)/shard_map/ppermute | solution.py:49
  773.2 42.3 %collective-permute-start.97 = (bf16[2,256,768]{1,2,0:T(8,128)(2,1)S(1)}, bf16[2,256,768]{1,2,0:T(8,128)(2,1)S(1)}, u32[]{:S(2)}, u32[]{:S(2)}) collective-permute-start(bf16[2,256,768]{1,2,0:T(8,128)(2,1)S(1)} %bitcast.729), channel_id=1, source_target_pairs={{0,4},{4,0},{1,5},{5,1},{2,6},{6,2},{3,7},{7,3},{8,12},{12,8},{9,1... | collective-permute-start | bytes 2359304 | tf_op jit(solution)/shard_map/ppermute | solution.py:49
  805.0 101.7 %collective-permute-start.64 = (bf16[1024,1024]{1,0:T(8,128)(2,1)S(1)}, bf16[1024,1024]{1,0:T(8,128)(2,1)S(1)}, u32[]{:S(2)}, u32[]{:S(2)}) collective-permute-start(bf16[1024,1024]{1,0:T(8,128)(2,1)S(1)} %copy-done.39), channel_id=1, source_target_pairs={{0,16},{16,0},{1,17},{17,1},{2,18},{18,2},{3,19},{19,3},{4,20},{20... | collective-permute-start | bytes 6291464 | tf_op jit(solution)/shard_map/ppermute | solution.py:90
  814.9 36.2 %collective-permute-start.89 = (bf16[256,256]{0,1:T(8,128)(2,1)S(1)}, bf16[256,256]{0,1:T(8,128)(2,1)S(1)}, u32[]{:S(2)}, u32[]{:S(2)}) collective-permute-start(bf16[256,256]{0,1:T(8,128)(2,1)S(1)} %get-tuple-element.331), channel_id=1, source_target_pairs={{0,3},{1,0},{2,1},{3,2},{4,7},{5,4},{6,5},{7,6},{8,11},{9,8},{10,9... | collective-permute-start | bytes 393224 | tf_op jit(solution)/shard_map/ppermute | solution.py:49
  815.5 36.6 %collective-permute-start.88 = (bf16[256,256]{0,1:T(8,128)(2,1)S(1)}, bf16[256,256]{0,1:T(8,128)(2,1)S(1)}, u32[]{:S(2)}, u32[]{:S(2)}) collective-permute-start(bf16[256,256]{0,1:T(8,128)(2,1)S(1)} %get-tuple-element.332), channel_id=1, source_target_pairs={{0,2},{1,3},{2,0},{3,1},{4,6},{5,7},{6,4},{7,5},{8,10},{9,11},{10,... | collective-permute-start | bytes 393224 | tf_op jit(solution)/shard_map/ppermute | solution.py:49
  850.7 27.6 %collective-permute-start.102 = (bf16[256,576]{0,1:T(8,128)(2,1)S(1)}, bf16[256,576]{0,1:T(8,128)(2,1)S(1)}, u32[]{:S(2)}, u32[]{:S(2)}) collective-permute-start(bf16[256,576]{0,1:T(8,128)(2,1)S(1)} %get-tuple-element.295), channel_id=1, source_target_pairs={{0,2},{1,3},{2,0},{3,1},{4,6},{5,7},{6,4},{7,5},{8,10},{9,11},{10,... | collective-permute-start | bytes 884744 | tf_op jit(solution)/shard_map/ppermute | solution.py:49
  852.1 27.8 %collective-permute-start.101 = (bf16[256,576]{0,1:T(8,128)(2,1)S(1)}, bf16[256,576]{0,1:T(8,128)(2,1)S(1)}, u32[]{:S(2)}, u32[]{:S(2)}) collective-permute-start(bf16[256,576]{0,1:T(8,128)(2,1)S(1)} %get-tuple-element.293), channel_id=1, source_target_pairs={{0,1},{1,2},{2,3},{3,0},{4,5},{5,6},{6,7},{7,4},{8,9},{9,10},{10,1... | collective-permute-start | bytes 884744 | tf_op jit(solution)/shard_map/ppermute | solution.py:49
  863.6 40.5 %collective-permute-start.81 = (bf16[256,576]{0,1:T(8,128)(2,1)S(1)}, bf16[256,576]{0,1:T(8,128)(2,1)S(1)}, u32[]{:S(2)}, u32[]{:S(2)}) collective-permute-start(bf16[256,576]{0,1:T(8,128)(2,1)S(1)} %get-tuple-element.292), channel_id=1, source_target_pairs={{0,2},{1,3},{2,0},{3,1},{4,6},{5,7},{6,4},{7,5},{8,10},{9,11},{10,... | collective-permute-start | bytes 884744 | tf_op jit(solution)/shard_map/ppermute | solution.py:49
  905.4 36.1 %collective-permute-start.118 = (f32[256,1088]{0,1:T(8,128)}, f32[256,1088]{0,1:T(8,128)}, u32[]{:S(2)}, u32[]{:S(2)}) collective-permute-start(f32[256,1088]{0,1:T(8,128)} %get-tuple-element.196), channel_id=1, source_target_pairs={{0,16},{16,0},{1,17},{17,1},{2,18},{18,2},{3,19},{19,3},{4,20},{20... | collective-permute-start | bytes 3342344 | tf_op jit(solution)/shard_map/ppermute | solution.py:90
  (286 other events, 4438.0 us)

commit v2 on v1

--- a/solution.py
+++ b/solution.py
@@ -49,15 +49,15 @@
     return lax.ppermute(value, axis, [(i, (i + steps) % count) for i in range(count)])
 
 
-def line_gather(value, axis):
+def line_gather(value, axis, dim=0):
     count = lax.axis_size(axis)
     place = lax.axis_index(axis)
     if count == 1:
-        return value[None]
+        return jnp.expand_dims(value, dim)
     if count == 2:
         other = rotated(value, axis, 1)
         first = place == 0
-        return jnp.stack([jnp.where(first, value, other), jnp.where(first, other, value)])
+        return jnp.stack([jnp.where(first, value, other), jnp.where(first, other, value)], axis=dim)
     up = down = value
     before, after = [], []
     for _ in range(1, count):
@@ -65,17 +65,20 @@
         down = shifted(down, axis, -1)
         before.insert(0, up)
         after.append(down)
-    line = jnp.stack(before + [value] + after)
-    return lax.dynamic_slice_in_dim(line, count - 1 - place, count, 0)
-
-
-def scatter_sum(value, axis):
+    line = jnp.stack(before + [value] + after, axis=dim)
+    return lax.dynamic_slice_in_dim(line, count - 1 - place, count, dim)
+
+
+def scatter_sum(parts, axis, dim=0):
     count = lax.axis_size(axis)
     place = lax.axis_index(axis)
-    total = lax.dynamic_index_in_dim(value, place, 0, False).astype(full)
+
+    def pick(at):
+        return columns(lax.dynamic_index_in_dim(part, at, dim, False) for part in parts)
+
+    total = pick(place).astype(full)
     for steps in range(1, count):
-        block = lax.dynamic_index_in_dim(value, (place + steps) % count, 0, False)
-        total = total + rotated(block, axis, steps).astype(full)
+        total = total + rotated(pick((place + steps) % count), axis, steps).astype(full)
     return total
 
 
@@ -108,14 +111,10 @@
     return result
 
 
-def gather_along_tp(packs):
-    return [line_gather(pack, "tp") for pack in packs]
-
-
 def gather_rows(early, late):
     width = early.shape[-1]
     half_a = line_gather(line_gather(early, "ctx"), "dp").reshape(-1, width)
-    half_b = jnp.swapaxes(line_gather(line_gather(late, "dp"), "ctx"), 0, 1).reshape(-1, width)
+    half_b = line_gather(line_gather(late, "dp"), "ctx", 1).reshape(-1, width)
     return half_a, half_b
 
 
@@ -123,14 +122,13 @@
     return jnp.concatenate(list(pieces), axis=-1)
 
 
-def reduce_rows(half_a, half_b):
-    ndp, nctx = lax.axis_size("dp"), lax.axis_size("ctx")
-    rows = half_a.shape[0] // (ndp * nctx)
-    blocks_a = jnp.swapaxes(half_a.reshape(ndp, nctx, rows, -1), 0, 1)
-    blocks_b = half_b.reshape(ndp, nctx, rows, -1)
-    sum_a = scatter_sum(blocks_a, "ctx").astype(low)
-    sum_b = scatter_sum(blocks_b, "dp").astype(low)
-    return scatter_sum(sum_a, "dp").astype(low), scatter_sum(sum_b, "ctx").astype(low)
+def as_rows(vector, width):
+    rows = -(-vector.shape[0] // (16 * width)) * 16
+    return jnp.pad(vector, (0, rows * width - vector.shape[0])).reshape(rows, width)
+
+
+def tied(value, other):
+    return lax.optimization_barrier((value, other))
 
 
 def fwd_kernel(x_ref, bc_ref, dt_ref, cum_ref, cumt_ref, skip_ref, enter_ref, y_ref, start_ref, state):
@@ -348,7 +346,10 @@
 
 
 def heads_to_channels(values):
-    return jnp.repeat(values, HEADDIM, axis=-1)
+    heads = values.shape[1]
+    head = lax.broadcasted_iota(jnp.int32, (heads, heads * HEADDIM), 0)
+    channel = lax.broadcasted_iota(jnp.int32, (heads, heads * HEADDIM), 1)
+    return dot_nn(values, (channel // HEADDIM == head).astype(full), highest)
 
 
 def silu_slope(value, sig):
@@ -366,7 +367,7 @@
     normed = (hidden * norm * gain).astype(low)
     feed_all = dot_nn(normed, feed_weight)
     feed = feed_all[:, :channels].astype(low)
-    raw_step = steps_out(feed_all[:, channels:], heads)
+    raw_step = feed_all[:, channels : channels + heads]
     rim = shifted(feed[rows - CONV + 1 :], "ctx", 1)
     padded = jnp.concatenate([rim, feed], axis=0)
     gate = dot_nn(normed, gate_weight)
@@ -407,21 +408,6 @@
     return result, kept
 
 
-def steps_out(block, heads):
-    count = lax.axis_size("tp")
-    each = heads // count
-    wide = block.shape[1] // count
-    return columns(block[:, j * wide : j * wide + each] for j in range(count))
-
-
-def steps_in(values, wide):
-    count = lax.axis_size("tp")
-    each = values.shape[1] // count
-    return columns(
-        jnp.pad(values[:, j * each : (j + 1) * each], ((0, 0), (0, wide - each))) for j in range(count)
-    )
-
-
 def conv_total(padded, taps, rows):
     wide = padded.astype(full)
     return taps[CONV] + sum(taps[k] * wide[k : k + rows] for k in range(CONV))
@@ -435,7 +421,7 @@
     return entering
 
 
-def layer_backward(incoming, valid, weights, params, kept):
+def layer_backward(incoming, valid, weights, params, kept, pending=None):
     gain, taps, step_bias, decay_log, skip, out_gain = params
     feed_weight, gate_weight, out_weight = weights
     (
@@ -462,7 +448,17 @@
     weighted = (back_ssm * heads_to_channels(decay_in)).astype(low)
     local_adjoint = dot_tn(weighted, act[:, inner + STATE :].astype(low))
     later = chain(local_adjoint, shrink, -1)
+    early = None
+    if pending is not None:
+        early = Reduction([grad_gate], [grad_out])
+        back_ssm, pending.sums = tied(back_ssm, pending.sums)
+        pending.second()
+        early.first()
     back_x, back_bc, back_dt, back_log = ssm_backward(act, *scan, back_ssm, starts, later)
+    if pending is not None:
+        back_x, (pending.sums, early.sums) = tied(back_x, (pending.sums, early.sums))
+        pending.sums = scatter_sum(pending.blocks(pending.sums), "tp")
+        early.second()
     back_dt, back_log = back_dt[:, :heads], back_log[:, :heads]
     grad_skip = jnp.sum((back_ssm * act[:, :inner]).reshape(rows, heads, HEADDIM), axis=(0, 2))
     grad_decay = jnp.sum(back_log * log_decay, axis=0)
@@ -478,9 +474,12 @@
     )
     extended = jnp.concatenate([back_pre, following], axis=0)
     back_feed = sum(taps[k] * extended[CONV - 1 - k : CONV - 1 - k + rows] for k in range(CONV))
-    step_lanes = (feed_weight.shape[1] - channels) // lax.axis_size("tp")
-    back_all = columns([back_feed.astype(low), steps_in(back_raw.astype(low), step_lanes)])
+    spare = feed_weight.shape[1] - channels - heads
+    back_all = columns([back_feed.astype(low), jnp.pad(back_raw.astype(low), ((0, 0), (0, spare)))])
     term = (dot_nt(back_all, feed_weight) + dot_nt(back_gate, gate_weight)).astype(low)
+    if pending is not None:
+        term, (pending.sums, early.sums) = tied(term, (pending.sums, early.sums))
+        early.sums = scatter_sum([by_tp(early.sums[0]), by_tp(early.sums[1])], "tp")
     back_in = term.astype(full) + swap_cores(term).astype(full)
     grad_feed = dot_tn(normed, back_all).astype(low)
     grad_gain = jnp.sum(back_in * hidden * norm, axis=0)
@@ -493,42 +492,37 @@
             grad_out_gain, grad_step_bias, grad_decay, grad_skip, grad_gain,
         ]
     )
-    return delta, (grad_feed, grad_gate, grad_out), small
-
-
-def reduce_grads(grads, inner):
-    grad_feed, grad_gate, grad_out = grads
-    count = lax.axis_size("tp")
-    half = inner // 2
-
-    def by_tp(half_a, half_b):
-        rows = half_a.shape[0]
-        joined = jnp.concatenate([half_a, half_b], axis=1).reshape(rows, count, -1)
-        return jnp.moveaxis(joined, 1, 0)
-
-    def plain(value):
-        half_a, half_b = reduce_rows(value[:, :half], value[:, half:])
-        return scatter_sum(by_tp(half_a, half_b), "tp")
-
-    out_sum = plain(grad_out)
-    gate_sum = plain(grad_gate)
-    rest = grad_feed[:, inner:]
-    steps = rest.shape[1] - 2 * STATE
-    half_a, half_b = reduce_rows(
-        columns([grad_feed[:, :half], rest[:, :STATE], rest[:, 2 * STATE : 2 * STATE + steps // 2]]),
-        columns([grad_feed[:, half:inner], rest[:, STATE : 2 * STATE], rest[:, 2 * STATE + steps // 2 :]]),
-    )
-    split = half + STATE
-    state = columns([half_a[:, half:split], half_b[:, half:split]])
-    feed_parts = columns(
-        [
-            by_tp(half_a[:, :half], half_b[:, :half]),
-            by_tp(half_a[:, split:], half_b[:, split:]),
-            jnp.broadcast_to(state[None], (count,) + state.shape),
+    return delta, (grad_feed, grad_gate, grad_out), small, early
+
+
+def by_tp(value):
+    return jnp.moveaxis(value.reshape(value.shape[0], lax.axis_size("tp"), -1), 1, 0)
+
+
+class Reduction:
+    def __init__(self, half_a, half_b):
+        ndp, nctx = lax.axis_size("dp"), lax.axis_size("ctx")
+        rows = half_a[0].shape[0] // (ndp * nctx)
+        self.halves = [
+            [part.reshape(ndp, nctx, rows, part.shape[1]) for part in half] for half in (half_a, half_b)
         ]
-    )
-    feed_sum = scatter_sum(feed_parts, "tp")
-    return columns([feed_sum, gate_sum, out_sum])
+
+    def first(self):
+        self.sums = (
+            scatter_sum(self.halves[0], "ctx", 1).astype(low),
+            scatter_sum(self.halves[1], "dp", 0).astype(low),
+        )
+
+    def second(self):
+        self.sums = (
+            scatter_sum([self.sums[0]], "dp").astype(low),
+            scatter_sum([self.sums[1]], "ctx").astype(low),
+        )
+
+
+def feed_blocks(feed, inner):
+    rest = feed[:, inner:]
+    return [by_tp(feed[:, :inner]), jnp.broadcast_to(rest, (lax.axis_size("tp"),) + rest.shape)]
 
 
 def on_device(
@@ -576,7 +570,7 @@
         )
 
     def pack_small(c):
-        return jnp.concatenate(
+        vector = jnp.concatenate(
             [
                 conv_inner[0, :, c * half : (c + 1) * half].reshape(-1),
                 out_gain[0, c * half : (c + 1) * half],
@@ -586,6 +580,12 @@
                 conv_state[0].reshape(-1),
             ]
         )
+        parts = []
+        for _ in range(3):
+            part = lax.reduce_precision(vector, 8, 7)
+            parts.append(part.astype(low))
+            vector = vector - part
+        return as_rows(jnp.concatenate(parts), cut)
 
     def both_layers(make):
         zero, one = make(0), make(1)
@@ -593,10 +593,10 @@
         came = swap_cores(jnp.where(first, one, zero))
         return jnp.where(first, keep, came), jnp.where(first, came, keep)
 
-    small_layers = line_gather(jnp.stack(both_layers(pack_small)), "tp")
-
-    def layer_params(layer):
-        part = small_layers[:, layer]
+    def layer_params(rows_of_small):
+        size = (CONV + 1) * half + half + 3 * step_half + (CONV + 1) * 2 * STATE
+        three = rows_of_small.reshape(tp_count, -1)[:, : 3 * size].reshape(tp_count, 3, size)
+        part = jnp.sum(three.astype(full), axis=1)
         at = (CONV + 1) * half
         taps_inner = jnp.moveaxis(part[:, :at].reshape(tp_count, CONV + 1, half), 0, 1)
         gains = part[:, at : at + half].reshape(-1)
@@ -612,52 +612,52 @@
     cut = half + quarter + wide
     middle = tp_count // 2
 
-    def gather_feed(part):
+    def gather_item(part, sections):
         def side(pieces):
-            return columns(
-                [
-                    columns(pieces[..., :half]),
-                    columns(pieces[..., half : half + quarter]),
-                    columns(pieces[..., half + quarter :]),
-                ]
-            )
+            parts, at = [], 0
+            for size in sections:
+                parts.append(columns(pieces[..., at : at + size]))
+                at += size
+            return columns(parts)
 
         half_a, half_b = gather_rows(side(part[:middle]), side(part[middle:]))
-        x_end, s_end = middle * half, middle * (half + quarter)
-        feed = columns(
-            [
-                half_a[:, :x_end], half_b[:, :x_end], half_a[:, x_end:s_end], half_b[:, x_end:s_end],
-                half_a[:, s_end:], half_b[:, s_end:],
-            ]
-        )
-        return feed, half_a[:, s_end + step_half].astype(full)
-
-    def gather_pair(part):
-        def side(pieces):
-            return columns([columns(pieces[..., :half]), columns(pieces[..., half:])])
-
-        half_a, half_b = gather_rows(side(part[:middle]), side(part[middle:]))
-        x_end = middle * half
-        return (
-            columns([half_a[:, :x_end], half_b[:, :x_end]]),
-            columns([half_a[:, x_end:], half_b[:, x_end:]]),
-        )
-
+        result, at = [], 0
+        for size in sections:
+            result.append((half_a[:, at : at + middle * size], half_b[:, at : at + middle * size]))
+            at += middle * size
+        return result
+
+    def feed_weights(parts):
+        tails = [side.reshape(-1, middle, wide)[:, :, :step_half].reshape(-1, heads // 2) for side in parts[2]]
+        gain = parts[2][0][:, step_half].astype(full)
+        steps = jnp.pad(columns(tails), ((0, 0), (0, LANES - heads)))
+        return columns(parts[0] + parts[1] + (steps,)), gain
+
+    smalls = both_layers(pack_small)
     packs = both_layers(pack)
-    along = []
-    previous = None
-    for layer in range(2):
-        for part in (packs[layer][:, :cut], packs[layer][:, cut:]):
-            if previous is not None:
-                part, previous = lax.optimization_barrier((part, previous))
-            previous = line_gather(part, "tp")
-            along.append(previous)
-    weights, params = [], []
-    for layer in range(2):
-        feed, gain = gather_feed(along[2 * layer])
-        gate, out = gather_pair(along[2 * layer + 1])
-        weights.append((feed, gate, out))
-        params.append((gain,) + layer_params(layer))
+    feed_sections, pair_sections = (half, quarter, wide), (half, half)
+    along_feed = line_gather(jnp.concatenate([packs[0][:, :cut], smalls[0]], axis=0), "tp")
+    pair_pack, along_feed = tied(packs[0][:, cut:], along_feed)
+    along_pair = line_gather(pair_pack, "tp")
+    feed_parts = gather_item(along_feed[:, :own_rows], feed_sections)
+    last_pack, feed_parts = tied(packs[1], feed_parts)
+    small_pad = jnp.pad(smalls[1], ((0, 0), (0, last_pack.shape[1] - cut)))
+    along_last = line_gather(jnp.concatenate([last_pack, small_pad], axis=0), "tp")
+    pair_parts = gather_item(along_pair, pair_sections)
+    along_last, pair_parts = tied(along_last, pair_parts)
+    last_parts = gather_item(along_last[:, :own_rows, :cut], feed_sections)
+    along_last, last_parts = tied(along_last, last_parts)
+    last_parts += gather_item(along_last[:, :own_rows, cut:], pair_sections)
+    feed_first, gain_first = feed_weights(feed_parts)
+    feed_last, gain_last = feed_weights(last_parts[:3])
+    weights = [
+        (feed_first, columns(pair_parts[0]), columns(pair_parts[1])),
+        (feed_last, columns(last_parts[3]), columns(last_parts[4])),
+    ]
+    params = [
+        (gain_first,) + layer_params(along_feed[:, own_rows:]),
+        (gain_last,) + layer_params(along_last[:, own_rows:, :cut]),
+    ]
 
     places = lax.axis_index("ctx") * rows + jnp.arange(rows, dtype=jnp.int32)
     length = lax.dynamic_index_in_dim(lengths[:, 0], lane, 0, False)
@@ -672,18 +672,38 @@
     quarter_rows = rows // tp_count
     section_out = spread_rows(own_result.reshape(tp_count, quarter_rows, width), (0, 1))
 
-    delta_last, grads_last, small_last = layer_backward(
+    delta_last, grads_last, small_last, _ = layer_backward(
         out_grad, valid, weights[1], params[1], kept_last
     )
+    feed_last, gate_last, out_last = grads_last
+    share = inner // 4
+    last = Reduction([feed_last, out_last[:, :share]], [gate_last, out_last[:, share:]])
+
+    def last_blocks(sums):
+        at = feed_last.shape[1]
+        out_part = columns([sums[0][:, at:], sums[1][:, inner:]])
+        return [by_tp(sums[1][:, :inner]), by_tp(out_part)] + feed_blocks(sums[0][:, :at], inner)
+
+    last.blocks = last_blocks
+    last.first()
     spread_last = spread_rows(delta_last.astype(low).reshape(tp_count, quarter_rows, width), (1,))
-    sums_last = reduce_grads(grads_last, inner)
     incoming = (out_grad + delta_last).astype(low).astype(full)
-    delta_first, grads_first, small_first = layer_backward(
-        incoming, valid, weights[0], params[0], kept_first
-    )
+    delta_first, grads_first, small_first, early = layer_backward(
+        incoming, valid, weights[0], params[0], kept_first, last
+    )
+    feed_first = grads_first[0]
+    part = inner // 2 + LANES
+    feed = Reduction([feed_first[:, :part]], [feed_first[:, part:]])
+    feed.first()
+    small = jnp.stack([small_first, small_last])
     grad_first = (incoming + delta_first).astype(low)
     spread_first = spread_rows(grad_first.reshape(tp_count, quarter_rows, width), (0,))
-    sums_first = reduce_grads(grads_first, inner)
+    small = all_sum(all_sum(small, "ctx"), "dp")
+    feed.second()
+    payload = columns(feed_blocks(columns(feed.sums), inner))
+    extra = as_rows(small.astype(low).reshape(-1), payload.shape[2])
+    payload = jnp.concatenate([payload, jnp.broadcast_to(extra, (tp_count,) + extra.shape)], axis=1)
+    feed_sums = scatter_sum([payload], "tp")
     own_cotangent = lax.dynamic_slice_in_dim(
         cotangent[:, 0], lane * quarter_rows, quarter_rows, 1
     )
@@ -691,13 +711,20 @@
         first, spread_first.astype(full), own_cotangent + spread_last.astype(full)
     )
 
-    small = jnp.stack([small_first, small_last])
-    for axis in ("dp", "ctx", "tp"):
-        small = all_sum(small, axis)
-    small_keep = jnp.where(first, small[0], small[1])
-    small_came = swap_cores(jnp.where(first, small[1], small[0]))
-    keep = jnp.where(first, sums_first, sums_last)
-    came = swap_cores(jnp.where(first, sums_last, sums_first))
+    size = small_first.shape[0]
+    small_sums = feed_sums[own_rows:].reshape(-1)[: 2 * size].reshape(2, size)
+    sums_first = columns([early.sums, feed_sums[:own_rows]])
+    sums_last = last.sums
+    total_width = sums_first.shape[1]
+    joined = [
+        jnp.concatenate([sums, as_rows(vector, total_width)])
+        for sums, vector in zip((sums_first, sums_last), small_sums)
+    ]
+    keep = jnp.where(first, joined[0], joined[1])
+    came = swap_cores(jnp.where(first, joined[1], joined[0]))
+    small_keep = keep[own_rows:].reshape(-1)[:size]
+    small_came = came[own_rows:].reshape(-1)[:size]
+    keep, came = keep[:own_rows], came[:own_rows]
 
     def halves(kept_part, came_part, axis):
         zero = jnp.where(first, kept_part, came_part)
@@ -707,15 +734,17 @@
     def own_lane(value, shape, axis):
         return lax.dynamic_index_in_dim(value.reshape(shape), lane, axis, False)
 
+    grad_gate = halves(keep[:, :half], came[:, :half], 1)
     at = half
-    grad_x = halves(keep[:, :at], came[:, :at], 1)
-    grad_step = halves(keep[:, at : at + step_half], came[:, at : at + step_half], 1)
-    at += wide
+    grad_out = halves(keep[:, at : at + half].T, came[:, at : at + half].T, 0)
+    at += half
+    grad_x = halves(keep[:, at : at + half], came[:, at : at + half], 1)
+    at += half
     grad_state = keep[:, at : at + 2 * STATE] + came[:, at : at + 2 * STATE]
-    at += 2 * STATE
-    grad_gate = halves(keep[:, at : at + half], came[:, at : at + half], 1)
-    at += half
-    grad_out = halves(keep[:, at : at + half].T, came[:, at : at + half].T, 0)
+    at += 2 * STATE + lane * step_half
+    grad_step = halves(
+        lax.dynamic_slice_in_dim(keep, at, step_half, 1), lax.dynamic_slice_in_dim(came, at, step_half, 1), 1
+    )
     grad_gate_x = jnp.stack([grad_gate, grad_x], axis=1)
 
     at = (CONV + 1) * inner

time: 971 us -> 848 us (0.87)
  waiting for transfers between devices: 195 us -> 127 us
  starting transfers between devices: 209 us -> 149 us
  other arithmetic: 145 us -> 175 us
  local copies, waits for them, and re-layouts: 201 us -> 173 us
    ppermute x63 -> x39, waiting for transfers between devices: 159 us -> 97 us  [rotated(): lax.ppermute(value, axis, [(i, (i + steps) % count) for i in range(count)])]
    ppermute x38 -> x26, starting transfers between devices: 98.5 us -> 67.5 us  [shifted(): lax.ppermute(value, axis, [(source, source + steps) for source in range(f...]
    ppermute x63 -> x39, starting transfers between devices: 64.7 us -> 35.7 us  [rotated(): lax.ppermute(value, axis, [(i, (i + steps) % count) for i in range(count)])]
    ppermute x38 -> x26, waiting for transfers between devices: 36.1 us -> 21 us  [shifted(): lax.ppermute(value, axis, [(source, source + steps) for source in range(f...]
    reshape x13 -> x15, local copies, waits for them, and re-layouts: 21.9 us -> 9.86 us  [the longest x6 8.97 us: by_tp(): value.reshape(value.shape[0], lax.axis_size('tp'), -1)]
    unnamed x457 -> x498, local copies, waits for them, and re-layouts: 64 us -> 52 us
    broadcast_in_dim x6 -> x1, local copies, waits for them, and re-layouts: 10.2 us -> 0.01 us  [on_device(): jnp.broadcast_to(extra, (tp_count,) + extra.shape)]
    convert_element_type x26 -> x19, other arithmetic: 8.85 us -> 19 us  [the longest x3 5.03 us: first(): scatter_sum(self.halves[1], 'dp', 0).astype(low)]
  transfers between devices with their start and end apart: 120 -> 83, of which waited for: 31 -> 27; matrix products, arithmetic and copies ran while one was open for 37% -> 38% of each run, Pallas kernels for 9% -> 12%
where the time goes in v2:
time: 848 us; the launch traced here: 836 us
  other arithmetic  175 us (21%)
  local copies, waits for them, and re-layouts  173 us (20%)
  starting transfers between devices  149 us (18%)
  waiting for transfers between devices  127 us (15%)
  matrix products  106 us (12%)
  Pallas kernels  99.5 us (12%)
    ppermute x39, waiting for transfers between devices, rotated(): lax.ppermute(value, axis, [(i, (i + steps) % count) for i in range(count)])  97 us
    pallas_call x2, Pallas kernels, ssm_backward(): pl.pallas_call(bwd_kernel, grid=(blocks,), in_specs=[pl.BlockSpec((CHUNK,...  75 us
    ppermute x26, starting transfers between devices, shifted(): lax.ppermute(value, axis, [(source, source + steps) for source in range(f...  67.5 us
    unnamed x498, local copies, waits for them, and re-layouts  52 us
    dot_general x10, matrix products, dot_nn(): lax.dot_general(a, b, (((1,), (0,)), ((), ())), precision=precision, pref...  47.7 us
    ppermute x39, starting transfers between devices, rotated(): lax.ppermute(value, axis, [(i, (i + steps) % count) for i in range(count)])  35.7 us
    dot_general x10, matrix products, dot_tn(): lax.dot_general(a, b, (((0,), (0,)), ((), ())), precision=precision, pref...  30.2 us
    ppermute x9, starting transfers between devices, swap_cores(): return lax.ppermute(value, 'section', [(0, 1), (1, 0)])  27.2 us
  transfers between devices with their start and end apart: 83, of which 27 were waited for; matrix products, arithmetic and copies ran while one was open for 38% of the time, Pallas kernels for 12%

profile of v2, /device:TPU:1, one launch (start us, length us, event | category | flops | bytes accessed | tf_op | source)
XLA Modules:
  0.0 835.5 jit_solution(11391074229249681865)
XLA Ops:
  32.8 5.1 collective-permute-done.7
  87.8 5.9 fusion.220
  106.3 5.0 fusion.203
  124.2 4.8 collective-permute-start.15
  136.6 12.2 %ssm_forward.2 = (f32[1024,1024]{1,0:T(8,128)S(1)}, bf16[8,1024,128]{2,1,0:T(8,128)(2,1)S(1)}) custom-call(f32[1024,1280]{1,0:T(8,128)S(1)} %copy-done.3, f32[1024,1280]{1,0:T(8,128)S(1)} %copy-done.3, f32[1024,128]{1,0:T(8,128)S(1)} %pad.62.dt_ref, f32[1024,128]{1,0:T(8,128)S(1)} %pad.63.clone.cum_ref, f32[16,1024]{1,0:T(8,128)S(1)} %get-tuple-element.405.cumt_ref, ...), custom_call_target="tpu_custom_call" | custom-call | flops 1073741824 | bytes 10485760 | tf_op jit(solution)/shard_map/ssm_forward/pallas_call | solution.py:263
  174.5 8.4 %multiply_reduce_fusion.13 = (f32[1024]{0:T(1024)S(1)}, f32[1024,1024]{1,0:T(8,128)S(1)}, f32[1024,1024]{1,0:T(8,128)}) fusion(f32[1024,1024]{1,0:T(8,128)} %copy-done.20, bf16[1024,1024]{1,0:T(8,128)(2,1)} %constant_dynamic-update-slice_fusion.4, f32[1024]{0:T(1024)S(1)} %copy-done.159, f32[1024]{0:T(1024)S(1)} %copy-done.162, ...), kind=kOutput, calls=%fused_computation.112 | convolution fusion | flops 2159016960 | bytes 16789508 | tf_op jit(solution)/shard_map/dot_general | solution.py:24
  189.8 15.5 %collective-permute-start.31 = (bf16[1024,1024]{1,0:T(8,128)(2,1)}, bf16[1024,1024]{1,0:T(8,128)(2,1)}, u32[]{:S(2)}, u32[]{:S(2)}) collective-permute-start(bf16[1024,1024]{1,0:T(8,128)(2,1)} %convolution_convert_fusion.5), channel_id=1, source_target_pairs={{0,16},{16,0},{1,17},{17,1},{2,18},{18,2},{3,19},{19,3},{4,20},{20... | collective-permute-start | bytes 6291464 | tf_op jit(solution)/shard_map/ppermute | solution.py:93
  211.3 13.4 %collective-permute-done.35 = bf16[2,256,768]{2,1,0:T(8,128)(2,1)S(1)} collective-permute-done((bf16[2,256,768]{2,1,0:T(8,128)(2,1)S(1)}, bf16[2,256,768]{2,1,0:T(8,128)(2,1)S(1)}, u32[]{:S(2)}, u32[]{:S(2)}) %collective-permute-start.35) | collective-permute-done | bytes 786464 | tf_op jit(solution)/shard_map/ppermute | solution.py:49
  246.2 4.7 fusion.28
  266.0 4.9 fusion.199
  286.1 12.2 %ssm_forward.3 = (f32[1024,1024]{1,0:T(8,128)S(1)}, bf16[8,1024,128]{2,1,0:T(8,128)(2,1)S(1)}) custom-call(f32[1024,1280]{1,0:T(8,128)S(1)} %copy-done.5, f32[1024,1280]{1,0:T(8,128)S(1)} %copy-done.5, f32[1024,128]{1,0:T(8,128)S(1)} %pad.66.dt_ref, f32[1024,128]{1,0:T(8,128)S(1)} %pad.67.clone.cum_ref, f32[16,1024]{1,0:T(8,128)S(1)} %get-tuple-element.403.cumt_ref, ...), custom_call_target="tpu_custom_call" | custom-call | flops 1073741824 | bytes 10485760 | tf_op jit(solution)/shard_map/ssm_forward/pallas_call | solution.py:263
  304.2 4.9 multiply_reduce_fusion.12
  331.5 9.4 %multiply_reduce_fusion.8 = (f32[1024]{0:T(1024)}, f32[1024,1024]{1,0:T(8,128)S(1)}, bf16[1024,1024]{1,0:T(8,128)(2,1)}, f32[1024]{0:T(1024)}) fusion(f32[1024,1280]{1,0:T(8,128)S(1)} %bitcast.604, f32[1024,1024]{1,0:T(8,128)} %get-tuple-element.448, f32[1024,1024]{1,0:T(8,128)} %copy-done.203, f32[1024]{0:T(1024)S(1)} %get-tuple-element.207, ...), kind=kOutput, calls=%fused_computation.90 | convolution fusion | flops 2173696000 | bytes 27283456 | tf_op jit(solution)/shard_map/dot_general | solution.py:24
  340.9 6.1 fusion.77
  369.3 37.5 %ssm_backward.2 = (f32[1024,1024]{1,0:T(8,128)S(1)}, f32[1024,256]{1,0:T(8,128)S(1)}, f32[1024,128]{1,0:T(8,128)S(1)}, f32[1024,128]{1,0:T(8,128)S(1)}) custom-call(f32[1024,1280]{1,0:T(8,128)} %copy-done.4, f32[1024,1280]{1,0:T(8,128)} %copy-done.4, f32[1024,128]{1,0:T(8,128)S(1)} %pad.66.dt_ref, f32[1024,128]{1,0:T(8,128)S(1)} %pad.67.clone.cum_ref, ...), custom_call_target="tpu_custom_call" | custom-call | flops 4294967296 | bytes 16777216 | tf_op jit(solution)/shard_map/ssm_backward/pallas_call | solution.py:302
  406.9 13.2 %multiply_reduce_fusion = (f32[1280]{0:T(1024)S(1)}, f32[1280]{0:T(1024)S(1)}, f32[1280]{0:T(1024)S(1)}, f32[1280]{0:T(1024)S(1)}, f32[1280]{0:T(1024)S(1)}, /*index=5*/f32[1024,1280]{1,0:T(8,128)}) fusion(f32[1027,1280]{1,0:T(8,128)} %copy-done.25, f32[1024,1280]{1,0:T(8,128)} %get-tuple-element.215, f32[1024,256]{1,0:T(8,128)S(1)} %get-tuple-element.83, ...), kind=kLoop, calls=%fused_computation.47 | loop fusion | flops 23586560 | bytes 36725760 | tf_op jit(solution)/shard_map/reduce_sum | solution.py:472
  425.3 8.8 %fusion.15 = bf16[1024,1280]{1,0:T(8,128)(2,1)S(1)} fusion(f32[3,1280]{1,0:T(4,128)S(1)} %collective-permute-done.48, f32[1024,1280]{1,0:T(8,128)} %get-tuple-element.204, f32[1280]{0:T(1024)S(1)} %get-tuple-element.186, f32[1280]{0:T(1024)S(1)} %get-tuple-element.183, f32[1280]{0:T(1024)S(1)} %get-tuple-element.184, f32[1280]{0:T(1024)S(1)} %get-tuple-element.185), kind=kLoop, calls=%fused_computation.38 | loop fusion | flops 14417920 | bytes 7900160 | tf_op jit(solution)/shard_map/convert_element_type | solution.py:478
  443.2 4.7 add_convert_fusion.1
  469.5 8.4 %collective-permute-done.50 = bf16[2,256,1664]{2,1,0:T(8,128)(2,1)} collective-permute-done((bf16[2,256,1664]{2,1,0:T(8,128)(2,1)}, bf16[2,256,1664]{2,1,0:T(8,128)(2,1)}, u32[]{:S(2)}, u32[]{:S(2)}) %collective-permute-start.50) | collective-permute-done | bytes 1703968 | tf_op jit(solution)/shard_map/ppermute | solution.py:49
  479.8 5.1 fusion.35
  485.0 6.6 fusion.26
  492.8 7.5 fusion.64
  545.0 37.5 %ssm_backward.3 = (f32[1024,1024]{1,0:T(8,128)S(1)}, f32[1024,256]{1,0:T(8,128)S(1)}, f32[1024,128]{1,0:T(8,128)S(1)}, f32[1024,128]{1,0:T(8,128)S(1)}) custom-call(f32[1024,1280]{1,0:T(8,128)} %copy-done.2, f32[1024,1280]{1,0:T(8,128)} %copy-done.2, f32[1024,128]{1,0:T(8,128)S(1)} %copy-done.9, f32[1024,128]{1,0:T(8,128)S(1)} %copy-done.11, ...), custom_call_target="tpu_custom_call" | custom-call | flops 4294967296 | bytes 16777216 | tf_op jit(solution)/shard_map/ssm_backward/pallas_call | solution.py:302
  594.1 15.8 %collective-permute-done.55 = bf16[2,256,1024]{2,1,0:T(8,128)(2,1)S(1)} collective-permute-done((bf16[2,256,1024]{2,1,0:T(8,128)(2,1)S(1)}, bf16[2,256,1024]{2,1,0:T(8,128)(2,1)S(1)}, u32[]{:S(2)}, u32[]{:S(2)}) %collective-permute-start.55) | collective-permute-done | bytes 1048608 | tf_op jit(solution)/shard_map/ppermute | solution.py:49
  613.3 7.7 multiply_reduce_fusion.4
  646.2 8.9 %fusion.7 = bf16[1024,1280]{1,0:T(8,128)(2,1)S(1)} fusion(f32[3,1280]{1,0:T(4,128)S(1)} %collective-permute-done.57, f32[1024,1280]{1,0:T(8,128)} %get-tuple-element.199, f32[1280]{0:T(1024)S(1)} %copy-done.157, f32[1280]{0:T(1024)S(1)} %copy-done.151, f32[1280]{0:T(1024)S(1)} %copy-done.153, f32[1280]{0:T(1024)S(1)} %copy-done.155), kind=kLoop, calls=%fused_computation.30 | loop fusion | flops 14417920 | bytes 7900160 | tf_op jit(solution)/shard_map/convert_element_type | solution.py:478
  658.9 6.1 convolution_convert_fusion
  683.8 5.7 collective-permute-done.59
  697.7 4.8 constant_dynamic-slice_fusion.20
  712.8 14.5 %collective-permute-done.71 = bf16[256,512]{1,0:T(8,128)(2,1)S(1)} collective-permute-done((bf16[256,512]{1,0:T(8,128)(2,1)S(1)}, bf16[256,512]{1,0:T(8,128)(2,1)S(1)}, u32[]{:S(2)}, u32[]{:S(2)}) %collective-permute-start.71) | collective-permute-done | bytes 262176 | tf_op jit(solution)/shard_map/ppermute | solution.py:49
  756.6 30.8 %collective-permute-done.80 = bf16[288,640]{1,0:T(8,128)(2,1)S(1)} collective-permute-done((bf16[288,640]{1,0:T(8,128)(2,1)S(1)}, bf16[288,640]{1,0:T(8,128)(2,1)S(1)}, u32[]{:S(2)}, u32[]{:S(2)}) %collective-permute-start.80) | collective-permute-done | bytes 368672 | tf_op jit(solution)/shard_map/ppermute | solution.py:49
  808.9 5.5 fusion.45
  (1057 shorter events, 488.2 us)
Async XLA Ops:
  70.0 46.7 %collective-permute-start.26 = (bf16[256,1024]{1,0:T(8,128)(2,1)}, bf16[256,1024]{1,0:T(8,128)(2,1)}, u32[]{:S(2)}, u32[]{:S(2)}) collective-permute-start(bf16[256,1024]{1,0:T(8,128)(2,1)} %pad_maximum_fusion.33), channel_id=1, source_target_pairs={{0,4},{4,0},{1,5},{5,1},{2,6},{6,2},{3,7},{7,3},{8,12},{12,8},{9,1... | collective-permute-start | bytes 1572872 | tf_op jit(solution)/shard_map/ppermute | solution.py:49
  72.1 41.5 %collective-permute-start.28 = (bf16[256,1024]{1,0:T(8,128)(2,1)}, bf16[256,1024]{1,0:T(8,128)(2,1)}, u32[]{:S(2)}, u32[]{:S(2)}) collective-permute-start(bf16[256,1024]{1,0:T(8,128)(2,1)} %pad_maximum_fusion.34), channel_id=1, source_target_pairs={{0,8},{8,0},{1,9},{9,1},{2,10},{10,2},{3,11},{11,3},{4,12},{12,4},... | collective-permute-start | bytes 1572872 | tf_op jit(solution)/shard_map/ppermute | solution.py:49
  76.3 47.8 %collective-permute-start.14 = (bf16[288,896]{1,0:T(8,128)(2,1)}, bf16[288,896]{1,0:T(8,128)(2,1)}, u32[]{:S(2)}, u32[]{:S(2)}) collective-permute-start(bf16[288,896]{1,0:T(8,128)(2,1)} %fusion.95), channel_id=1, source_target_pairs={{0,1},{1,2},{2,3},{4,5},{5,6},{6,7},{8,9},{9,10},{10,11},{12,13},{... | collective-permute-start | bytes 1548296 | tf_op jit(solution)/shard_map/ppermute | solution.py:44
  79.8 49.2 %collective-permute-start.17 = (bf16[288,896]{1,0:T(8,128)(2,1)}, bf16[288,896]{1,0:T(8,128)(2,1)}, u32[]{:S(2)}, u32[]{:S(2)}) collective-permute-start(bf16[288,896]{1,0:T(8,128)(2,1)} %fusion.95), channel_id=1, source_target_pairs={{1,0},{2,1},{3,2},{5,4},{6,5},{7,6},{9,8},{10,9},{11,10},{13,12},{... | collective-permute-start | bytes 1548296 | tf_op jit(solution)/shard_map/ppermute | solution.py:44
  116.7 38.0 %collective-permute-start.29 = (bf16[2,256,1024]{2,1,0:T(8,128)(2,1)}, bf16[2,256,1024]{2,1,0:T(8,128)(2,1)}, u32[]{:S(2)}, u32[]{:S(2)}) collective-permute-start(bf16[2,256,1024]{2,1,0:T(8,128)(2,1)} %pad_maximum_fusion.21), channel_id=1, source_target_pairs={{0,4},{4,0},{1,5},{5,1},{2,6},{6,2},{3,7},{7,3},{8,12},{12,8},{9,1... | collective-permute-start | bytes 3145736 | tf_op jit(solution)/shard_map/ppermute | solution.py:49
  119.1 37.4 %collective-permute-start.27 = (bf16[2,256,1024]{2,1,0:T(8,128)(2,1)}, bf16[2,256,1024]{2,1,0:T(8,128)(2,1)}, u32[]{:S(2)}, u32[]{:S(2)}) collective-permute-start(bf16[2,256,1024]{2,1,0:T(8,128)(2,1)} %pad_maximum_fusion.20), channel_id=1, source_target_pairs={{0,8},{8,0},{1,9},{9,1},{2,10},{10,2},{3,11},{11,3},{4,12},{12,4},... | collective-permute-start | bytes 3145736 | tf_op jit(solution)/shard_map/ppermute | solution.py:49
  124.2 24.7 %collective-permute-start.15 = (bf16[288,896]{1,0:T(8,128)(2,1)}, bf16[288,896]{1,0:T(8,128)(2,1)}, u32[]{:S(2)}, u32[]{:S(2)}) collective-permute-start(bf16[288,896]{1,0:T(8,128)(2,1)} %collective-permute-done.14), channel_id=1, source_target_pairs={{0,1},{1,2},{2,3},{4,5},{5,6},{6,7},{8,9},{9,10},{10,11},{12,13},{... | collective-permute-start | bytes 1548296 | tf_op jit(solution)/shard_map/ppermute | solution.py:44
  171.1 34.2 %collective-permute-start.34 = (bf16[256,768]{1,0:T(8,128)(2,1)}, bf16[256,768]{1,0:T(8,128)(2,1)S(1)}, u32[]{:S(2)}, u32[]{:S(2)}) collective-permute-start(bf16[256,768]{1,0:T(8,128)(2,1)} %concatenate.219), channel_id=1, source_target_pairs={{0,8},{8,0},{1,9},{9,1},{2,10},{10,2},{3,11},{11,3},{4,12},{12,4},... | collective-permute-start | bytes 1179656 | tf_op jit(solution)/shard_map/ppermute | solution.py:49
  189.8 56.3 %collective-permute-start.31 = (bf16[1024,1024]{1,0:T(8,128)(2,1)}, bf16[1024,1024]{1,0:T(8,128)(2,1)}, u32[]{:S(2)}, u32[]{:S(2)}) collective-permute-start(bf16[1024,1024]{1,0:T(8,128)(2,1)} %convolution_convert_fusion.5), channel_id=1, source_target_pairs={{0,16},{16,0},{1,17},{17,1},{2,18},{18,2},{3,19},{19,3},{4,20},{20... | collective-permute-start | bytes 6291464 | tf_op jit(solution)/shard_map/ppermute | solution.py:93
  244.0 54.4 %collective-permute-start.41 = (bf16[2,256,1024]{2,1,0:T(8,128)(2,1)}, bf16[2,256,1024]{2,1,0:T(8,128)(2,1)}, u32[]{:S(2)}, u32[]{:S(2)}) collective-permute-start(bf16[2,256,1024]{2,1,0:T(8,128)(2,1)} %pad_maximum_fusion.23), channel_id=1, source_target_pairs={{0,4},{4,0},{1,5},{5,1},{2,6},{6,2},{3,7},{7,3},{8,12},{12,8},{9,1... | collective-permute-start | bytes 3145736 | tf_op jit(solution)/shard_map/ppermute | solution.py:49
  354.1 96.4 %collective-permute-start.44 = (bf16[256,1024]{1,0:T(8,128)(2,1)}, bf16[256,1024]{1,0:T(8,128)(2,1)}, u32[]{:S(2)}, u32[]{:S(2)}) collective-permute-start(bf16[256,1024]{1,0:T(8,128)(2,1)} %get-tuple-element.266), channel_id=1, source_target_pairs={{0,1},{1,2},{2,3},{3,0},{16,17},{17,18},{18,19},{19,16},{4,5},{5,6... | collective-permute-start | bytes 1572872 | tf_op jit(solution)/shard_map/ppermute | solution.py:109
  356.3 103.1 %collective-permute-start.45 = (bf16[256,1024]{1,0:T(8,128)(2,1)}, bf16[256,1024]{1,0:T(8,128)(2,1)}, u32[]{:S(2)}, u32[]{:S(2)}) collective-permute-start(bf16[256,1024]{1,0:T(8,128)(2,1)} %get-tuple-element.265), channel_id=1, source_target_pairs={{0,2},{1,3},{2,0},{3,1},{16,18},{17,19},{18,16},{19,17},{4,6},{5,7... | collective-permute-start | bytes 1572872 | tf_op jit(solution)/shard_map/ppermute | solution.py:109
  364.9 101.2 %collective-permute-start.51 = (bf16[2,256,1792]{2,1,0:T(8,128)(2,1)}, bf16[2,256,1792]{2,1,0:T(8,128)(2,1)}, u32[]{:S(2)}, u32[]{:S(2)}) collective-permute-start(bf16[2,256,1792]{2,1,0:T(8,128)(2,1)} %pad_maximum_fusion.8), channel_id=1, source_target_pairs={{0,8},{8,0},{1,9},{9,1},{2,10},{10,2},{3,11},{11,3},{4,12},{12,4},... | collective-permute-start | bytes 5505032 | tf_op jit(solution)/shard_map/ppermute | solution.py:49
  441.4 36.5 %collective-permute-start.50 = (bf16[2,256,1664]{2,1,0:T(8,128)(2,1)}, bf16[2,256,1664]{2,1,0:T(8,128)(2,1)}, u32[]{:S(2)}, u32[]{:S(2)}) collective-permute-start(bf16[2,256,1664]{2,1,0:T(8,128)(2,1)} %pad_maximum_fusion.9), channel_id=1, source_target_pairs={{0,4},{4,0},{1,5},{5,1},{2,6},{6,2},{3,7},{7,3},{8,12},{12,8},{9,1... | collective-permute-start | bytes 5111816 | tf_op jit(solution)/shard_map/ppermute | solution.py:49
  447.9 31.9 %collective-permute-start.49 = (bf16[1024,1024]{1,0:T(8,128)(2,1)}, bf16[1024,1024]{1,0:T(8,128)(2,1)}, u32[]{:S(2)}, u32[]{:S(2)}) collective-permute-start(bf16[1024,1024]{1,0:T(8,128)(2,1)} %add_convert_fusion.1), channel_id=1, source_target_pairs={{0,16},{16,0},{1,17},{17,1},{2,18},{18,2},{3,19},{19,3},{4,20},{20... | collective-permute-start | bytes 6291464 | tf_op jit(solution)/shard_map/ppermute | solution.py:93
  513.6 71.6 %collective-permute-start.67 = (bf16[256,1024]{1,0:T(8,128)(2,1)}, bf16[256,1024]{1,0:T(8,128)(2,1)}, u32[]{:S(2)}, u32[]{:S(2)}) collective-permute-start(bf16[256,1024]{1,0:T(8,128)(2,1)} %get-tuple-element.262), channel_id=1, source_target_pairs={{16,17},{17,18},{18,19},{19,16},{20,21},{21,22},{22,23},{23,20},{2... | collective-permute-start | bytes 1572872 | tf_op jit(solution)/shard_map/ppermute | solution.py:109
  516.3 70.2 %collective-permute-start.68 = (bf16[256,1024]{1,0:T(8,128)(2,1)}, bf16[256,1024]{1,0:T(8,128)(2,1)}, u32[]{:S(2)}, u32[]{:S(2)}) collective-permute-start(bf16[256,1024]{1,0:T(8,128)(2,1)} %get-tuple-element.261), channel_id=1, source_target_pairs={{16,18},{17,19},{18,16},{19,17},{20,22},{21,23},{22,20},{23,21},{2... | collective-permute-start | bytes 1572872 | tf_op jit(solution)/shard_map/ppermute | solution.py:109
  519.8 68.0 %collective-permute-start.69 = (bf16[256,1024]{1,0:T(8,128)(2,1)}, bf16[256,1024]{1,0:T(8,128)(2,1)}, u32[]{:S(2)}, u32[]{:S(2)}) collective-permute-start(bf16[256,1024]{1,0:T(8,128)(2,1)} %get-tuple-element.260), channel_id=1, source_target_pairs={{16,19},{17,16},{18,17},{19,18},{20,23},{21,20},{22,21},{23,22},{2... | collective-permute-start | bytes 1572872 | tf_op jit(solution)/shard_map/ppermute | solution.py:109
  530.4 59.8 %collective-permute-start.53 = (bf16[256,1664]{1,0:T(8,128)(2,1)}, bf16[256,1664]{1,0:T(8,128)(2,1)}, u32[]{:S(2)}, u32[]{:S(2)}) collective-permute-start(bf16[256,1664]{1,0:T(8,128)(2,1)} %dynamic-slice_bitcast_fusion.7), channel_id=1, source_target_pairs={{0,8},{8,0},{1,9},{9,1},{2,10},{10,2},{3,11},{11,3},{4,12},{12,4},... | collective-permute-start | bytes 2555912 | tf_op jit(solution)/shard_map/ppermute | solution.py:49
  540.6 51.1 %collective-permute-start.54 = (bf16[256,1792]{1,0:T(8,128)(2,1)}, bf16[256,1792]{1,0:T(8,128)(2,1)}, u32[]{:S(2)}, u32[]{:S(2)}) collective-permute-start(bf16[256,1792]{1,0:T(8,128)(2,1)} %dynamic-slice_bitcast_fusion.6), channel_id=1, source_target_pairs={{0,4},{4,0},{1,5},{5,1},{2,6},{6,2},{3,7},{7,3},{8,12},{12,8},{9,1... | collective-permute-start | bytes 2752520 | tf_op jit(solution)/shard_map/ppermute | solution.py:49
  637.6 46.2 %collective-permute-start.60 = (bf16[256,1152]{1,0:T(8,128)(2,1)}, bf16[256,1152]{1,0:T(8,128)(2,1)}, u32[]{:S(2)}, u32[]{:S(2)}) collective-permute-start(bf16[256,1152]{1,0:T(8,128)(2,1)} %get-tuple-element.398), channel_id=1, source_target_pairs={{0,3},{1,0},{2,1},{3,2},{4,7},{5,4},{6,5},{7,6},{8,11},{9,8},{10,9... | collective-permute-start | bytes 1769480 | tf_op jit(solution)/shard_map/ppermute | solution.py:49
  637.6 51.9 %collective-permute-start.59 = (bf16[256,1152]{1,0:T(8,128)(2,1)}, bf16[256,1152]{1,0:T(8,128)(2,1)}, u32[]{:S(2)}, u32[]{:S(2)}) collective-permute-start(bf16[256,1152]{1,0:T(8,128)(2,1)} %get-tuple-element.397), channel_id=1, source_target_pairs={{0,2},{1,3},{2,0},{3,1},{4,6},{5,7},{6,4},{7,5},{8,10},{9,11},{10,... | collective-permute-start | bytes 1769480 | tf_op jit(solution)/shard_map/ppermute | solution.py:49
  638.9 50.7 %collective-permute-start.58 = (bf16[256,1152]{1,0:T(8,128)(2,1)}, bf16[256,1152]{1,0:T(8,128)(2,1)}, u32[]{:S(2)}, u32[]{:S(2)}) collective-permute-start(bf16[256,1152]{1,0:T(8,128)(2,1)} %get-tuple-element.396), channel_id=1, source_target_pairs={{0,1},{1,2},{2,3},{3,0},{4,5},{5,6},{6,7},{7,4},{8,9},{9,10},{10,1... | collective-permute-start | bytes 1769480 | tf_op jit(solution)/shard_map/ppermute | solution.py:49
  642.3 36.0 %collective-permute-start.61 = (bf16[256,1024]{1,0:T(8,128)(2,1)}, bf16[256,1024]{1,0:T(8,128)(2,1)}, u32[]{:S(2)}, u32[]{:S(2)}) collective-permute-start(bf16[256,1024]{1,0:T(8,128)(2,1)} %dynamic-slice_bitcast_fusion.17), channel_id=1, source_target_pairs={{0,8},{8,0},{1,9},{9,1},{2,10},{10,2},{3,11},{11,3},{4,12},{12,4},... | collective-permute-start | bytes 1572872 | tf_op jit(solution)/shard_map/ppermute | solution.py:49
  644.1 37.7 %collective-permute-start.62 = (bf16[256,1024]{1,0:T(8,128)(2,1)}, bf16[256,1024]{1,0:T(8,128)(2,1)}, u32[]{:S(2)}, u32[]{:S(2)}) collective-permute-start(bf16[256,1024]{1,0:T(8,128)(2,1)} %dynamic-slice_bitcast_fusion.16), channel_id=1, source_target_pairs={{0,4},{4,0},{1,5},{5,1},{2,6},{6,2},{3,7},{7,3},{8,12},{12,8},{9,1... | collective-permute-start | bytes 1572872 | tf_op jit(solution)/shard_map/ppermute | solution.py:49
  678.3 30.0 %collective-permute-start.75 = (bf16[2,256,768]{1,2,0:T(8,128)(2,1)}, bf16[2,256,768]{1,2,0:T(8,128)(2,1)}, u32[]{:S(2)}, u32[]{:S(2)}) collective-permute-start(bf16[2,256,768]{1,2,0:T(8,128)(2,1)} %bitcast.641), channel_id=1, source_target_pairs={{0,8},{8,0},{1,9},{9,1},{2,10},{10,2},{3,11},{11,3},{4,12},{12,4},... | collective-permute-start | bytes 2359304 | tf_op jit(solution)/shard_map/ppermute | solution.py:49
  691.4 37.9 %collective-permute-start.63 = (bf16[1024,1024]{1,0:T(8,128)(2,1)S(1)}, bf16[1024,1024]{1,0:T(8,128)(2,1)}, u32[]{:S(2)}, u32[]{:S(2)}) collective-permute-start(bf16[1024,1024]{1,0:T(8,128)(2,1)S(1)} %add_convert_fusion), channel_id=1, source_target_pairs={{0,16},{16,0},{1,17},{17,1},{2,18},{18,2},{3,19},{19,3},{4,20},{20... | collective-permute-start | bytes 6291464 | tf_op jit(solution)/shard_map/ppermute | solution.py:93
  743.9 43.5 %collective-permute-start.80 = (bf16[288,640]{1,0:T(8,128)(2,1)S(1)}, bf16[288,640]{1,0:T(8,128)(2,1)S(1)}, u32[]{:S(2)}, u32[]{:S(2)}) collective-permute-start(bf16[288,640]{1,0:T(8,128)(2,1)S(1)} %get-tuple-element.333), channel_id=1, source_target_pairs={{0,2},{1,3},{2,0},{3,1},{4,6},{5,7},{6,4},{7,5},{8,10},{9,11},{10,... | collective-permute-start | bytes 1105928 | tf_op jit(solution)/shard_map/ppermute | solution.py:49
  745.8 41.6 %collective-permute-start.79 = (bf16[288,640]{1,0:T(8,128)(2,1)S(1)}, bf16[288,640]{1,0:T(8,128)(2,1)S(1)}, u32[]{:S(2)}, u32[]{:S(2)}) collective-permute-start(bf16[288,640]{1,0:T(8,128)(2,1)S(1)} %get-tuple-element.331), channel_id=1, source_target_pairs={{0,1},{1,2},{2,3},{3,0},{4,5},{5,6},{6,7},{7,4},{8,9},{9,10},{10,1... | collective-permute-start | bytes 1105928 | tf_op jit(solution)/shard_map/ppermute | solution.py:49
  751.9 53.7 %collective-permute-start.64 = (bf16[256,1024]{1,0:T(8,128)(2,1)}, bf16[256,1024]{1,0:T(8,128)(2,1)}, u32[]{:S(2)}, u32[]{:S(2)}) collective-permute-start(bf16[256,1024]{1,0:T(8,128)(2,1)} %get-tuple-element.256), channel_id=1, source_target_pairs={{0,1},{1,2},{2,3},{3,0},{4,5},{5,6},{6,7},{7,4},{8,9},{9,10},{10,1... | collective-permute-start | bytes 1572872 | tf_op jit(solution)/shard_map/ppermute | solution.py:109
  753.6 53.2 %collective-permute-start.65 = (bf16[256,1024]{1,0:T(8,128)(2,1)}, bf16[256,1024]{1,0:T(8,128)(2,1)}, u32[]{:S(2)}, u32[]{:S(2)}) collective-permute-start(bf16[256,1024]{1,0:T(8,128)(2,1)} %get-tuple-element.255), channel_id=1, source_target_pairs={{0,2},{1,3},{2,0},{3,1},{4,6},{5,7},{6,4},{7,5},{8,10},{9,11},{10,... | collective-permute-start | bytes 1572872 | tf_op jit(solution)/shard_map/ppermute | solution.py:109
  755.0 52.8 %collective-permute-start.66 = (bf16[256,1024]{1,0:T(8,128)(2,1)}, bf16[256,1024]{1,0:T(8,128)(2,1)}, u32[]{:S(2)}, u32[]{:S(2)}) collective-permute-start(bf16[256,1024]{1,0:T(8,128)(2,1)} %get-tuple-element.254), channel_id=1, source_target_pairs={{0,3},{1,0},{2,1},{3,2},{4,7},{5,4},{6,5},{7,6},{8,11},{9,8},{10,9... | collective-permute-start | bytes 1572872 | tf_op jit(solution)/shard_map/ppermute | solution.py:109
  (271 other events, 3042.9 us)

commit v3 on v2

--- a/solution.py
+++ b/solution.py
@@ -13,6 +13,7 @@
 CONV = 4
 CHUNK = 128
 LANES = 128
+RIM = 16
 
 highest = lax.Precision.HIGHEST
 epsilon = 1e-05
@@ -129,6 +130,100 @@
 
 def tied(value, other):
     return lax.optimization_barrier((value, other))
+
+
+def conv_taps_sum(taps_ref, rows_of):
+    total = taps_ref[CONV : CONV + 1, :]
+    for k in range(CONV):
+        total = total + taps_ref[k : k + 1, :] * rows_of(k)
+    return total
+
+
+def prep_kernel(
+    feed_ref, rim_ref, taps_ref, raw_ref, bias_ref, rate_ref,
+    act_ref, dt_ref, cum_ref, cumt_ref, since_ref, local_ref,
+    window, run,
+):
+    inner = local_ref.shape[0]
+
+    @pl.when(pl.program_id(0) == 0)
+    def _():
+        window[:RIM, :] = rim_ref[...].astype(full)
+        run[...] = jnp.zeros_like(run)
+        local_ref[...] = jnp.zeros_like(local_ref)
+
+    window[RIM:, :] = feed_ref[...].astype(full)
+    pre = conv_taps_sum(taps_ref, lambda k: window[RIM - CONV + 1 + k : RIM - CONV + 1 + k + CHUNK, :])
+    act = pre * jax.nn.sigmoid(pre)
+    act_ref[...] = act
+    window[:RIM, :] = window[CHUNK:, :]
+    raw = raw_ref[...] + bias_ref[...]
+    dt = jnp.maximum(raw, 0.0) + jnp.log1p(jnp.exp(-jnp.abs(raw)))
+    row = lax.broadcasted_iota(jnp.int32, (CHUNK, CHUNK), 0)
+    col = lax.broadcasted_iota(jnp.int32, (CHUNK, CHUNK), 1)
+    cum = dot_nn((row >= col).astype(full), rate_ref[...] * dt, highest)
+    dt_ref[...] = dt
+    cum_ref[...] = cum
+    cumt_ref[...] = cum.T[: cumt_ref.shape[0]]
+    since_ref[...] = jnp.exp(run[0:1, :] + cum)
+    end = cum[CHUNK - 1 : CHUNK, :]
+    run[...] = run[...] + end
+    weight = jnp.exp(end - cum) * dt
+    shrink = jnp.exp(end)
+    left = col < HEADDIM
+    upper = row < HEADDIM
+    b_low = act[:, inner : inner + STATE].astype(low)
+    for pair in range(inner // LANES):
+        h0, h1 = 2 * pair, 2 * pair + 1
+        span = slice(pair * LANES, (pair + 1) * LANES)
+        each = jnp.where(left, weight[:, h0 : h0 + 1], weight[:, h1 : h1 + 1])
+        fresh = dot_tn((act[:, span] * each).astype(low), b_low)
+        keep = jnp.where(upper, shrink[:, h0 : h0 + 1], shrink[:, h1 : h1 + 1])
+        local_ref[span, :] = keep * local_ref[span, :] + fresh
+
+
+def mixer_prep(feed, rim, taps, raw, bias, rate, heads):
+    rows, channels = feed.shape
+    inner = heads * HEADDIM
+    lanes = pl.BlockSpec((CHUNK, LANES), lambda i: (i, 0))
+    lane_row = pl.BlockSpec((1, LANES), lambda i: (0, 0))
+    by_lane = jax.ShapeDtypeStruct((rows, LANES), full)
+    return pl.pallas_call(
+        prep_kernel,
+        grid=(rows // CHUNK,),
+        in_specs=[
+            pl.BlockSpec((CHUNK, channels), lambda i: (i, 0)),
+            pl.BlockSpec((RIM, channels), lambda i: (0, 0)),
+            pl.BlockSpec((8, channels), lambda i: (0, 0)),
+            lanes,
+            lane_row,
+            lane_row,
+        ],
+        out_specs=[
+            pl.BlockSpec((CHUNK, channels), lambda i: (i, 0)),
+            lanes,
+            lanes,
+            pl.BlockSpec((heads, CHUNK), lambda i: (0, i)),
+            lanes,
+            pl.BlockSpec((inner, STATE), lambda i: (0, 0)),
+        ],
+        out_shape=[
+            jax.ShapeDtypeStruct((rows, channels), full),
+            by_lane,
+            by_lane,
+            jax.ShapeDtypeStruct((heads, rows), full),
+            by_lane,
+            jax.ShapeDtypeStruct((inner, STATE), full),
+        ],
+        scratch_shapes=[pltpu.VMEM((CHUNK + RIM, channels), full), pltpu.VMEM((8, LANES), full)],
+        compiler_params=pltpu.CompilerParams(
+            dimension_semantics=("arbitrary",), vmem_limit_bytes=40 * 1024 * 1024
+        ),
+        cost_estimate=pl.CostEstimate(
+            flops=rows * inner * 2 * STATE, bytes_accessed=rows * channels * 6, transcendentals=rows * channels
+        ),
+        name="mixer_prep",
+    )(feed, rim, taps, raw, bias, rate)
 
 
 def fwd_kernel(x_ref, bc_ref, dt_ref, cum_ref, cumt_ref, skip_ref, enter_ref, y_ref, start_ref, state):
@@ -171,12 +266,22 @@
 
 def bwd_kernel(
     x_ref, bc_ref, dt_ref, cum_ref, cumt_ref, skip_ref, dy_ref, start_ref, later_ref,
-    dx_ref, dbc_ref, ddt_ref, dlog_ref,
-    adjoint, dye, uw, xdu, dyi, udu,
+    feed_ref, before_ref, rim_ref, taps_ref, raw_ref, bias_ref, rate_ref,
+    back_ref, first_ref, sums_ref, head_sums_ref,
+    adjoint, dye, uw, xdu, dyi, udu, window, back,
 ):
+    channels = feed_ref.shape[1]
+
     @pl.when(pl.program_id(0) == 0)
     def _():
         adjoint[...] = later_ref[...].astype(full)
+        back[CHUNK:, :] = jnp.zeros((8, channels), full)
+        sums_ref[...] = jnp.zeros_like(sums_ref)
+        head_sums_ref[...] = jnp.zeros_like(head_sums_ref)
+
+    at_start = pl.program_id(0) == pl.num_programs(0) - 1
+    window[:RIM, :] = jnp.where(at_start, rim_ref[...].astype(full), before_ref[...].astype(full))
+    window[RIM:, :] = feed_ref[...].astype(full)
 
     heads = cumt_ref.shape[0]
     inner = heads * HEADDIM
@@ -223,7 +328,8 @@
         since = jnp.exp(cum_pair)
         du_state = ahead * dot_nt(b_low, adjoint[span, :].astype(low))
         du = dot_tn(w_both, dy_both) + du_state
-        dx_ref[:, span] = dt_pair * du + skip_ref[:, span] * dy_pair
+        back[:CHUNK, span] = dt_pair * du + skip_ref[:, span] * dy_pair
+        sums_ref[CONV + 1 : CONV + 2, span] += jnp.sum(x_pair * dy_pair, axis=0, keepdims=True)
         y_state = since * dot_nt(c_low, start_ref[0, span, :])
         xdu[:, span] = x_pair * du
         dyi[:, span] = dy_pair * y_state
@@ -233,7 +339,7 @@
     inner_row = lax.broadcasted_iota(jnp.int32, (inner, LANES), 0)
     inner_col = lax.broadcasted_iota(jnp.int32, (inner, LANES), 1)
     pick = (inner_row // HEADDIM == inner_col).astype(full)
-    ddt_ref[...] = dot_nn(xdu[...], pick, highest)
+    ddt = dot_nn(xdu[...], pick, highest)
     by_state = dot_nn(dyi[...], pick, highest)
     by_later = dot_nn(udu[...], pick, highest)
     adjoint_now = adjoint[...]
@@ -243,16 +349,44 @@
     ends = jnp.exp(cum_ref[CHUNK - 1 : CHUNK, :])
     dlog = dlog + over[0:1] * ends
     dlog = dlog + dot_nn((row <= col).astype(full), by_state, highest)
-    dlog_ref[...] = dlog + dot_nn((row > col).astype(full), by_later, highest)
+    dlog = dlog + dot_nn((row > col).astype(full), by_later, highest)
+    rate = rate_ref[...]
+    step = (ddt + rate * dlog) * jax.nn.sigmoid(raw_ref[...] + bias_ref[...])
+    back_ref[:, channels:] = step.astype(low)
+    head_sums_ref[0:1, :] += jnp.sum(step, axis=0, keepdims=True)
+    head_sums_ref[1:2, :] += jnp.sum(dlog * rate * dt_ref[...], axis=0, keepdims=True)
     d_aff = jnp.where(causal, d_affinity, 0.0).astype(low)
-    dbc_ref[:, :STATE] = dot_tn(d_aff, c_low) + dot_nn(uw[...], adjoint_now.astype(low))
-    dbc_ref[:, STATE:] = dot_nn(d_aff, b_low) + dot_nn(dye[...], start_now)
+    back[:CHUNK, inner : inner + STATE] = dot_tn(d_aff, c_low) + dot_nn(uw[...], adjoint_now.astype(low))
+    back[:CHUNK, inner + STATE :] = dot_nn(d_aff, b_low) + dot_nn(dye[...], start_now)
     fresh = dot_tn(dye[...], c_low)
     for pair in range(heads // 2):
         h0, h1 = 2 * pair, 2 * pair + 1
         span = slice(pair * LANES, (pair + 1) * LANES)
         shrink = jnp.where(row < HEADDIM, ends[:, h0 : h0 + 1], ends[:, h1 : h1 + 1])
         adjoint[span, :] = shrink * adjoint_now[span, :] + fresh[span, :]
+    for group in range(channels // LANES):
+        span = slice(group * LANES, (group + 1) * LANES)
+        taken = [
+            window[RIM - CONV + 1 + k : RIM - CONV + 1 + k + CHUNK, span] for k in range(CONV)
+        ]
+        pre = taps_ref[CONV : CONV + 1, span]
+        for k in range(CONV):
+            pre = pre + taps_ref[k : k + 1, span] * taken[k]
+        sig = jax.nn.sigmoid(pre)
+        back_pre = back[:CHUNK, span] * (sig * (1.0 + pre * (1.0 - sig)))
+        back[:CHUNK, span] = back_pre
+        for k in range(CONV):
+            sums_ref[k : k + 1, span] += jnp.sum(back_pre * taken[k], axis=0, keepdims=True)
+        sums_ref[CONV : CONV + 1, span] += jnp.sum(back_pre, axis=0, keepdims=True)
+        total = taps_ref[CONV - 1 : CONV, span] * back_pre
+        for k in range(CONV - 1):
+            total = total + taps_ref[k : k + 1, span] * back[CONV - 1 - k : CONV - 1 - k + CHUNK, span]
+        back_ref[:, span] = total.astype(low)
+    back[CHUNK:, :] = back[:8, :]
+
+    @pl.when(at_start)
+    def _():
+        first_ref[...] = back[:8, :]
 
 
 def ssm_forward(act, dt, cum, cum_t, skip_row, entering):
@@ -293,8 +427,10 @@
     )(act, act, dt, cum, cum_t, skip_row, entering)
 
 
-def ssm_backward(act, dt, cum, cum_t, skip_row, dy, starts, later):
-    rows = act.shape[0]
+def ssm_backward(act, dt, cum, cum_t, skip_row, dy, starts, later, feed, rim, taps, raw, bias, rate):
+    rows, channels = feed.shape
+    lane_row = pl.BlockSpec((1, LANES), lambda i: (0, 0))
+    per_block = CHUNK // RIM
     heads = cum_t.shape[0]
     inner = heads * HEADDIM
     blocks = rows // CHUNK
@@ -312,18 +448,25 @@
             pl.BlockSpec((CHUNK, inner), lambda i: (last - i, 0)),
             pl.BlockSpec((1, inner, STATE), lambda i: (last - i, 0, 0)),
             pl.BlockSpec((inner, STATE), lambda i: (0, 0)),
+            pl.BlockSpec((CHUNK, channels), lambda i: (last - i, 0)),
+            pl.BlockSpec((RIM, channels), lambda i: (jnp.maximum((last - i) * per_block - 1, 0), 0)),
+            pl.BlockSpec((RIM, channels), lambda i: (0, 0)),
+            pl.BlockSpec((8, channels), lambda i: (0, 0)),
+            pl.BlockSpec((CHUNK, LANES), lambda i: (last - i, 0)),
+            lane_row,
+            lane_row,
         ],
         out_specs=[
-            pl.BlockSpec((CHUNK, inner), lambda i: (last - i, 0)),
-            pl.BlockSpec((CHUNK, 2 * STATE), lambda i: (last - i, 0)),
-            pl.BlockSpec((CHUNK, LANES), lambda i: (last - i, 0)),
-            pl.BlockSpec((CHUNK, LANES), lambda i: (last - i, 0)),
+            pl.BlockSpec((CHUNK, channels + LANES), lambda i: (last - i, 0)),
+            pl.BlockSpec((8, channels), lambda i: (0, 0)),
+            pl.BlockSpec((8, channels), lambda i: (0, 0)),
+            pl.BlockSpec((8, LANES), lambda i: (0, 0)),
         ],
         out_shape=[
-            jax.ShapeDtypeStruct((rows, inner), full),
-            jax.ShapeDtypeStruct((rows, 2 * STATE), full),
-            jax.ShapeDtypeStruct((rows, LANES), full),
-            jax.ShapeDtypeStruct((rows, LANES), full),
+            jax.ShapeDtypeStruct((rows, channels + LANES), low),
+            jax.ShapeDtypeStruct((8, channels), full),
+            jax.ShapeDtypeStruct((8, channels), full),
+            jax.ShapeDtypeStruct((8, LANES), full),
         ],
         scratch_shapes=[
             pltpu.VMEM((inner, STATE), full),
@@ -332,6 +475,8 @@
             pltpu.VMEM((CHUNK, inner), full),
             pltpu.VMEM((CHUNK, inner), full),
             pltpu.VMEM((CHUNK, inner), full),
+            pltpu.VMEM((CHUNK + RIM, channels), full),
+            pltpu.VMEM((CHUNK + 8, channels), full),
         ],
         compiler_params=pltpu.CompilerParams(
             dimension_semantics=("arbitrary",), vmem_limit_bytes=40 * 1024 * 1024
@@ -342,7 +487,7 @@
             transcendentals=rows * heads * CHUNK * 2,
         ),
         name="ssm_backward",
-    )(act, act, dt, cum, cum_t, skip_row, dy, starts, later)
+    )(act, act, dt, cum, cum_t, skip_row, dy, starts, later, feed, feed, rim, taps, raw, bias, rate)
 
 
 def heads_to_channels(values):
@@ -367,32 +512,20 @@
     normed = (hidden * norm * gain).astype(low)
     feed_all = dot_nn(normed, feed_weight)
     feed = feed_all[:, :channels].astype(low)
-    raw_step = feed_all[:, channels : channels + heads]
-    rim = shifted(feed[rows - CONV + 1 :], "ctx", 1)
-    padded = jnp.concatenate([rim, feed], axis=0)
+    raw = feed_all[:, channels:]
+    rim = shifted(feed[rows - RIM :], "ctx", 1)
     gate = dot_nn(normed, gate_weight)
-    pre = conv_total(padded, taps, rows)
-    act = pre * jax.nn.sigmoid(pre)
-    dt = jax.nn.softplus(raw_step + step_bias)
-    log_decay = -jnp.exp(decay_log) * dt
-    blocks = rows // CHUNK
-    tril = jnp.tril(jnp.ones((CHUNK, CHUNK), full))
-    cum = jnp.einsum("ts,csh->cth", tril, log_decay.reshape(blocks, CHUNK, heads), precision=highest)
-    ends = cum[:, -1]
-    running = jnp.cumsum(ends, axis=0)
-    total = running[-1]
-    since = (running - ends)[:, None] + cum
-    decay_in = jnp.exp(since).reshape(rows, heads)
-    to_end = jnp.exp(total - since).reshape(rows, heads) * dt
-    cum = cum.reshape(rows, heads)
-    weighted = (act[:, :inner] * heads_to_channels(to_end)).astype(low)
-    local_state = dot_tn(weighted, act[:, inner : inner + STATE].astype(low))
-    shrink = jnp.repeat(jnp.exp(total), HEADDIM)[:, None]
+    lanes = ((0, 0), (0, LANES - heads))
+    bias = jnp.pad(step_bias[None], lanes)
+    rate = jnp.pad(-jnp.exp(decay_log)[None], lanes)
+    taps = jnp.pad(taps, ((0, 8 - CONV - 1), (0, 0)))
+    act, dt, cum, cum_t, since, local_state = mixer_prep(feed, rim, taps, raw, bias, rate, heads)
+    shrink = jnp.repeat(since[rows - 1, :heads], HEADDIM)[:, None]
     entering = chain(local_state, shrink, 1)
-    lanes = ((0, 0), (0, LANES - heads))
     skip_row = jnp.repeat(skip, HEADDIM)[None]
-    scan = (jnp.pad(dt, lanes), jnp.pad(cum, lanes), cum.T, skip_row)
-    ssm_out, starts = ssm_forward(act, *scan, entering)
+    scan = (act, dt, cum, cum_t, skip_row)
+    conv = (feed, rim, taps, raw, bias, rate)
+    ssm_out, starts = ssm_forward(*scan, entering)
     gated = ssm_out * (gate * jax.nn.sigmoid(gate))
     squares = jnp.sum(gated * gated, axis=-1)
     scaled = (gated * out_gain).astype(low)
@@ -402,15 +535,10 @@
     out_norm = lax.rsqrt(squares / INNER + epsilon)[:, None]
     result = hidden + valid * out_norm * branch
     kept = (
-        hidden, norm, normed, padded, act, gate, raw_step, dt, log_decay, decay_in, shrink,
-        scan, starts, ssm_out, scaled, branch.astype(low), out_norm,
+        hidden, norm, normed, act, gate, since, shrink,
+        scan, conv, starts, ssm_out, scaled, branch.astype(low), out_norm,
     )
     return result, kept
-
-
-def conv_total(padded, taps, rows):
-    wide = padded.astype(full)
-    return taps[CONV] + sum(taps[k] * wide[k : k + rows] for k in range(CONV))
 
 
 def chain(local_state, shrink, steps):
@@ -425,8 +553,8 @@
     gain, taps, step_bias, decay_log, skip, out_gain = params
     feed_weight, gate_weight, out_weight = weights
     (
-        hidden, norm, normed, padded, act, gate, raw_step, dt, log_decay, decay_in, shrink,
-        scan, starts, ssm_out, scaled, branch, out_norm,
+        hidden, norm, normed, act, gate, since, shrink,
+        scan, conv, starts, ssm_out, scaled, branch, out_norm,
     ) = kept
     rows, width = hidden.shape
     heads = step_bias.shape[0]
@@ -445,7 +573,7 @@
     back_ssm = back_gated * silu
     back_gate = (back_gated * ssm_out * silu_slope(gate, sig)).astype(low)
     grad_gate = dot_tn(normed, back_gate).astype(low)
-    weighted = (back_ssm * heads_to_channels(decay_in)).astype(low)
+    weighted = (back_ssm * heads_to_channels(since[:, :heads])).astype(low)
     local_adjoint = dot_tn(weighted, act[:, inner + STATE :].astype(low))
     later = chain(local_adjoint, shrink, -1)
     early = None
@@ -454,28 +582,22 @@
         back_ssm, pending.sums = tied(back_ssm, pending.sums)
         pending.second()
         early.first()
-    back_x, back_bc, back_dt, back_log = ssm_backward(act, *scan, back_ssm, starts, later)
+    back_all, first_rows, sums, head_sums = ssm_backward(*scan, back_ssm, starts, later, *conv)
+    following = shifted(first_rows, "ctx", -1)
+    taps = conv[2]
+    edge = sum(
+        jnp.pad(taps[k] * following[: CONV - 1 - k], ((RIM - CONV + 1 + k, 0), (0, LANES))) for k in range(CONV - 1)
+    )
+    back_all = lax.dynamic_update_slice_in_dim(
+        back_all, (back_all[rows - RIM :].astype(full) + edge).astype(low), rows - RIM, 0
+    )
     if pending is not None:
-        back_x, (pending.sums, early.sums) = tied(back_x, (pending.sums, early.sums))
+        back_all, (pending.sums, early.sums) = tied(back_all, (pending.sums, early.sums))
         pending.sums = scatter_sum(pending.blocks(pending.sums), "tp")
         early.second()
-    back_dt, back_log = back_dt[:, :heads], back_log[:, :heads]
-    grad_skip = jnp.sum((back_ssm * act[:, :inner]).reshape(rows, heads, HEADDIM), axis=(0, 2))
-    grad_decay = jnp.sum(back_log * log_decay, axis=0)
-    back_raw = (back_dt - jnp.exp(decay_log) * back_log) * jax.nn.sigmoid(raw_step + step_bias)
-    grad_step_bias = jnp.sum(back_raw, axis=0)
-    pre = conv_total(padded, taps, rows)
-    back_pre = columns([back_x, back_bc]) * silu_slope(pre, jax.nn.sigmoid(pre))
-    following = shifted(back_pre[: CONV - 1], "ctx", -1)
-    wide = padded.astype(full)
-    grad_taps = jnp.stack(
-        [jnp.sum(back_pre * wide[k : k + rows], axis=0) for k in range(CONV)]
-        + [jnp.sum(back_pre, axis=0)]
-    )
-    extended = jnp.concatenate([back_pre, following], axis=0)
-    back_feed = sum(taps[k] * extended[CONV - 1 - k : CONV - 1 - k + rows] for k in range(CONV))
-    spare = feed_weight.shape[1] - channels - heads
-    back_all = columns([back_feed.astype(low), jnp.pad(back_raw.astype(low), ((0, 0), (0, spare)))])
+    grad_skip = jnp.sum(sums[CONV + 1, :inner].reshape(heads, HEADDIM), axis=1)
+    grad_step_bias, grad_decay = head_sums[0, :heads], head_sums[1, :heads]
+    grad_taps = sums[: CONV + 1]
     term = (dot_nt(back_all, feed_weight) + dot_nt(back_gate, gate_weight)).astype(low)
     if pending is not None:
         term, (pending.sums, early.sums) = tied(term, (pending.sums, early.sums))
@@ -692,11 +814,12 @@
         incoming, valid, weights[0], params[0], kept_first, last
     )
     feed_first = grads_first[0]
+    grad_first = (incoming + delta_first).astype(low)
+    feed_first, grad_first = tied(feed_first, grad_first)
     part = inner // 2 + LANES
     feed = Reduction([feed_first[:, :part]], [feed_first[:, part:]])
     feed.first()
     small = jnp.stack([small_first, small_last])
-    grad_first = (incoming + delta_first).astype(low)
     spread_first = spread_rows(grad_first.reshape(tp_count, quarter_rows, width), (0,))
     small = all_sum(all_sum(small, "ctx"), "dp")
     feed.second()
@@ -711,14 +834,16 @@
         first, spread_first.astype(full), own_cotangent + spread_last.astype(full)
     )
 
+    pair_width = 2 * half
+    pair_keep = jnp.where(first, early.sums, last.sums[:, :pair_width])
+    pair_came = swap_cores(jnp.where(first, last.sums[:, :pair_width], early.sums))
     size = small_first.shape[0]
     small_sums = feed_sums[own_rows:].reshape(-1)[: 2 * size].reshape(2, size)
-    sums_first = columns([early.sums, feed_sums[:own_rows]])
-    sums_last = last.sums
-    total_width = sums_first.shape[1]
+    sums_last = last.sums[:, pair_width:]
+    total_width = sums_last.shape[1]
     joined = [
         jnp.concatenate([sums, as_rows(vector, total_width)])
-        for sums, vector in zip((sums_first, sums_last), small_sums)
+        for sums, vector in zip((feed_sums[:own_rows], sums_last), small_sums)
     ]
     keep = jnp.where(first, joined[0], joined[1])
     came = swap_cores(jnp.where(first, joined[1], joined[0]))
@@ -734,10 +859,9 @@
     def own_lane(value, shape, axis):
         return lax.dynamic_index_in_dim(value.reshape(shape), lane, axis, False)
 
-    grad_gate = halves(keep[:, :half], came[:, :half], 1)
-    at = half
-    grad_out = halves(keep[:, at : at + half].T, came[:, at : at + half].T, 0)
-    at += half
+    grad_gate = halves(pair_keep[:, :half], pair_came[:, :half], 1)
+    grad_out = halves(pair_keep[:, half:].T, pair_came[:, half:].T, 0)
+    at = 0
     grad_x = halves(keep[:, at : at + half], came[:, at : at + half], 1)
     at += half
     grad_state = keep[:, at : at + 2 * STATE] + came[:, at : at + 2 * STATE]

time: 848 us -> 834 us (0.983)
  other arithmetic: 175 us -> 117 us
  waiting for transfers between devices: 127 us -> 164 us
  Pallas kernels: 99.5 us -> 133 us
  local copies, waits for them, and re-layouts: 173 us -> 147 us
  starting transfers between devices: 149 us -> 160 us
  matrix products: 106 us -> 97.2 us
    ppermute x39, waiting for transfers between devices: 97 us -> 124 us  [rotated(): lax.ppermute(value, axis, [(i, (i + steps) % count) for i in range(count)])]
    reduce_sum x7 -> x2, other arithmetic: 28 us -> 1.41 us  [layer_backward(): grad_skip = jnp.sum(sums[CONV + 1, :inner].reshape(heads, HEADDIM), axis=1)]
    pallas_call x0 -> x2, Pallas kernels: none -> 19.5 us  [mixer_prep(): pl.pallas_call(prep_kernel, grid=(rows // CHUNK,), in_specs=[pl.BlockSpec...]
    convert_element_type x4 -> x2, other arithmetic: 19.5 us -> 0.85 us  [chain(): entering = shifted(local_state.astype(low), 'ctx', steps)]
    ppermute x9 -> x10, starting transfers between devices: 27.2 us -> 42.7 us  [swap_cores(): return lax.ppermute(value, 'section', [(0, 1), (1, 0)])]
    pallas_call x2, Pallas kernels: 75 us -> 88.9 us  [ssm_backward(): pl.pallas_call(bwd_kernel, grid=(blocks,), in_specs=[pl.BlockSpec((CHUNK,...]
    reduce_sum x2, other arithmetic: 6.76 us -> 18.9 us  [layer_forward(): jnp.mean(hidden * hidden, axis=-1, keepdims=True) + epsilon]
    another operation x4 -> x0, other arithmetic: 10 us -> none
  transfers between devices with their start and end apart: 83 -> 84, of which waited for: 27 -> 30; matrix products, arithmetic and copies ran while one was open for 38% -> 28% of each run, Pallas kernels for 12% -> 16%
where the time goes in v3:
time: 834 us; the launch traced here: 822 us
  waiting for transfers between devices  164 us (20%)
  starting transfers between devices  160 us (19%)
  local copies, waits for them, and re-layouts  147 us (18%)
  Pallas kernels  133 us (16%)
  other arithmetic  117 us (14%)
  matrix products  97.2 us (12%)
    ppermute x39, waiting for transfers between devices, rotated(): lax.ppermute(value, axis, [(i, (i + steps) % count) for i in range(count)])  124 us
    pallas_call x2, Pallas kernels, ssm_backward(): pl.pallas_call(bwd_kernel, grid=(blocks,), in_specs=[pl.BlockSpec((CHUNK,...  88.9 us
    ppermute x26, starting transfers between devices, shifted(): lax.ppermute(value, axis, [(source, source + steps) for source in range(f...  64.6 us
    unnamed x410, local copies, waits for them, and re-layouts  48 us
    ppermute x10, starting transfers between devices, swap_cores(): return lax.ppermute(value, 'section', [(0, 1), (1, 0)])  42.7 us
    dot_general x8, matrix products, dot_nn(): lax.dot_general(a, b, (((1,), (0,)), ((), ())), precision=precision, pref...  40.4 us
    ppermute x39, starting transfers between devices, rotated(): lax.ppermute(value, axis, [(i, (i + steps) % count) for i in range(count)])  32.4 us
    dot_general x8, matrix products, dot_tn(): lax.dot_general(a, b, (((0,), (0,)), ((), ())), precision=precision, pref...  30.6 us
  transfers between devices with their start and end apart: 84, of which 30 were waited for; matrix products, arithmetic and copies ran while one was open for 28% of the time, Pallas kernels for 16%

profile of v3, /device:TPU:1, one launch (start us, length us, event | category | flops | bytes accessed | tf_op | source)
XLA Modules:
  0.0 821.9 jit_solution(14182613330026513223)
XLA Ops:
  31.1 5.1 collective-permute-done.7
  85.3 6.9 fusion.158
  98.8 4.8 collective-permute-start.15
  109.7 9.7 %mixer_prep.2 = (f32[1024,1280]{1,0:T(8,128)S(1)}, f32[1024,128]{1,0:T(8,128)S(1)}, f32[1024,128]{1,0:T(8,128)S(1)}, f32[16,1024]{1,0:T(8,128)S(1)}, f32[1024,128]{1,0:T(8,128)S(1)}, /*index=5*/f32[1024,128]{1,0:T(8,128)S(1)}) custom-call(bf16[1024,1280]{1,0:T(8,128)(2,1)S(1)} %slice.741.feed_ref.before_ref, ...), custom_call_target="tpu_custom_call" | custom-call | flops 268435456 | bytes 7864320 | tf_op jit(solution)/shard_map/mixer_prep/pallas_call | solution.py:191
  130.9 12.2 %ssm_forward.2 = (f32[1024,1024]{1,0:T(8,128)S(1)}, bf16[8,1024,128]{2,1,0:T(8,128)(2,1)S(1)}) custom-call(f32[1024,1280]{1,0:T(8,128)S(1)} %copy-done.3, f32[1024,1280]{1,0:T(8,128)S(1)} %copy-done.3, f32[1024,128]{1,0:T(8,128)S(1)} %get-tuple-element.80.dt_ref, f32[1024,128]{1,0:T(8,128)S(1)} %get-tuple-element.81.cum_ref, ...), custom_call_target="tpu_custom_call" | custom-call | flops 1073741824 | bytes 10485760 | tf_op jit(solution)/shard_map/ssm_forward/pallas_call | solution.py:397
  170.7 8.3 %multiply_reduce_fusion.3 = (f32[1024]{0:T(1024)S(1)}, f32[1024,1024]{1,0:T(8,128)S(1)}, f32[1024,1024]{1,0:T(8,128)}) fusion(f32[1024,1024]{1,0:T(8,128)} %copy-done.41, bf16[1024,1024]{1,0:T(8,128)(2,1)} %constant_dynamic-update-slice_fusion.4, f32[1024]{0:T(1024)S(1)} %convert_reduce_fusion.1, f32[1024]{0:T(1024)S(1)} %add_rsqrt_fusion.3, ...), kind=kOutput, calls=%fused_computation.66 | convolution fusion | flops 2159016960 | bytes 16789508 | tf_op jit(solution)/shard_map/dot_general | solution.py:25
  187.7 16.0 %collective-permute-start.31 = (bf16[1024,1024]{1,0:T(8,128)(2,1)}, bf16[1024,1024]{1,0:T(8,128)(2,1)}, u32[]{:S(2)}, u32[]{:S(2)}) collective-permute-start(bf16[1024,1024]{1,0:T(8,128)(2,1)} %convolution_convert_fusion.5), channel_id=1, source_target_pairs={{0,16},{16,0},{1,17},{17,1},{2,18},{18,2},{3,19},{19,3},{4,20},{20... | collective-permute-start | bytes 6291464 | tf_op jit(solution)/shard_map/ppermute | solution.py:94
  209.8 12.8 %collective-permute-done.35 = bf16[2,256,768]{2,1,0:T(8,128)(2,1)S(1)} collective-permute-done((bf16[2,256,768]{2,1,0:T(8,128)(2,1)S(1)}, bf16[2,256,768]{2,1,0:T(8,128)(2,1)S(1)}, u32[]{:S(2)}, u32[]{:S(2)}) %collective-permute-start.35) | collective-permute-done | bytes 786464 | tf_op jit(solution)/shard_map/ppermute | solution.py:50
  240.4 16.9 %fusion.6 = (f32[1024]{0:T(1024)S(1)}, bf16[1024,1024]{1,0:T(8,128)(2,1)S(1)}) fusion(bf16[1024,1024]{1,0:T(8,128)(2,1)} %collective-permute-done.31, bf16[1024,1024]{1,0:T(8,128)(2,1)} %convolution_convert_fusion.5, f32[1024]{0:T(1024)S(1)} %copy-done.149, bf16[4,1,1024,1024]{3,2,1,0:T(8,128)(2,1)} %param.14, s32[]{:T(128)S(6)} %select_n.629), kind=kLoop, calls=%fused_computation.24 | loop fusion | flops 10484736 | bytes 8396804 | tf_op jit(solution)/shard_map/reduce_sum | solution.py:511
  265.2 9.7 %mixer_prep.3 = (f32[1024,1280]{1,0:T(8,128)S(1)}, f32[1024,128]{1,0:T(8,128)S(1)}, f32[1024,128]{1,0:T(8,128)S(1)}, f32[16,1024]{1,0:T(8,128)S(1)}, f32[1024,128]{1,0:T(8,128)S(1)}, /*index=5*/f32[1024,128]{1,0:T(8,128)S(1)}) custom-call(bf16[1024,1280]{1,0:T(8,128)(2,1)S(1)} %slice.763.feed_ref.before_ref, ...), custom_call_target="tpu_custom_call" | custom-call | flops 268435456 | bytes 7864320 | tf_op jit(solution)/shard_map/mixer_prep/pallas_call | solution.py:191
  282.3 12.2 %ssm_forward.3 = (f32[1024,1024]{1,0:T(8,128)S(1)}, bf16[8,1024,128]{2,1,0:T(8,128)(2,1)S(1)}) custom-call(f32[1024,1280]{1,0:T(8,128)S(1)} %get-tuple-element.99.x_ref.bc_ref, f32[1024,1280]{1,0:T(8,128)S(1)} %get-tuple-element.99.x_ref.bc_ref, f32[1024,128]{1,0:T(8,128)S(1)} %get-tuple-element.100.dt_ref, f32[1024,128]{1,0:T(8,128)S(1)} %get-tuple-element.101.cum_ref, ...), custom_call_target="tpu_custom_call" | custom-call | flops 1073741824 | bytes 10485760 | tf_op jit(solution)/shard_map/ssm_forward/pallas_call | solution.py:397
  296.4 4.6 collective-permute-done.39
  301.5 5.0 multiply_reduce_fusion.2
  310.2 4.9 collective-permute-start.43
  330.0 7.7 fusion.40
  364.4 44.0 %ssm_backward.2 = (bf16[1024,1408]{1,0:T(8,128)(2,1)S(1)}, f32[8,1280]{1,0:T(8,128)S(1)}, f32[8,1280]{1,0:T(8,128)S(1)}, f32[8,128]{1,0:T(8,128)S(1)}) custom-call(f32[1024,1280]{1,0:T(8,128)} %copy-done.4, f32[1024,1280]{1,0:T(8,128)} %copy-done.4, f32[1024,128]{1,0:T(8,128)S(1)} %copy-done.20, f32[1024,128]{1,0:T(8,128)S(1)} %copy-done.22, ...), custom_call_target="tpu_custom_call" | custom-call | flops 4294967296 | bytes 16777216 | tf_op jit(solution)/shard_map/ssm_backward/pallas_call | solution.py:438
  446.4 8.9 %collective-permute-done.50 = bf16[2,256,1664]{2,1,0:T(8,128)(2,1)} collective-permute-done((bf16[2,256,1664]{2,1,0:T(8,128)(2,1)}, bf16[2,256,1664]{2,1,0:T(8,128)(2,1)}, u32[]{:S(2)}, u32[]{:S(2)}) %collective-permute-start.50) | collective-permute-done | bytes 1703968 | tf_op jit(solution)/shard_map/ppermute | solution.py:50
  461.8 5.8 fusion.4
  473.2 5.1 multiply_convert_fusion
  478.3 5.8 convolution_convert_fusion.2
  516.1 44.9 %ssm_backward.3 = (bf16[1024,1408]{1,0:T(8,128)(2,1)S(1)}, f32[8,1280]{1,0:T(8,128)}, f32[8,1280]{1,0:T(8,128)S(1)}, f32[8,128]{1,0:T(8,128)S(1)}) custom-call(f32[1024,1280]{1,0:T(8,128)} %copy-done.2, f32[1024,1280]{1,0:T(8,128)} %copy-done.2, f32[1024,128]{1,0:T(8,128)S(1)} %copy-done.16, f32[1024,128]{1,0:T(8,128)S(1)} %copy-done.18, ...), custom_call_target="tpu_custom_call" | custom-call | flops 4294967296 | bytes 16777216 | tf_op jit(solution)/shard_map/ssm_backward/pallas_call | solution.py:438
  578.8 9.5 %collective-permute-done.57 = bf16[2,256,1024]{2,1,0:T(8,128)(2,1)S(1)} collective-permute-done((bf16[2,256,1024]{2,1,0:T(8,128)(2,1)}, bf16[2,256,1024]{2,1,0:T(8,128)(2,1)S(1)}, u32[]{:S(2)}, u32[]{:S(2)}) %collective-permute-start.57) | collective-permute-done | bytes 1048608 | tf_op jit(solution)/shard_map/ppermute | solution.py:50
  601.2 6.3 add_convert_fusion
  619.4 31.8 %collective-permute-done.59 = bf16[256,1152]{1,0:T(8,128)(2,1)S(1)} collective-permute-done((bf16[256,1152]{1,0:T(8,128)(2,1)S(1)}, bf16[256,1152]{1,0:T(8,128)(2,1)S(1)}, u32[]{:S(2)}, u32[]{:S(2)}) %collective-permute-start.59) | collective-permute-done | bytes 589856 | tf_op jit(solution)/shard_map/ppermute | solution.py:50
  652.6 11.9 %collective-permute-start.63 = (bf16[1024,1024]{1,0:T(8,128)(2,1)}, bf16[1024,1024]{1,0:T(8,128)(2,1)}, u32[]{:S(2)}, u32[]{:S(2)}) collective-permute-start(bf16[1024,1024]{1,0:T(8,128)(2,1)} %add_convert_fusion), channel_id=1, source_target_pairs={{0,16},{16,0},{1,17},{17,1},{2,18},{18,2},{3,19},{19,3},{4,20},{20... | collective-permute-start | bytes 6291464 | tf_op jit(solution)/shard_map/ppermute | solution.py:94
  681.1 18.0 %collective-permute-done.80 = bf16[256,512]{1,0:T(8,128)(2,1)S(1)} collective-permute-done((bf16[256,512]{1,0:T(8,128)(2,1)S(1)}, bf16[256,512]{1,0:T(8,128)(2,1)S(1)}, u32[]{:S(2)}, u32[]{:S(2)}) %collective-permute-start.80) | collective-permute-done | bytes 262176 | tf_op jit(solution)/shard_map/ppermute | solution.py:50
  700.0 6.9 convolution_convert_fusion
  708.9 4.7 fusion.21
  739.4 8.4 %collective-permute-done.70 = bf16[2,256,640]{1,2,0:T(8,128)(2,1)S(1)} collective-permute-done((bf16[2,256,640]{1,2,0:T(8,128)(2,1)}, bf16[2,256,640]{1,2,0:T(8,128)(2,1)S(1)}, u32[]{:S(2)}, u32[]{:S(2)}) %collective-permute-start.70) | collective-permute-done | bytes 655392 | tf_op jit(solution)/shard_map/ppermute | solution.py:50
  770.3 18.6 %collective-permute-done.77 = bf16[288,640]{1,0:T(8,128)(2,1)S(1)} collective-permute-done((bf16[288,640]{1,0:T(8,128)(2,1)S(1)}, bf16[288,640]{1,0:T(8,128)(2,1)S(1)}, u32[]{:S(2)}, u32[]{:S(2)}) %collective-permute-start.77) | collective-permute-done | bytes 368672 | tf_op jit(solution)/shard_map/ppermute | solution.py:50
  793.8 5.9 collective-permute-start.83
  800.8 6.0 fusion.23
  (937 shorter events, 437.4 us)
Async XLA Ops:
  66.1 29.3 %collective-permute-start.26 = (bf16[256,1024]{1,0:T(8,128)(2,1)}, bf16[256,1024]{1,0:T(8,128)(2,1)}, u32[]{:S(2)}, u32[]{:S(2)}) collective-permute-start(bf16[256,1024]{1,0:T(8,128)(2,1)} %pad_maximum_fusion.32), channel_id=1, source_target_pairs={{0,4},{4,0},{1,5},{5,1},{2,6},{6,2},{3,7},{7,3},{8,12},{12,8},{9,1... | collective-permute-start | bytes 1572872 | tf_op jit(solution)/shard_map/ppermute | solution.py:50
  71.9 27.0 %collective-permute-start.14 = (bf16[288,896]{1,0:T(8,128)(2,1)}, bf16[288,896]{1,0:T(8,128)(2,1)}, u32[]{:S(2)}, u32[]{:S(2)}) collective-permute-start(bf16[288,896]{1,0:T(8,128)(2,1)} %fusion.69), channel_id=1, source_target_pairs={{0,1},{1,2},{2,3},{4,5},{5,6},{6,7},{8,9},{9,10},{10,11},{12,13},{... | collective-permute-start | bytes 1548296 | tf_op jit(solution)/shard_map/ppermute | solution.py:45
  75.9 27.8 %collective-permute-start.17 = (bf16[288,896]{1,0:T(8,128)(2,1)}, bf16[288,896]{1,0:T(8,128)(2,1)}, u32[]{:S(2)}, u32[]{:S(2)}) collective-permute-start(bf16[288,896]{1,0:T(8,128)(2,1)} %fusion.69), channel_id=1, source_target_pairs={{1,0},{2,1},{3,2},{5,4},{6,5},{7,6},{9,8},{10,9},{11,10},{13,12},{... | collective-permute-start | bytes 1548296 | tf_op jit(solution)/shard_map/ppermute | solution.py:45
  85.0 65.5 %collective-permute-start.29 = (bf16[2,256,1024]{2,1,0:T(8,128)(2,1)}, bf16[2,256,1024]{2,1,0:T(8,128)(2,1)}, u32[]{:S(2)}, u32[]{:S(2)}) collective-permute-start(bf16[2,256,1024]{2,1,0:T(8,128)(2,1)} %pad_maximum_fusion.18), channel_id=1, source_target_pairs={{0,4},{4,0},{1,5},{5,1},{2,6},{6,2},{3,7},{7,3},{8,12},{12,8},{9,1... | collective-permute-start | bytes 3145736 | tf_op jit(solution)/shard_map/ppermute | solution.py:50
  97.9 54.4 %collective-permute-start.27 = (bf16[2,256,1024]{2,1,0:T(8,128)(2,1)}, bf16[2,256,1024]{2,1,0:T(8,128)(2,1)}, u32[]{:S(2)}, u32[]{:S(2)}) collective-permute-start(bf16[2,256,1024]{2,1,0:T(8,128)(2,1)} %pad_maximum_fusion.17), channel_id=1, source_target_pairs={{0,8},{8,0},{1,9},{9,1},{2,10},{10,2},{3,11},{11,3},{4,12},{12,4},... | collective-permute-start | bytes 3145736 | tf_op jit(solution)/shard_map/ppermute | solution.py:50
  98.8 46.3 %collective-permute-start.15 = (bf16[288,896]{1,0:T(8,128)(2,1)}, bf16[288,896]{1,0:T(8,128)(2,1)}, u32[]{:S(2)}, u32[]{:S(2)}) collective-permute-start(bf16[288,896]{1,0:T(8,128)(2,1)} %collective-permute-done.14), channel_id=1, source_target_pairs={{0,1},{1,2},{2,3},{4,5},{5,6},{6,7},{8,9},{9,10},{10,11},{12,13},{... | collective-permute-start | bytes 1548296 | tf_op jit(solution)/shard_map/ppermute | solution.py:45
  103.6 45.5 %collective-permute-start.18 = (bf16[288,896]{1,0:T(8,128)(2,1)}, bf16[288,896]{1,0:T(8,128)(2,1)}, u32[]{:S(2)}, u32[]{:S(2)}) collective-permute-start(bf16[288,896]{1,0:T(8,128)(2,1)} %collective-permute-done.17), channel_id=1, source_target_pairs={{1,0},{2,1},{3,2},{5,4},{6,5},{7,6},{9,8},{10,9},{11,10},{13,12},{... | collective-permute-start | bytes 1548296 | tf_op jit(solution)/shard_map/ppermute | solution.py:45
  167.8 36.0 %collective-permute-start.34 = (bf16[256,768]{1,0:T(8,128)(2,1)S(1)}, bf16[256,768]{1,0:T(8,128)(2,1)S(1)}, u32[]{:S(2)}, u32[]{:S(2)}) collective-permute-start(bf16[256,768]{1,0:T(8,128)(2,1)S(1)} %concatenate.191), channel_id=1, source_target_pairs={{0,8},{8,0},{1,9},{9,1},{2,10},{10,2},{3,11},{11,3},{4,12},{12,4},... | collective-permute-start | bytes 1179656 | tf_op jit(solution)/shard_map/ppermute | solution.py:50
  183.0 25.7 %collective-permute-start.33 = (bf16[2,256,768]{2,1,0:T(8,128)(2,1)S(1)}, bf16[2,256,768]{2,1,0:T(8,128)(2,1)S(1)}, u32[]{:S(2)}, u32[]{:S(2)}) collective-permute-start(bf16[2,256,768]{2,1,0:T(8,128)(2,1)S(1)} %pad_maximum_fusion.27), channel_id=1, source_target_pairs={{0,8},{8,0},{1,9},{9,1},{2,10},{10,2},{3,11},{11,3},{4,12},{12,4},... | collective-permute-start | bytes 2359304 | tf_op jit(solution)/shard_map/ppermute | solution.py:50
  187.7 52.7 %collective-permute-start.31 = (bf16[1024,1024]{1,0:T(8,128)(2,1)}, bf16[1024,1024]{1,0:T(8,128)(2,1)}, u32[]{:S(2)}, u32[]{:S(2)}) collective-permute-start(bf16[1024,1024]{1,0:T(8,128)(2,1)} %convolution_convert_fusion.5), channel_id=1, source_target_pairs={{0,16},{16,0},{1,17},{17,1},{2,18},{18,2},{3,19},{19,3},{4,20},{20... | collective-permute-start | bytes 6291464 | tf_op jit(solution)/shard_map/ppermute | solution.py:94
  228.1 35.6 %collective-permute-start.38 = (bf16[256,1024]{1,0:T(8,128)(2,1)}, bf16[256,1024]{1,0:T(8,128)(2,1)}, u32[]{:S(2)}, u32[]{:S(2)}) collective-permute-start(bf16[256,1024]{1,0:T(8,128)(2,1)} %pad_maximum_fusion.34), channel_id=1, source_target_pairs={{0,4},{4,0},{1,5},{5,1},{2,6},{6,2},{3,7},{7,3},{8,12},{12,8},{9,1... | collective-permute-start | bytes 1572872 | tf_op jit(solution)/shard_map/ppermute | solution.py:50
  239.7 54.8 %collective-permute-start.41 = (bf16[2,256,1024]{2,1,0:T(8,128)(2,1)S(1)}, bf16[2,256,1024]{2,1,0:T(8,128)(2,1)S(1)}, u32[]{:S(2)}, u32[]{:S(2)}) collective-permute-start(bf16[2,256,1024]{2,1,0:T(8,128)(2,1)S(1)} %pad_maximum_fusion.20), channel_id=1, source_target_pairs={{0,4},{4,0},{1,5},{5,1},{2,6},{6,2},{3,7},{7,3},{8,12},{12,8},{9,1... | collective-permute-start | bytes 3145736 | tf_op jit(solution)/shard_map/ppermute | solution.py:50
  349.2 78.6 %collective-permute-start.44 = (bf16[256,1024]{1,0:T(8,128)(2,1)S(1)}, bf16[256,1024]{1,0:T(8,128)(2,1)S(1)}, u32[]{:S(2)}, u32[]{:S(2)}) collective-permute-start(bf16[256,1024]{1,0:T(8,128)(2,1)S(1)} %get-tuple-element.220), channel_id=1, source_target_pairs={{0,1},{1,2},{2,3},{3,0},{16,17},{17,18},{18,19},{19,16},{4,5},{5,6... | collective-permute-start | bytes 1572872 | tf_op jit(solution)/shard_map/ppermute | solution.py:110
  351.3 87.2 %collective-permute-start.45 = (bf16[256,1024]{1,0:T(8,128)(2,1)}, bf16[256,1024]{1,0:T(8,128)(2,1)}, u32[]{:S(2)}, u32[]{:S(2)}) collective-permute-start(bf16[256,1024]{1,0:T(8,128)(2,1)} %get-tuple-element.219), channel_id=1, source_target_pairs={{0,2},{1,3},{2,0},{3,1},{16,18},{17,19},{18,16},{19,17},{4,6},{5,7... | collective-permute-start | bytes 1572872 | tf_op jit(solution)/shard_map/ppermute | solution.py:110
  360.0 84.3 %collective-permute-start.51 = (bf16[2,256,1792]{2,1,0:T(8,128)(2,1)}, bf16[2,256,1792]{2,1,0:T(8,128)(2,1)}, u32[]{:S(2)}, u32[]{:S(2)}) collective-permute-start(bf16[2,256,1792]{2,1,0:T(8,128)(2,1)} %pad_maximum_fusion.6), channel_id=1, source_target_pairs={{0,8},{8,0},{1,9},{9,1},{2,10},{10,2},{3,11},{11,3},{4,12},{12,4},... | collective-permute-start | bytes 5505032 | tf_op jit(solution)/shard_map/ppermute | solution.py:50
  418.8 36.4 %collective-permute-start.50 = (bf16[2,256,1664]{2,1,0:T(8,128)(2,1)}, bf16[2,256,1664]{2,1,0:T(8,128)(2,1)}, u32[]{:S(2)}, u32[]{:S(2)}) collective-permute-start(bf16[2,256,1664]{2,1,0:T(8,128)(2,1)} %pad_maximum_fusion.7), channel_id=1, source_target_pairs={{0,4},{4,0},{1,5},{5,1},{2,6},{6,2},{3,7},{7,3},{8,12},{12,8},{9,1... | collective-permute-start | bytes 5111816 | tf_op jit(solution)/shard_map/ppermute | solution.py:50
  424.6 32.7 %collective-permute-start.49 = (bf16[1024,1024]{1,0:T(8,128)(2,1)S(1)}, bf16[1024,1024]{1,0:T(8,128)(2,1)}, u32[]{:S(2)}, u32[]{:S(2)}) collective-permute-start(bf16[1024,1024]{1,0:T(8,128)(2,1)S(1)} %add_convert_fusion.1), channel_id=1, source_target_pairs={{0,16},{16,0},{1,17},{17,1},{2,18},{18,2},{3,19},{19,3},{4,20},{20... | collective-permute-start | bytes 6291464 | tf_op jit(solution)/shard_map/ppermute | solution.py:94
  491.5 78.9 %collective-permute-start.67 = (bf16[256,1024]{1,0:T(8,128)(2,1)}, bf16[256,1024]{1,0:T(8,128)(2,1)}, u32[]{:S(2)}, u32[]{:S(2)}) collective-permute-start(bf16[256,1024]{1,0:T(8,128)(2,1)} %get-tuple-element.216), channel_id=1, source_target_pairs={{16,17},{17,18},{18,19},{19,16},{20,21},{21,22},{22,23},{23,20},{2... | collective-permute-start | bytes 1572872 | tf_op jit(solution)/shard_map/ppermute | solution.py:110
  501.4 70.9 %collective-permute-start.54 = (bf16[256,1664]{1,0:T(8,128)(2,1)}, bf16[256,1664]{1,0:T(8,128)(2,1)}, u32[]{:S(2)}, u32[]{:S(2)}) collective-permute-start(bf16[256,1664]{1,0:T(8,128)(2,1)} %dynamic-slice_bitcast_fusion.7), channel_id=1, source_target_pairs={{0,8},{8,0},{1,9},{9,1},{2,10},{10,2},{3,11},{11,3},{4,12},{12,4},... | collective-permute-start | bytes 2555912 | tf_op jit(solution)/shard_map/ppermute | solution.py:50
  503.6 70.5 %collective-permute-start.55 = (bf16[256,1792]{1,0:T(8,128)(2,1)}, bf16[256,1792]{1,0:T(8,128)(2,1)}, u32[]{:S(2)}, u32[]{:S(2)}) collective-permute-start(bf16[256,1792]{1,0:T(8,128)(2,1)} %dynamic-slice_bitcast_fusion.6), channel_id=1, source_target_pairs={{0,4},{4,0},{1,5},{5,1},{2,6},{6,2},{3,7},{7,3},{8,12},{12,8},{9,1... | collective-permute-start | bytes 2752520 | tf_op jit(solution)/shard_map/ppermute | solution.py:50
  506.8 69.0 %collective-permute-start.56 = (bf16[2,256,1024]{2,1,0:T(8,128)(2,1)}, bf16[2,256,1024]{2,1,0:T(8,128)(2,1)}, u32[]{:S(2)}, u32[]{:S(2)}) collective-permute-start(bf16[2,256,1024]{2,1,0:T(8,128)(2,1)} %dynamic-slice_bitcast_fusion.3), channel_id=1, source_target_pairs={{0,4},{4,0},{1,5},{5,1},{2,6},{6,2},{3,7},{7,3},{8,12},{12,8},{9,1... | collective-permute-start | bytes 3145736 | tf_op jit(solution)/shard_map/ppermute | solution.py:50
  600.2 51.0 %collective-permute-start.59 = (bf16[256,1152]{1,0:T(8,128)(2,1)S(1)}, bf16[256,1152]{1,0:T(8,128)(2,1)S(1)}, u32[]{:S(2)}, u32[]{:S(2)}) collective-permute-start(bf16[256,1152]{1,0:T(8,128)(2,1)S(1)} %get-tuple-element.366), channel_id=1, source_target_pairs={{0,2},{1,3},{2,0},{3,1},{4,6},{5,7},{6,4},{7,5},{8,10},{9,11},{10,... | collective-permute-start | bytes 1769480 | tf_op jit(solution)/shard_map/ppermute | solution.py:50
  600.2 51.0 %collective-permute-start.58 = (bf16[256,1152]{1,0:T(8,128)(2,1)S(1)}, bf16[256,1152]{1,0:T(8,128)(2,1)S(1)}, u32[]{:S(2)}, u32[]{:S(2)}) collective-permute-start(bf16[256,1152]{1,0:T(8,128)(2,1)S(1)} %get-tuple-element.365), channel_id=1, source_target_pairs={{0,1},{1,2},{2,3},{3,0},{4,5},{5,6},{6,7},{7,4},{8,9},{9,10},{10,1... | collective-permute-start | bytes 1769480 | tf_op jit(solution)/shard_map/ppermute | solution.py:50
  609.0 66.8 %collective-permute-start.68 = (bf16[256,1024]{1,0:T(8,128)(2,1)}, bf16[256,1024]{1,0:T(8,128)(2,1)}, u32[]{:S(2)}, u32[]{:S(2)}) collective-permute-start(bf16[256,1024]{1,0:T(8,128)(2,1)} %get-tuple-element.215), channel_id=1, source_target_pairs={{16,18},{17,19},{18,16},{19,17},{20,22},{21,23},{22,20},{23,21},{2... | collective-permute-start | bytes 1572872 | tf_op jit(solution)/shard_map/ppermute | solution.py:110
  613.9 65.3 %collective-permute-start.69 = (bf16[256,1024]{1,0:T(8,128)(2,1)}, bf16[256,1024]{1,0:T(8,128)(2,1)}, u32[]{:S(2)}, u32[]{:S(2)}) collective-permute-start(bf16[256,1024]{1,0:T(8,128)(2,1)} %get-tuple-element.214), channel_id=1, source_target_pairs={{16,19},{17,16},{18,17},{19,18},{20,23},{21,20},{22,21},{23,22},{2... | collective-permute-start | bytes 1572872 | tf_op jit(solution)/shard_map/ppermute | solution.py:110
  652.6 56.3 %collective-permute-start.63 = (bf16[1024,1024]{1,0:T(8,128)(2,1)}, bf16[1024,1024]{1,0:T(8,128)(2,1)}, u32[]{:S(2)}, u32[]{:S(2)}) collective-permute-start(bf16[1024,1024]{1,0:T(8,128)(2,1)} %add_convert_fusion), channel_id=1, source_target_pairs={{0,16},{16,0},{1,17},{17,1},{2,18},{18,2},{3,19},{19,3},{4,20},{20... | collective-permute-start | bytes 6291464 | tf_op jit(solution)/shard_map/ppermute | solution.py:94
  672.5 26.6 %collective-permute-start.80 = (bf16[256,512]{1,0:T(8,128)(2,1)S(1)}, bf16[256,512]{1,0:T(8,128)(2,1)S(1)}, u32[]{:S(2)}, u32[]{:S(2)}) collective-permute-start(bf16[256,512]{1,0:T(8,128)(2,1)S(1)} %pad_maximum_fusion.38), channel_id=1, source_target_pairs={{0,2},{1,3},{2,0},{3,1},{4,6},{5,7},{6,4},{7,5},{8,10},{9,11},{10,... | collective-permute-start | bytes 786440 | tf_op jit(solution)/shard_map/ppermute | solution.py:50
  720.2 42.6 %collective-permute-start.64 = (bf16[256,1024]{1,0:T(8,128)(2,1)}, bf16[256,1024]{1,0:T(8,128)(2,1)}, u32[]{:S(2)}, u32[]{:S(2)}) collective-permute-start(bf16[256,1024]{1,0:T(8,128)(2,1)} %get-tuple-element.210), channel_id=1, source_target_pairs={{0,1},{1,2},{2,3},{3,0},{4,5},{5,6},{6,7},{7,4},{8,9},{9,10},{10,1... | collective-permute-start | bytes 1572872 | tf_op jit(solution)/shard_map/ppermute | solution.py:110
  721.7 43.6 %collective-permute-start.65 = (bf16[256,1024]{1,0:T(8,128)(2,1)}, bf16[256,1024]{1,0:T(8,128)(2,1)}, u32[]{:S(2)}, u32[]{:S(2)}) collective-permute-start(bf16[256,1024]{1,0:T(8,128)(2,1)} %get-tuple-element.209), channel_id=1, source_target_pairs={{0,2},{1,3},{2,0},{3,1},{4,6},{5,7},{6,4},{7,5},{8,10},{9,11},{10,... | collective-permute-start | bytes 1572872 | tf_op jit(solution)/shard_map/ppermute | solution.py:110
  723.2 76.6 %collective-permute-start.66 = (bf16[256,1024]{1,0:T(8,128)(2,1)}, bf16[256,1024]{1,0:T(8,128)(2,1)}, u32[]{:S(2)}, u32[]{:S(2)}) collective-permute-start(bf16[256,1024]{1,0:T(8,128)(2,1)} %get-tuple-element.208), channel_id=1, source_target_pairs={{0,3},{1,0},{2,1},{3,2},{4,7},{5,4},{6,5},{7,6},{8,11},{9,8},{10,9... | collective-permute-start | bytes 1572872 | tf_op jit(solution)/shard_map/ppermute | solution.py:110
  762.7 26.2 %collective-permute-start.77 = (bf16[288,640]{1,0:T(8,128)(2,1)S(1)}, bf16[288,640]{1,0:T(8,128)(2,1)S(1)}, u32[]{:S(2)}, u32[]{:S(2)}) collective-permute-start(bf16[288,640]{1,0:T(8,128)(2,1)S(1)} %get-tuple-element.287), channel_id=1, source_target_pairs={{0,2},{1,3},{2,0},{3,1},{4,6},{5,7},{6,4},{7,5},{8,10},{9,11},{10,... | collective-permute-start | bytes 1105928 | tf_op jit(solution)/shard_map/ppermute | solution.py:50
  762.8 26.1 %collective-permute-start.76 = (bf16[288,640]{1,0:T(8,128)(2,1)S(1)}, bf16[288,640]{1,0:T(8,128)(2,1)S(1)}, u32[]{:S(2)}, u32[]{:S(2)}) collective-permute-start(bf16[288,640]{1,0:T(8,128)(2,1)S(1)} %get-tuple-element.285), channel_id=1, source_target_pairs={{0,1},{1,2},{2,3},{3,0},{4,5},{5,6},{6,7},{7,4},{8,9},{9,10},{10,1... | collective-permute-start | bytes 1105928 | tf_op jit(solution)/shard_map/ppermute | solution.py:50
  (232 other events, 2555.4 us)
